TPU v7x, 32 devices: a whole 2x2x4 slice. The times are simulated.
32 devices in a mesh: head: 2 (over x), blk: 16 (over z, y, core).
Axes of the slice: x: 2, y: 2, z: 4, core: 2. Of those that a mesh axis runs over, the one named last changes fastest.
Arguments:
- hidden_in: bfloat16 [512, 2048], P('blk'), may hold values from -6 to 6
- attn_gain: float32 [2048], replicated, may hold values from 0.25 to 1.75
- w_query: bfloat16 [1536, 2048], P('head'), may hold values from -0.125 to 0.125
- w_latent: bfloat16 [576, 2048], P('head'), may hold values from -0.125 to 0.125
- kv_gain: float32 [512], replicated, may hold values from 0.25 to 1.75
- w_key_up: bfloat16 [512, 1024], P(None, 'head'), may hold values from -0.25 to 0.25
- w_value_up: bfloat16 [512, 1024], P(None, 'head'), may hold values from -0.25 to 0.25
- w_out: bfloat16 [1024, 2048], P('head'), may hold values from -0.1875 to 0.1875
- cache_rows: bfloat16 [6144, 576], P('blk'), may hold values from -6 to 6
- slot_request: int32 [48], P('blk'), may hold values from -1 to 15, as said below
- slot_block: int32 [48], P('blk'), may hold values from 0 to 16
- lengths: int32 [16], replicated, may hold values from 1 to 2176, as said below
- parents: int32 [16, 32], P('blk'), may hold values from -1 to 30, as said below
- accepted: int32 [16, 8], P('blk'), may hold values from 0 to 28, as said below
- new_slots: int32 [16, 8], P('blk'), may hold values from 0 to 255, as said below
- moe_gain: float32 [2048], replicated, may hold values from 0.25 to 1.75
- routes: int32 [512, 6], P('blk'), may hold values from 0 to 15, all different within a row; in each aligned block of 32 rows (0 to 31, 32 to 63, ...) at most 24 rows name the same one
- route_logits: float32 [512, 6], P('blk'), may hold values from -8 to 8
- w_gate: bfloat16 [16, 1408, 2048], P('blk', 'head'), may hold values from -0.125 to 0.125
- w_up: bfloat16 [16, 1408, 2048], P('blk', 'head'), may hold values from -0.125 to 0.125
- w_down: bfloat16 [16, 1408, 2048], P('blk', 'head'), may hold values from -0.15625 to 0.15625
Outputs:
- layer_out: bfloat16 [512, 2048], P('blk')
- new_rows: bfloat16 [256, 576], P('blk')
Inputs may be any that keep to these rules, and one draw needn't show every extreme that they name: A pool slot holds block slot_block of request slot_request or is free (-1); each request's blocks are distinct slots. Request r holds exactly ceil(lengths[r] / 128) pool blocks, numbered 0 upwards; one request holds 17 full blocks. `parents`: entry 0 of each request is -1 (the root); entry i names one of the tokens i - 4 .. i - 1. `accepted`: the first 8 tokens of a path from the root down the request's tree, root first. `new_slots`: all distinct. `routes`: within the 32 rows of one index of blk no expert is named more than 24 times.
All inputs are finite; a program needn't handle non-finite values.
Results may differ from a plain program's by a relative error of at most 0.0075.
Values may be sent and summed in bfloat16 or wider, within the bound.
No kernel may reach another device: no remote copies, remote signals or barrier semaphores. Data moves between devices by JAX's collectives and lax.ppermute only.
A program may use at most 128 MiB of HBM per device.

v0:
```python
import jax
import jax.numpy as jnp
from jax import lax
from jax.sharding import PartitionSpec as P

NOPE = 128
ROPE = 64
VDIM = 128
RANK = 512
NEW_DEV = 16


EPSILON = 1e-06
ROUTE_SCALE = 2.446
ROPE_BASE = 50000.0


def rms_scale(values, gain):
    values = values.astype(jnp.float32)
    mean_square = jnp.mean(values * values, axis=-1, keepdims=True)
    return values * lax.rsqrt(mean_square + EPSILON) * gain


def rotate(values, positions):
    width = values.shape[-1]
    half = width // 2
    freqs = ROPE_BASE ** (-2.0 * jnp.arange(half, dtype=jnp.float32) / width)
    angles = positions[:, None] * freqs[None, :]
    cosine = jnp.cos(angles)[:, None, :]
    sine = jnp.sin(angles)[:, None, :]
    first = values[..., :half]
    second = values[..., half:]
    return jnp.concatenate(
        [first * cosine - second * sine, second * cosine + first * sine], axis=-1
    )


def ancestry(parents):
    count = parents.shape[-1]
    nodes = jnp.arange(count, dtype=jnp.int32)
    reach = (parents[:, :, None] == nodes[None, None, :]).astype(jnp.float32) + jnp.eye(
        count, dtype=jnp.float32
    )[None]
    for level in range(count.bit_length()):
        reach = jnp.minimum(
            jnp.einsum("rij,rjk->rik", reach, reach, precision=lax.Precision.HIGHEST), 1.0
        )
    return reach


def expand(rows, key_up, value_up):
    count = rows.shape[0]
    heads_here = key_up.shape[1] // NOPE
    key_nope = (
        jnp.dot(rows[:, :RANK], key_up, preferred_element_type=jnp.float32)
        .astype(jnp.bfloat16)
        .reshape(count, heads_here, NOPE)
    )
    values = (
        jnp.dot(rows[:, :RANK], value_up, preferred_element_type=jnp.float32)
        .astype(jnp.bfloat16)
        .reshape(count, heads_here, VDIM)
    )
    shared = jnp.broadcast_to(rows[:, None, RANK:], (count, heads_here, ROPE))
    return (jnp.concatenate([key_nope, shared], axis=-1), values)


def project_rows(left, weight_rows):
    return lax.dot_general(
        left, weight_rows, (((1,), (1,)), ((), ())), preferred_element_type=jnp.float32
    )


def shards(
    hidden_in,
    attn_gain,
    w_query,
    w_latent,
    kv_gain,
    w_key_up,
    w_value_up,
    w_out,
    cache_rows,
    slot_request,
    slot_block,
    lengths,
    parents,
    accepted,
    new_slots,
    moe_gain,
    routes,
    route_logits,
    w_gate,
    w_up,
    w_down,
):
    block_count = lax.axis_size("blk")
    block_index = lax.axis_index("blk")
    tok_rows = hidden_in.shape[0]
    model_width = hidden_in.shape[1]
    req_local = parents.shape[0]
    draft_len = parents.shape[1]
    requests = lengths.shape[0]
    heads_here = w_key_up.shape[1] // NOPE
    top_count = routes.shape[1]
    scale = (NOPE + ROPE) ** (-0.5)
    normed = rms_scale(hidden_in, attn_gain).astype(jnp.bfloat16)
    reach = ancestry(parents)
    depth = jnp.sum(reach, axis=-1) - 1.0
    local_lengths = lax.dynamic_slice_in_dim(lengths, block_index * req_local, req_local, 0)
    positions = (local_lengths.astype(jnp.float32)[:, None] + depth).reshape(tok_rows)
    query_full = project_rows(normed, w_query).reshape(tok_rows, heads_here, NOPE + ROPE)
    queries = jnp.concatenate(
        [query_full[..., :NOPE], rotate(query_full[..., NOPE:], positions)], axis=-1
    ).astype(jnp.bfloat16)
    latent_part = project_rows(normed, w_latent)
    compressed = lax.all_gather(latent_part, "head", axis=1, tiled=True)
    draft_rows = jnp.concatenate(
        [
            rms_scale(compressed[:, :RANK], kv_gain),
            rotate(compressed[:, None, RANK:], positions)[:, 0],
        ],
        axis=-1,
    ).astype(jnp.bfloat16)
    chosen = (jnp.arange(req_local, dtype=jnp.int32)[:, None] * draft_len + accepted).reshape(-1)
    all_queries, all_chosen, all_targets = (
        lax.all_gather(
            queries.reshape(tok_rows, heads_here * (NOPE + ROPE)), "blk", axis=0, tiled=True
        ),
        lax.all_gather(draft_rows[chosen], "blk", axis=0, tiled=True),
        lax.all_gather(new_slots.reshape(-1), "blk", axis=0, tiled=True),
    )
    local_target = all_targets - block_index * NEW_DEV
    local_target = jnp.where((local_target >= 0) & (local_target < NEW_DEV), local_target, NEW_DEV)
    new_rows = (
        jnp.zeros((NEW_DEV, RANK + ROPE), jnp.bfloat16)
        .at[local_target]
        .set(all_chosen, mode="drop")
    )
    cache_keys, cache_values = expand(cache_rows, w_key_up, w_value_up)
    slot_count = slot_request.shape[0]
    block_len = cache_rows.shape[0] // slot_count
    owner = jnp.maximum(slot_request, 0)
    slot_queries = all_queries.reshape(requests, draft_len, heads_here, NOPE + ROPE)[owner]
    key_blocks = cache_keys.reshape(slot_count, block_len, heads_here, NOPE + ROPE)
    value_blocks = cache_values.reshape(slot_count, block_len, heads_here, VDIM)
    key_place = slot_block[:, None] * block_len + jnp.arange(block_len, dtype=jnp.int32)[None, :]
    live = (key_place < lengths[owner][:, None]) & (slot_request >= 0)[:, None]
    scores = (
        jnp.einsum("sqhd,skhd->sqhk", slot_queries, key_blocks, preferred_element_type=jnp.float32)
        * scale
    )
    weights = jnp.where(live[:, None, None, :], jnp.exp(scores), 0.0)
    slot_denom = jnp.sum(weights, axis=-1)
    slot_numer = jnp.einsum(
        "sqhk,skhv->sqhv",
        weights.astype(jnp.bfloat16),
        value_blocks,
        preferred_element_type=jnp.float32,
    )
    selector = (slot_request[None, :] == jnp.arange(requests, dtype=jnp.int32)[:, None]).astype(
        jnp.float32
    )
    numer_out = jnp.einsum(
        "rs,sqhv->rqhv", selector, slot_numer, precision=lax.Precision.HIGHEST
    ).reshape(requests * draft_len, heads_here * VDIM)
    denom_out = jnp.einsum(
        "rs,sqh->rqh", selector, slot_denom, precision=lax.Precision.HIGHEST
    ).reshape(requests * draft_len, heads_here)
    numer_in, denom_in = (
        lax.all_to_all(numer_out, "blk", split_axis=0, concat_axis=0, tiled=True),
        lax.all_to_all(denom_out, "blk", split_axis=0, concat_axis=0, tiled=True),
    )
    numer_far = numer_in.reshape(block_count, tok_rows, heads_here * VDIM).sum(axis=0)
    denom_far = denom_in.reshape(block_count, tok_rows, heads_here).sum(axis=0)
    draft_keys, draft_values = expand(draft_rows, w_key_up, w_value_up)
    own_keys = draft_keys.reshape(req_local, draft_len, heads_here, NOPE + ROPE)
    own_values = draft_values.reshape(req_local, draft_len, heads_here, VDIM)
    own_queries = queries.reshape(req_local, draft_len, heads_here, NOPE + ROPE)
    own_scores = (
        jnp.einsum("rqhd,rkhd->rqhk", own_queries, own_keys, preferred_element_type=jnp.float32)
        * scale
    )
    own_weights = jnp.where((reach > 0.5)[:, :, None, :], jnp.exp(own_scores), 0.0)
    denom = jnp.sum(own_weights, axis=-1).reshape(tok_rows, heads_here) + denom_far
    numer = jnp.einsum(
        "rqhk,rkhv->rqhv",
        own_weights.astype(jnp.bfloat16),
        own_values,
        preferred_element_type=jnp.float32,
    ).reshape(tok_rows, heads_here, VDIM)
    numer = numer + numer_far.reshape(tok_rows, heads_here, VDIM)
    attended = (numer / denom[..., None]).astype(jnp.bfloat16).reshape(tok_rows, heads_here * VDIM)
    attn_sum = lax.psum(jnp.dot(attended, w_out, preferred_element_type=jnp.float32), "head")
    resid = (hidden_in.astype(jnp.float32) + attn_sum).astype(jnp.bfloat16)
    moe_in = rms_scale(resid, moe_gain).astype(jnp.bfloat16)
    sigma = jax.nn.sigmoid(route_logits)
    route_weight = (ROUTE_SCALE * sigma / jnp.sum(sigma, axis=-1, keepdims=True)).reshape(-1)
    local_experts = w_gate.shape[0]
    expert_total = local_experts * block_count
    capacity = 2 * tok_rows * top_count // expert_total
    flat_routes = routes.reshape(-1)
    onehot = (flat_routes[:, None] == jnp.arange(expert_total, dtype=jnp.int32)[None, :]).astype(
        jnp.int32
    )
    rank = jnp.sum((jnp.cumsum(onehot, axis=0) - onehot) * onehot, axis=-1)
    slot_ids = flat_routes * capacity + rank
    source_rows = (
        jnp.full((expert_total * capacity,), tok_rows, jnp.int32)
        .at[slot_ids]
        .set(jnp.arange(tok_rows * top_count, dtype=jnp.int32) // top_count)
    )
    moe_pad = jnp.concatenate([moe_in, jnp.zeros((1, model_width), jnp.bfloat16)], axis=0)
    send_rows = moe_pad[source_rows]
    received = lax.all_to_all(send_rows, "blk", split_axis=0, concat_axis=0, tiled=True)
    grouped = received.reshape(block_count, local_experts, capacity, model_width)
    gate_val = jnp.einsum("sjcd,jfd->sjcf", grouped, w_gate, preferred_element_type=jnp.float32)
    up_val = jnp.einsum("sjcd,jfd->sjcf", grouped, w_up, preferred_element_type=jnp.float32)
    act = (jax.nn.silu(gate_val) * up_val).astype(jnp.bfloat16)
    expert_out = jnp.einsum(
        "sjcf,jfd->sjcd", act, w_down, preferred_element_type=jnp.float32
    ).reshape(block_count * local_experts * capacity, model_width)
    back = lax.all_to_all(expert_out, "blk", split_axis=0, concat_axis=0, tiled=True)
    routed_part = (
        (back[slot_ids] * route_weight[:, None])
        .reshape(tok_rows, top_count, model_width)
        .sum(axis=1)
    )
    routed = lax.psum(routed_part, "head")
    layer_out = (resid.astype(jnp.float32) + routed).astype(jnp.bfloat16)
    return (layer_out, new_rows)


def solution(mesh):
    return jax.shard_map(
        shards,
        mesh=mesh,
        in_specs=(
            P("blk", None),
            P(),
            P("head", None),
            P("head", None),
            P(),
            P(None, "head"),
            P(None, "head"),
            P("head", None),
            P("blk", None),
            P("blk"),
            P("blk"),
            P(),
            P("blk", None),
            P("blk", None),
            P("blk", None),
            P(),
            P("blk", None),
            P("blk", None),
            P("blk", "head", None),
            P("blk", "head", None),
            P("blk", "head", None),
        ),
        out_specs=(P("blk", None), P("blk", None)),
        check_vma=False,
    )
```

profile of v0, /device:TPU:0, one launch (start us, length us, event | category | flops | bytes accessed | tf_op | source)
XLA Modules:
  0.0 325.3 jit_solution(3864422452794586233)
XLA Ops:
  20.8 2.3 convolution_convert_fusion
  25.1 27.0 %all_gather.13 = bf16[512,768]{1,0:T(8,128)(2,1)} all-gather(bf16[32,768]{1,0:T(8,128)(2,1)} %convert_element_type.121), channel_id=1, replica_groups=mesh['head'=2,'blk'=16] {'blk'}, dimensions={0}, use_global_device_ids=true | all-gather | bytes 835584 | tf_op jit(solution)/shard_map/all_gather | solution.py:127
  52.2 3.4 %reshape.528 = bf16[16,32,4,192]{3,2,1,0:T(4,128)(2,1)} reshape(bf16[512,768]{1,0:T(8,128)(2,1)} %all_gather.13) | data formatting | bytes 1572864 | tf_op jit(solution)/shard_map/reshape | solution.py:144
  55.6 2.5 copy.84
  60.8 2.0 fusion.95
  63.8 3.5 %all-to-all-start.1 = ((f32[16,1,128]{2,1,0:T(1,128)}), f32[16,1,128]{2,1,0:T(1,128)S(1)}, u32[]{:S(2)}, u32[]{:S(2)}) async-start(f32[16,1,128]{2,1,0:T(1,128)} %reshape.622), calls=%async_computation.1 | async-start | bytes 16384 | tf_op jit(solution)/shard_map/all_to_all | solution.py:172
  71.2 4.8 %all-gather.2 = f32[2,288,32]{1,2,0:T(8,128)S(1)} all-gather(f32[1,288,32]{1,2,0:T(8,128)S(1)} %convolution_bitcast_fusion.2), channel_id=1, replica_groups=mesh['head'=2,'blk'=16] {'head'}, dimensions={0}, use_global_device_ids=true | all-gather | bytes 110592 | tf_op jit(solution)/shard_map/all_gather | solution.py:117
  76.3 2.3 convolution_convert_fusion.1
  85.1 2.7 copy.87
  87.8 2.6 all_to_all.22
  90.5 6.2 %all-to-all-start = ((f32[16,32,512]{2,1,0:T(8,128)}), f32[16,32,512]{2,1,0:T(8,128)}, u32[]{:S(2)}, u32[]{:S(2)}) async-start(f32[16,32,512]{2,1,0:T(8,128)} %all_to_all.22), calls=%async_computation | async-start | bytes 2097152 | tf_op jit(solution)/shard_map/all_to_all | solution.py:171
  105.3 14.4 %all-to-all-done = f32[16,32,512]{2,1,0:T(8,128)} async-done(((f32[16,32,512]{2,1,0:T(8,128)}), f32[16,32,512]{2,1,0:T(8,128)}, u32[]{:S(2)}, u32[]{:S(2)}) %all-to-all-start) | async-done | bytes 1048608 | tf_op jit(solution)/shard_map/all_to_all | solution.py:171
  121.1 2.8 fusion.56
  123.9 25.5 %all-reduce.6.cloned.1.call-done = f32[32,2048]{1,0:T(8,128)} async-done(((f32[32,2048]{1,0:T(8,128)}), f32[32,2048]{1,0:T(8,128)}) %all-reduce.6.cloned.1.call-update) | async-done | bytes 262160 | tf_op jit(solution)/shard_map/psum | solution.py:194
  150.6 3.1 gather_fusion.2
  153.8 42.0 %all_to_all.33 = bf16[16,24,2048]{2,1,0:T(8,128)(2,1)S(1)} all-to-all(bf16[16,24,2048]{2,1,0:T(8,128)(2,1)} %bitcast.171), channel_id=1, replica_groups=mesh['head'=2,'blk'=16] {'blk'}, dimensions={0} | all-to-all | bytes 3145728 | tf_op jit(solution)/shard_map/all_to_all | solution.py:215
  196.9 2.6 fusion.6
  199.4 8.3 %fusion = f32[16,24,2048]{2,1,0:T(8,128)} fusion(bf16[1,704,2048]{2,1,0:T(8,128)(2,1)} %param.41, bf16[16,24,2048]{2,1,0:T(8,128)(2,1)} %copy-done.3, bf16[1,704,2048]{2,1,0:T(8,128)(2,1)} %param.40, f32[16,1,24,704]{3,2,0,1:T(8,128)} %fusion.6), kind=kOutput, calls=%fused_computation.7 | convolution fusion | flops 2216214528 | bytes 11567104 | tf_op jit(solution)/shard_map/sjcf,jfd->sjcd/dot_general | solution.py:220
  207.7 5.2 %all-to-all-start.3 = ((f32[16,24,2048]{2,1,0:T(8,128)}), f32[16,24,2048]{2,1,0:T(8,128)}, u32[]{:S(2)}, u32[]{:S(2)}) async-start(f32[16,24,2048]{2,1,0:T(8,128)} %fusion), calls=%async_computation.3 | async-start | bytes 6291456 | tf_op jit(solution)/shard_map/all_to_all | solution.py:223
  215.2 69.5 %all-reduce.2 = s32[128]{0:T(128)S(1)} all-reduce(s32[128]{0:T(128)S(1)} %bitcast_dynamic-update-slice_fusion), channel_id=2, replica_groups=mesh['head'=2,'blk'=16] {'blk'}, use_global_device_ids=true, to_apply=%add.2 | all-reduce | flops 128 | bytes 1024
  284.7 4.9 %gather_fusion.3 = f32[192,2048]{1,0:T(8,128)} fusion(f32[384,2048]{1,0:T(8,128)} %bitcast.37, s32[1024]{0:T(1024)S(1)} %pad_clamp_fusion.1), kind=kCustom, calls=%fused_computation.3 | custom fusion | bytes 3146496 | tf_op jit(solution)/shard_map/gather | solution.py:225
  289.6 2.7 gather.21
  292.3 3.1 multiply_reduce_fusion
  295.3 19.8 %all-gather.1 = bf16[128,576]{1,0:T(8,128)(2,1)S(1)} all-gather(bf16[8,576]{1,0:T(8,128)(2,1)S(1)} %gather_fusion.4), channel_id=3, replica_groups=mesh['head'=2,'blk'=16] {'blk'}, dimensions={0}, use_global_device_ids=true | all-gather | bytes 156672 | tf_op jit(solution)/shard_map/all_gather | solution.py:130
  (172 shorter events, 46.4 us)
Async XLA Ops:
  10.8 5.3 %copy-start.26 = (s32[1,32]{1,0:T(1,128)S(1)}, s32[1,32]{1,0:T(1,128)}, u32[]{:S(2)}) copy-start(s32[1,32]{1,0:T(1,128)} %param.33) | copy-start | bytes 388
  55.6 7.2 %copy-start.24 = (s32[3]{0:T(128)S(1)}, s32[3]{0:T(128)}, u32[]{:S(2)}) copy-start(s32[3]{0:T(128)} %param.30) | copy-start | bytes 40
  58.1 11.4 %copy-start.2 = (bf16[32,2048]{1,0:T(8,128)(2,1)S(1)}, bf16[32,2048]{1,0:T(8,128)(2,1)}, u32[]{:S(2)}) copy-start(bf16[32,2048]{1,0:T(8,128)(2,1)} %param.21) | copy-start | bytes 393220
  58.1 11.4 %copy-start.10 = (f32[2048]{0:T(1024)S(1)}, f32[2048]{0:T(1024)}, u32[]{:S(2)}) copy-start(f32[2048]{0:T(1024)} %param.22) | copy-start | bytes 24580
  63.8 26.7 %all-to-all-start.1 = ((f32[16,1,128]{2,1,0:T(1,128)}), f32[16,1,128]{2,1,0:T(1,128)S(1)}, u32[]{:S(2)}, u32[]{:S(2)}) async-start(f32[16,1,128]{2,1,0:T(1,128)} %reshape.622), calls=%async_computation.1 | async-start | bytes 16384 | tf_op jit(solution)/shard_map/all_to_all | solution.py:172
  68.8 9.8 %copy-start.13 = (s32[192]{0:T(256)}, s32[192]{0:T(256)S(1)}, u32[]{:S(2)}) copy-start(s32[192]{0:T(256)S(1)} %eq.99) | copy-start | bytes 2308
  76.2 5.5 %copy-start.25 = (s32[3]{0:T(128)S(1)}, s32[3]{0:T(128)}, u32[]{:S(2)}) copy-start(s32[3]{0:T(128)} %param.30) | copy-start | bytes 40
  85.1 5.3 %copy-start.20 = (s32[16,3]{0,1:T(4,128)}, s32[16,3]{0,1:T(4,128)S(1)}, u32[]{:S(2)}) copy-start(s32[16,3]{0,1:T(4,128)S(1)} %reduce-window.9) | copy-start | bytes 580
  90.4 7.5 %copy-start.17 = (f32[32]{0:T(128)S(1)}, f32[32]{0:T(128)}, u32[]{:S(2)}) copy-start(f32[32]{0:T(128)} %copy-done.16) | copy-start | bytes 388
  90.5 7.5 %copy-start.19 = (f32[32]{0:T(128)S(1)}, f32[32]{0:T(128)}, u32[]{:S(2)}) copy-start(f32[32]{0:T(128)} %copy-done.18) | copy-start | bytes 388
  90.5 9.0 %copy-start.5 = (bf16[32,4,192]{2,0,1:T(8,128)(2,1)S(1)}, bf16[32,4,192]{2,0,1:T(8,128)(2,1)}, u32[]{:S(2)}) copy-start(bf16[32,4,192]{2,0,1:T(8,128)(2,1)} %copy-done.4) | copy-start | bytes 147460
  90.5 7.8 %copy-start.11 = (f32[16,1,128]{2,1,0:T(1,128)}, f32[16,1,128]{2,1,0:T(1,128)S(1)}, u32[]{:S(2)}) copy-start(f32[16,1,128]{2,1,0:T(1,128)S(1)} %all-to-all-done.1) | copy-start | bytes 24580
  90.5 29.2 %all-to-all-start = ((f32[16,32,512]{2,1,0:T(8,128)}), f32[16,32,512]{2,1,0:T(8,128)}, u32[]{:S(2)}, u32[]{:S(2)}) async-start(f32[16,32,512]{2,1,0:T(8,128)} %all_to_all.22), calls=%async_computation | async-start | bytes 2097152 | tf_op jit(solution)/shard_map/all_to_all | solution.py:171
  96.7 52.7 %all-reduce.6.cloned.1.call-start = ((), (), s32[]{:S(2)}) async-start(), calls=%async_computation.4 | async-start | bytes 524288 | tf_op jit(solution)/shard_map/psum | solution.py:194
  98.2 25.6 %copy-start.8 = (bf16[32,64]{1,0:T(8,128)(2,1)}, bf16[32,64]{1,0:T(8,128)(2,1)S(1)}, u32[]{:S(2)}) copy-start(bf16[32,64]{1,0:T(8,128)(2,1)S(1)} %maximum_bitcast_fusion) | copy-start | bytes 12292
  121.0 29.4 %copy-start.14 = (f32[2048]{0:T(1024)S(1)}, f32[2048]{0:T(1024)}, u32[]{:S(2)}) copy-start(f32[2048]{0:T(1024)} %param.36) | copy-start | bytes 24580
  153.8 43.1 %copy-start.27 = (bf16[1,704,2048]{2,1,0:T(8,128)(2,1)S(1)}, bf16[1,704,2048]{2,1,0:T(8,128)(2,1)}, u32[]{:S(2)}) copy-start(bf16[1,704,2048]{2,1,0:T(8,128)(2,1)} %param.39) | copy-start | bytes 8650756
  207.7 5.3 %copy-start.12 = (f32[32,6]{0,1:T(8,128)S(1)}, f32[32,6]{0,1:T(8,128)}, u32[]{:S(2)}) copy-start(f32[32,6]{0,1:T(8,128)} %param.38) | copy-start | bytes 2308
  207.7 5.4 %copy-start.31 = (u32[32]{0:T(128)S(1)}, u32[32]{0:T(128)}, u32[]{:S(2)}) copy-start(u32[32]{0:T(128)} %constant.93) | copy-start | bytes 388
  207.7 6.7 %copy-start.29 = (s32[1,8]{1,0:T(1,128)S(1)}, s32[1,8]{1,0:T(1,128)}, u32[]{:S(2)}) copy-start(s32[1,8]{1,0:T(1,128)} %param.34) | copy-start | bytes 100
  207.7 6.7 %copy-start.9 = (bf16[32,64]{1,0:T(8,128)(2,1)S(1)}, bf16[32,64]{1,0:T(8,128)(2,1)}, u32[]{:S(2)}) copy-start(bf16[32,64]{1,0:T(8,128)(2,1)} %copy-done.8) | copy-start | bytes 12292
  207.7 7.3 %copy-start.30 = (s32[1,8]{1,0:T(1,128)S(1)}, s32[1,8]{1,0:T(1,128)}, u32[]{:S(2)}) copy-start(s32[1,8]{1,0:T(1,128)} %param.35) | copy-start | bytes 100
  207.7 77.0 %all-to-all-start.3 = ((f32[16,24,2048]{2,1,0:T(8,128)}), f32[16,24,2048]{2,1,0:T(8,128)}, u32[]{:S(2)}, u32[]{:S(2)}) async-start(f32[16,24,2048]{2,1,0:T(8,128)} %fusion), calls=%async_computation.3 | async-start | bytes 6291456 | tf_op jit(solution)/shard_map/all_to_all | solution.py:223
  213.0 103.8 %all-reduce.8.cloned.1.call-start = ((), (), s32[]{:S(2)}) async-start(), calls=%async_computation.5 | async-start | bytes 524288 | tf_op jit(solution)/shard_map/psum | solution.py:229
  (14 other events, 39.9 us)
Sparse Core Ops, SparseCore 0:
  124.0 25.3 all-reduce.5
  295.5 21.2 all-reduce.7
where the time goes:
time: 327 us; the launch traced here: 325 us
  blocking collectives  163 us (50%)
  local copies, waits for them, and re-layouts  43.3 us (13%)
  waiting for transfers between devices  39.9 us (12%)
  matrix products  31.6 us (10%)
  other arithmetic  16.5 us (5%)
  between operations  15.9 us (5%)
  starting transfers between devices  14.9 us (5%)
    unnamed x1, blocking collectives  69.5 us
    all_to_all x1, blocking collectives, shards(): lax.all_to_all(send_rows, 'blk', split_axis=0, concat_axis=0, tiled=True)  42 us
    all_gather x1, blocking collectives, shards(): lax.all_gather(queries.reshape(tok_rows, heads_here * (NOPE + ROPE)), 'bl...  27 us
    psum x1, waiting for transfers between devices, shards(): lax.psum(jnp.dot(attended, w_out, preferred_element_type=jnp.float32), 'h...  25.5 us
    all_gather x1, blocking collectives, shards(): lax.all_gather(draft_rows[chosen], 'blk', axis=0, tiled=True)  19.8 us
    all_to_all x1, waiting for transfers between devices, shards(): lax.all_to_all(numer_out, 'blk', split_axis=0, concat_axis=0, tiled=True)  14.4 us
    dot_general x1, matrix products, shards(): jnp.einsum('sjcf,jfd->sjcd', act, w_down, preferred_element_type=jnp.floa...  8.28 us
    gather x2, local copies, waits for them, and re-layouts, shards(): back[slot_ids] * route_weight[:, None]  7.57 us
  transfers between devices with their start and end apart: 5, of which 2 were waited for; matrix products, arithmetic and copies ran while one was open for 8% of the time, Pallas kernels for 0%

commit v1 on v0

v1 whole, which is shorter than its diff:
```python
import functools

import jax
import jax.numpy as jnp
from jax import lax
from jax.experimental import pallas as pl
from jax.experimental.pallas import tpu as pltpu
from jax.sharding import PartitionSpec as P

NOPE = 128
ROPE = 64
HALF = ROPE // 2
VDIM = 128
RANK = 512
NEW_DEV = 16
LANES = 128

EPSILON = 1e-06
ROUTE_SCALE = 2.446
ROPE_BASE = 50000.0
MIB = 1 << 20

f32 = jnp.float32
bf16 = jnp.bfloat16


def params(mib):
    return pltpu.CompilerParams(vmem_limit_bytes=mib * MIB)


def cost(flops, nbytes, trans=0):
    return pl.CostEstimate(flops=flops, bytes_accessed=nbytes, transcendentals=trans)


def nt(left, right):
    return lax.dot_general(left, right, (((1,), (1,)), ((), ())), preferred_element_type=f32)


def nn(left, right):
    return jnp.dot(left, right, preferred_element_type=f32)


def phases(count):
    out, stride = [], count
    while stride > 1:
        radix = 4 if stride == count and count >= 4 else 2
        stride //= radix
        out.append((radix, stride))
    return out


def swap(value, axis, bit):
    count = lax.axis_size(axis)
    return lax.ppermute(value, axis, [(i, i ^ bit) for i in range(count)])


def gather_blocks(value, count):
    (radix, stride), *rest = phases(count)
    pieces = [jnp.stack([value] + [swap(value, "blk", stride * j) for j in range(1, radix)])]
    for _, stride in rest:
        pieces = pieces + [swap(p, "blk", stride) for p in pieces]
    return pieces


def add16(left, right):
    return (left.astype(f32) + right.astype(f32)).astype(bf16)


def scatter_blocks(pieces, count):
    (radix, stride0), *rest = phases(count)
    for _, stride in reversed(rest):
        half = len(pieces) // 2
        got = [swap(p, "blk", stride) for p in pieces[half:]]
        pieces = [add16(p, g) for p, g in zip(pieces[:half], got)]
    (last,) = pieces
    return [last[0]] + [swap(last[j], "blk", stride0 * j) for j in range(1, radix)]


def place_of(relative, count):
    (radix, stride), *rest = phases(count)
    place = relative // stride
    size = radix
    for _, step in rest:
        place = place + (relative // step) % 2 * size
        size *= 2
    return place


def pre_kernel(
    heads, experts, place_ref, len_ref, hidden_ref, gain_ref, parents_ref, routes_ref, logits_ref,
    query_hbm, latent_hbm, out_ref, latent_ref, trig_ref, reach_ref, wq, wl, sems,
):
    copy_q = pltpu.make_async_copy(query_hbm, wq, sems.at[0])
    copy_l = pltpu.make_async_copy(latent_hbm, wl, sems.at[1])
    copy_q.start()
    copy_l.start()
    tok = hidden_ref.shape[0]
    rows = lax.broadcasted_iota(jnp.int32, (tok, tok), 0)
    cols = lax.broadcasted_iota(jnp.int32, (tok, tok), 1)
    eye = (rows == cols).astype(f32)
    below = jnp.where(rows == parents_ref[...], 1.0, 0.0) + eye
    for _ in range(max(1, (tok - 1).bit_length())):
        step = below.astype(bf16)
        below = jnp.minimum(nn(step, step), 1.0)
    reach = nt(eye.astype(bf16), below.astype(bf16))
    reach_ref[...] = reach
    depth = jnp.sum(reach, axis=-1, keepdims=True) - 1.0
    position = len_ref[place_ref[0]].astype(f32) + depth
    lane = lax.broadcasted_iota(jnp.int32, (1, LANES), 1)
    freqs = ROPE_BASE ** (-2.0 * (lane % HALF).astype(f32) / ROPE)
    angles = position * freqs
    cosine, sine = jnp.cos(angles), jnp.sin(angles)
    trig_ref[:, :LANES] = cosine
    trig_ref[:, LANES:] = sine
    sigma = jax.nn.sigmoid(logits_ref[...])
    weight = ROUTE_SCALE * sigma / jnp.sum(sigma, axis=-1, keepdims=True)
    mix = jnp.zeros((tok, LANES), f32)
    for k in range(weight.shape[1]):
        mix = mix + jnp.where(lane % experts == routes_ref[:, k : k + 1], weight[:, k : k + 1], 0.0)
    high = mix.astype(bf16).astype(f32)
    mix = jnp.where(lane < experts, high, jnp.where(lane < 2 * experts, mix - high, 0.0))
    hidden = hidden_ref[...].astype(f32)
    mean_square = jnp.mean(hidden * hidden, axis=-1, keepdims=True)
    normed = (hidden * lax.rsqrt(mean_square + EPSILON) * gain_ref[...]).astype(bf16)
    copy_q.wait()
    size = NOPE + ROPE
    for h in range(heads):
        part = nt(normed, wq[h * size : h * size + NOPE])
        out_ref[:, h * NOPE : (h + 1) * NOPE] = part.astype(bf16)
    pad = [jnp.zeros((LANES - heads * HALF, wq.shape[1]), bf16)] if heads * HALF < LANES else []
    first, second = (
        nt(normed, jnp.concatenate(
            [wq[h * size + NOPE + at : h * size + NOPE + at + HALF] for h in range(heads)] + pad))
        for at in (0, HALF)
    )
    base = heads * NOPE
    out_ref[:, base : base + LANES] = (first * cosine - second * sine).astype(bf16)
    out_ref[:, base + LANES : base + 2 * LANES] = (second * cosine + first * sine).astype(bf16)
    out_ref[:, base + 2 * LANES :] = mix.astype(bf16)
    copy_l.wait()
    latent_ref[...] = nt(normed, wl[...])


def prepare(place, lengths, hidden, gain, parents, routes, logits, w_query, w_latent, heads, experts):
    tok, width = hidden.shape
    smem = pl.BlockSpec(memory_space=pltpu.SMEM)
    vmem = pl.BlockSpec(memory_space=pltpu.VMEM)
    anyw = pl.BlockSpec(memory_space=pl.ANY)
    lanes = heads * NOPE + 3 * LANES
    return pl.pallas_call(
        functools.partial(pre_kernel, heads, experts),
        out_shape=(
            jax.ShapeDtypeStruct((tok, lanes), bf16),
            jax.ShapeDtypeStruct((tok, w_latent.shape[0]), f32),
            jax.ShapeDtypeStruct((tok, 2 * LANES), f32),
            jax.ShapeDtypeStruct((tok, tok), f32),
        ),
        in_specs=[smem, smem, vmem, vmem, vmem, vmem, vmem, anyw, anyw],
        out_specs=(vmem,) * 4,
        scratch_shapes=[
            pltpu.VMEM(w_query.shape, bf16),
            pltpu.VMEM(w_latent.shape, bf16),
            pltpu.SemaphoreType.DMA((2,)),
        ],
        compiler_params=params(24),
        cost_estimate=cost(2 * tok * width * 1100, 2 * width * 1100),
        name="prepare",
    )(place, lengths, hidden, gain[None], parents, routes, logits, w_query, w_latent)


def spread(heads):
    row = lax.broadcasted_iota(jnp.int32, (ROPE, 2 * LANES), 0)
    col = lax.broadcasted_iota(jnp.int32, (ROPE, 2 * LANES), 1)
    inside = col % LANES < heads * HALF
    return jnp.where((row == col // LANES * HALF + col % HALF) & inside, 1.0, 0.0).astype(bf16)


def keys_values(rows, key_up, value_up, heads):
    low = rows[:, :RANK]
    nope = nn(low, key_up).astype(bf16)
    rope = nn(rows[:, RANK:], spread(heads)).astype(bf16)
    return jnp.concatenate([nope, rope], axis=-1), nn(low, value_up).astype(bf16)


def expand_kernel(heads, rows_ref, key_ref, value_ref, keys_out, values_out):
    keys_out[...], values_out[...] = keys_values(rows_ref[...], key_ref[...], value_ref[...], heads)


def expand(rows, key_up, value_up, heads):
    vmem = pl.BlockSpec(memory_space=pltpu.VMEM)
    count = rows.shape[0]
    return pl.pallas_call(
        functools.partial(expand_kernel, heads),
        out_shape=(
            jax.ShapeDtypeStruct((count, heads * NOPE + 2 * LANES), bf16),
            jax.ShapeDtypeStruct((count, heads * VDIM), bf16),
        ),
        in_specs=[vmem] * 3,
        out_specs=(vmem,) * 2,
        compiler_params=params(16),
        cost_estimate=cost(4 * count * RANK * heads * NOPE, 4 * count * RANK),
        name="expand",
    )(rows, key_up, value_up)


def by_head(query, heads):
    tok, lanes = query.shape[0], heads * NOPE + 2 * LANES
    lane = lax.broadcasted_iota(jnp.int32, (1, lanes), 1)
    head = jnp.where(lane < heads * NOPE, lane // NOPE, lane % LANES // HALF)
    query = query[:, :lanes].astype(f32)
    return jnp.concatenate(
        [jnp.where(head == h, query, 0.0) for h in range(heads)], axis=0
    ).astype(bf16)


def attend(query, keys, values, seen, heads):
    tok = query.shape[0] // heads
    scale = (NOPE + ROPE) ** (-0.5)
    weight = jnp.where(seen, jnp.exp(nt(query, keys) * scale), 0.0)
    high = weight.astype(bf16)
    low = (weight - high.astype(f32)).astype(bf16)
    full = nn(high, values)
    numer = jnp.concatenate(
        [full[h * tok : (h + 1) * tok, h * VDIM : (h + 1) * VDIM] for h in range(heads)], axis=0
    )
    ones = jnp.ones((16, keys.shape[0]), bf16)
    denom = nt(ones, high) + nt(ones, low)
    if denom.shape[1] < LANES:
        denom = jnp.concatenate([denom, jnp.zeros((16, LANES - denom.shape[1]), f32)], axis=-1)
    return jnp.concatenate([numer, denom], axis=0)


def slots_kernel(heads, slots, block, pieces, place_ref, live_ref, keys_ref, values_ref, *refs):
    queries, outs = refs[:pieces], refs[pieces:]
    each = queries[0].shape[0]
    for out in outs:
        out[...] = jnp.zeros(out.shape, out.dtype)
    parts = []
    lane = lax.broadcasted_iota(jnp.int32, (1, block), 1)
    for s in range(slots):
        place = place_ref[s]
        query = queries[0][place % each]
        for p in range(1, pieces):
            query = jnp.where(place // each == p, queries[p][place % each], query)
        keys, values = (r[s * block : (s + 1) * block] for r in (keys_ref, values_ref))
        parts.append(attend(by_head(query, heads), keys, values, lane < live_ref[s], heads))
    for s in range(slots):
        place = place_ref[s]
        total = parts[s]
        for other in range(slots):
            if other != s:
                total = total + jnp.where(place_ref[other] == place, parts[other], 0.0)
        for p, out in enumerate(outs):
            @pl.when(place // each == p)
            def _():
                out[place % each] = total.astype(bf16)


def attend_slots(place, live, keys, values, queries, heads, block):
    smem = pl.BlockSpec(memory_space=pltpu.SMEM)
    vmem = pl.BlockSpec(memory_space=pltpu.VMEM)
    slots, each, tok = place.shape[0], queries[0].shape[0], queries[0].shape[1]
    out = jax.ShapeDtypeStruct((each, heads * tok + 16, LANES), bf16)
    return pl.pallas_call(
        functools.partial(slots_kernel, heads, slots, block, len(queries)),
        out_shape=(out,) * len(queries),
        in_specs=[smem, smem, vmem, vmem] + [vmem] * len(queries),
        out_specs=(vmem,) * len(queries),
        compiler_params=params(24),
        cost_estimate=cost(1 << 28, 2 << 20),
        name="attend_slots",
    )(place, live, keys, values, *queries)


def own_kernel(heads, rows_ref, query_ref, reach_ref, key_ref, value_ref, out_ref):
    keys, values = keys_values(rows_ref[...], key_ref[...], value_ref[...], heads)
    seen = jnp.concatenate([reach_ref[...]] * heads, axis=0) > 0.5
    out_ref[...] = attend(by_head(query_ref[...], heads), keys, values, seen, heads)


def attend_own(rows, query, reach, key_up, value_up, heads):
    vmem = pl.BlockSpec(memory_space=pltpu.VMEM)
    return pl.pallas_call(
        functools.partial(own_kernel, heads),
        out_shape=jax.ShapeDtypeStruct((heads * rows.shape[0] + 16, LANES), f32),
        in_specs=[vmem] * 5,
        out_specs=vmem,
        compiler_params=params(16),
        cost_estimate=cost(1 << 26, 2 << 20),
        name="attend_own",
    )(rows, query, reach, key_up, value_up)


def project_kernel(heads, parts, w_ref, own_ref, *refs):
    total = own_ref[...]
    for ref in refs[:parts]:
        total = total + ref[...].astype(f32)
    count = heads * (total.shape[0] - 16) // heads
    tok = count // heads
    row = lax.broadcasted_iota(jnp.int32, (count, LANES), 0)
    col = lax.broadcasted_iota(jnp.int32, (count, LANES), 1)
    denom = jnp.sum(jnp.where(row == col, total[count : count + 1], 0.0), axis=-1, keepdims=True)
    attended = (total[:count] / denom).astype(bf16)
    wide = jnp.concatenate([attended[h * tok : (h + 1) * tok] for h in range(heads)], axis=-1)
    refs[parts][...] = nn(wide, w_ref[...]).astype(bf16)


def project_out(w_out, own, parts, heads, tok):
    vmem = pl.BlockSpec(memory_space=pltpu.VMEM)
    return pl.pallas_call(
        functools.partial(project_kernel, heads, len(parts)),
        out_shape=jax.ShapeDtypeStruct((tok, w_out.shape[1]), bf16),
        in_specs=[vmem] * (2 + len(parts)),
        out_specs=vmem,
        compiler_params=params(16),
        cost_estimate=cost(2 * tok * w_out.size, 2 * w_out.size),
        name="project_out",
    )(w_out, own, *parts)


def norm_kernel(hidden_ref, mine_ref, other_ref, gain_ref, resid_ref, out_ref):
    added = mine_ref[...].astype(f32) + other_ref[...].astype(f32)
    resid = (hidden_ref[...].astype(f32) + added).astype(bf16)
    resid_ref[...] = resid
    value = resid.astype(f32)
    mean_square = jnp.mean(value * value, axis=-1, keepdims=True)
    out_ref[...] = (value * lax.rsqrt(mean_square + EPSILON) * gain_ref[...]).astype(bf16)


def norm(hidden, mine, other, gain):
    out = jax.ShapeDtypeStruct(hidden.shape, bf16)
    vmem = pl.BlockSpec(memory_space=pltpu.VMEM)
    return pl.pallas_call(
        norm_kernel, out_shape=(out, out), in_specs=[vmem] * 4, out_specs=(vmem, vmem),
        compiler_params=params(16), name="norm",
    )(hidden, mine, other, gain[None])


def expert_kernel(
    experts, index_ref, low_ref, high_ref, mix_low, mix_high, gate_hbm, up_hbm, down_hbm,
    out_low, out_high, gate, up, down, sems,
):
    copies = [
        pltpu.make_async_copy(src.at[0], dst, sems.at[i])
        for i, (src, dst) in enumerate(((gate_hbm, gate), (up_hbm, up), (down_hbm, down)))
    ]
    for copy in copies:
        copy.start()
    each, tok, width = low_ref.shape
    rows = jnp.concatenate(
        [r[...].reshape(each * tok, width) for r in (low_ref, high_ref)], axis=0
    )
    mix = jnp.concatenate(
        [r[...].reshape(each * tok, LANES) for r in (mix_low, mix_high)], axis=0
    ).astype(f32)
    lane = lax.broadcasted_iota(jnp.int32, (1, LANES), 1)
    index = index_ref[0]
    mine = (lane == index) | (lane == index + experts)
    weight = jnp.sum(jnp.where(mine, mix, 0.0), axis=-1, keepdims=True)
    copies[0].wait()
    gated = nt(rows, gate[...])
    gated = gated / (1.0 + jnp.exp(-gated))
    copies[1].wait()
    act = (gated * nt(rows, up[...])).astype(bf16)
    copies[2].wait()
    out = (nn(act, down[...]) * weight).astype(bf16)
    out_low[...] = out[: each * tok].reshape(each, tok, width)
    out_high[...] = out[each * tok :].reshape(each, tok, width)


def expert(index, low, high, mix_low, mix_high, w_gate, w_up, w_down, experts):
    smem = pl.BlockSpec(memory_space=pltpu.SMEM)
    vmem = pl.BlockSpec(memory_space=pltpu.VMEM)
    anyw = pl.BlockSpec(memory_space=pl.ANY)
    each, tok, _ = low.shape
    last = mix_low.shape[-1] // LANES - 1
    mixed = pl.BlockSpec((each, tok, LANES), lambda i: (0, 0, last))
    out = jax.ShapeDtypeStruct(low.shape, bf16)
    whole = pl.BlockSpec(low.shape, lambda i: (0, 0, 0))
    return pl.pallas_call(
        functools.partial(expert_kernel, experts),
        grid=(1,),
        out_shape=(out, out),
        in_specs=[smem, whole, whole, mixed, mixed, anyw, anyw, anyw],
        out_specs=(whole, whole),
        scratch_shapes=[pltpu.VMEM(w.shape[1:], bf16) for w in (w_gate, w_up, w_down)]
        + [pltpu.SemaphoreType.DMA((3,))],
        compiler_params=params(40),
        cost_estimate=cost(12 * each * tok * w_gate.size, 6 * w_gate.size),
        name="expert",
    )(index, low, high, mix_low, mix_high, w_gate, w_up, w_down)


def sum_heads(value):
    count, bit = lax.axis_size("head"), 1
    other = swap(value, "head", bit)
    while 2 * bit < count:
        bit *= 2
        value = add16(value, other)
        other = swap(value, "head", bit)
    return value, other


def join_heads(value):
    if lax.axis_size("head") == 2:
        other = swap(value, "head", 1)
        first = lax.axis_index("head") == 0
        parts = [jnp.where(first, value, other), jnp.where(first, other, value)]
        return jnp.concatenate(parts, axis=1)
    return lax.all_gather(value, "head", axis=1, tiled=True)


def shards(
    hidden_in, attn_gain, w_query, w_latent, kv_gain, w_key_up, w_value_up, w_out, cache_rows,
    slot_request, slot_block, lengths, parents, accepted, new_slots, moe_gain, routes,
    route_logits, w_gate, w_up, w_down,
):
    count = lax.axis_size("blk")
    me = lax.axis_index("blk").astype(jnp.int32)
    tok = hidden_in.shape[0]
    heads = w_key_up.shape[1] // NOPE
    experts = w_gate.shape[0] * count
    index = me[None]
    payload, latent, trig, reach = prepare(
        index, lengths, hidden_in, attn_gain, parents, routes, route_logits, w_query, w_latent,
        heads, experts,
    )
    queries = gather_blocks(payload, count)

    compressed = join_heads(latent)
    low = compressed[:, :RANK]
    low = low * lax.rsqrt(jnp.mean(low * low, axis=-1, keepdims=True) + EPSILON) * kv_gain
    first, second = compressed[:, RANK : RANK + HALF], compressed[:, RANK + HALF :]
    cosine, sine = trig[:, :HALF], trig[:, LANES : LANES + HALF]
    draft_rows = jnp.concatenate(
        [low, first * cosine - second * sine, second * cosine + first * sine], axis=-1
    ).astype(bf16)

    keys, values = expand(cache_rows, w_key_up, w_value_up, heads)
    slots = slot_request.shape[0]
    block = cache_rows.shape[0] // slots
    owner = jnp.maximum(slot_request, 0)
    owner_length = jnp.sum(
        jnp.where(owner[:, None] == jnp.arange(lengths.shape[0])[None, :], lengths[None, :], 0), axis=1
    )
    live = jnp.where(slot_request >= 0, owner_length - slot_block * block, 0)
    place = place_of(owner ^ me, count)
    partial = attend_slots(place, live, keys, values, queries, heads, block)
    parts = scatter_blocks(list(partial), count)
    own = attend_own(draft_rows, payload, reach, w_key_up, w_value_up, heads)
    mine, other = sum_heads(project_out(w_out, own, parts, heads, tok))
    resid, moe_in = norm(hidden_in, mine, other, moe_gain)

    node = jnp.arange(tok, dtype=jnp.int32)
    pick = (accepted.reshape(-1)[:, None] == node[None, :]).astype(bf16)
    chosen = jnp.dot(pick, draft_rows, preferred_element_type=f32).astype(bf16)
    target = new_slots.reshape(-1, 1)
    tail = jnp.concatenate([target // 256, target % 256], axis=1).astype(bf16)
    sent = jnp.concatenate(
        [chosen, tail, jnp.zeros((chosen.shape[0], LANES - ROPE - 2), bf16)], axis=1
    )
    rows = jnp.concatenate(gather_blocks(sent, count)).reshape(-1, sent.shape[1])
    at = RANK + ROPE
    slot = rows[:, at].astype(f32) * 256.0 + rows[:, at + 1].astype(f32)
    here = (me * NEW_DEV + jnp.arange(NEW_DEV, dtype=jnp.int32)).astype(f32)
    new_rows = jnp.dot(
        (here[:, None] == slot[None, :]).astype(bf16), rows[:, :at], preferred_element_type=f32
    ).astype(bf16)

    tokens = gather_blocks(moe_in, count)
    half = len(tokens) // 2
    outs = [
        expert(index, tokens[i], tokens[i + half], queries[i], queries[i + half],
               w_gate, w_up, w_down, experts)
        for i in range(half)
    ]
    back = scatter_blocks([o[0] for o in outs] + [o[1] for o in outs], count)
    total = back[0].astype(f32)
    for value in back[1:]:
        total = total + value.astype(f32)
    mine, other = sum_heads(total.astype(bf16))
    routed = mine.astype(f32) + other.astype(f32)
    layer_out = (resid.astype(f32) + routed).astype(bf16)
    return (layer_out, new_rows)


def solution(mesh):
    return jax.shard_map(
        shards,
        mesh=mesh,
        in_specs=(
            P("blk", None),
            P(),
            P("head", None),
            P("head", None),
            P(),
            P(None, "head"),
            P(None, "head"),
            P("head", None),
            P("blk", None),
            P("blk"),
            P("blk"),
            P(),
            P("blk", None),
            P("blk", None),
            P("blk", None),
            P(),
            P("blk", None),
            P("blk", None),
            P("blk", "head", None),
            P("blk", "head", None),
            P("blk", "head", None),
        ),
        out_specs=(P("blk", None), P("blk", None)),
        check_vma=False,
    )
```

time: 327 us -> 140 us (0.43)
  blocking collectives: 163 us -> 0 us
  matrix products: 31.6 us -> 1 us
  local copies, waits for them, and re-layouts: 43.3 us -> 15.5 us
  waiting for transfers between devices: 39.9 us -> 65.2 us
  starting transfers between devices: 14.9 us -> 36.3 us
  Pallas kernels: 0 us -> 17.4 us
  between operations: 15.9 us -> 1.08 us
  other arithmetic: 16.5 us -> 3.14 us
    unnamed x1 -> x0, blocking collectives: 69.5 us -> none
    ppermute x0 -> x33, waiting for transfers between devices: none -> 65.2 us  [swap(): return lax.ppermute(value, axis, [(i, i ^ bit) for i in range(count)])]
    all_gather x3 -> x0, blocking collectives: 51.6 us -> none  [the longest x1 27 us: shards(): lax.all_gather(queries.reshape(tok_rows, heads_here * (NOPE + ROPE)), 'bl...]
    all_to_all x1 -> x0, blocking collectives: 42 us -> none  [shards(): lax.all_to_all(send_rows, 'blk', split_axis=0, concat_axis=0, tiled=True)]
    ppermute x0 -> x33, starting transfers between devices: none -> 36.3 us  [swap(): return lax.ppermute(value, axis, [(i, i ^ bit) for i in range(count)])]
    dot_general x21 -> x2, matrix products: 31.6 us -> 1 us  [the longest x1 0.81 us: shards(): jnp.dot((here[:, None] == slot[None, :]).astype(bf16), rows[:, :at], pref...]
    psum x2 -> x0, waiting for transfers between devices: 25.5 us -> none  [the longest x1 25.5 us: shards(): lax.psum(jnp.dot(attended, w_out, preferred_element_type=jnp.float32), 'h...]
    pallas_call x0 -> x8, Pallas kernels: none -> 17.4 us  [the longest x2 10.5 us: expert(): pl.pallas_call(functools.partial(expert_kernel, experts), grid=(1,), out_...]
  transfers between devices with their start and end apart: 5 -> 33, of which waited for: 2 -> 18; matrix products, arithmetic and copies ran while one was open for 8% -> 2% of each run, Pallas kernels for 0% -> 8%
where the time goes in v1:
time: 140 us
  waiting for transfers between devices  65.2 us (47%)
  starting transfers between devices  36.3 us (26%)
  Pallas kernels  17.4 us (12%)
  local copies, waits for them, and re-layouts  15.5 us (11%)
  other arithmetic  3.14 us (2%)
    ppermute x33, waiting for transfers between devices, swap(): return lax.ppermute(value, axis, [(i, i ^ bit) for i in range(count)])  65.2 us
    ppermute x33, starting transfers between devices, swap(): return lax.ppermute(value, axis, [(i, i ^ bit) for i in range(count)])  36.3 us
    unnamed x80, local copies, waits for them, and re-layouts  15.2 us
    pallas_call x2, Pallas kernels, expert(): pl.pallas_call(functools.partial(expert_kernel, experts), grid=(1,), out_...  10.5 us
    pallas_call x1, Pallas kernels, prepare(): pl.pallas_call(functools.partial(pre_kernel, heads, experts), out_shape=(...  3.57 us
  transfers between devices with their start and end apart: 33, of which 18 were waited for; matrix products, arithmetic and copies ran while one was open for 2% of the time, Pallas kernels for 8%

profile of v1, /device:TPU:0, one launch (start us, length us, event | category | flops | bytes accessed | tf_op | source)
XLA Modules:
  0.0 139.7 jit_solution(11039445760204172838)
XLA Ops:
  2.2 1.9 %copy-done.3 = bf16[768,2048]{1,0:T(8,128)(2,1)S(1)} copy-done((bf16[768,2048]{1,0:T(8,128)(2,1)S(1)}, bf16[768,2048]{1,0:T(8,128)(2,1)}, u32[]{:S(2)}) %copy-start.3) | copy-done | bytes 3145752
  8.3 3.6 %prepare.1 = (bf16[32,896]{1,0:T(8,128)(2,1)S(1)}, f32[32,288]{1,0:T(8,128)S(1)}, f32[32,256]{1,0:T(8,128)S(1)}, f32[32,32]{1,0:T(8,128)S(1)}) custom-call(s32[1]{0:T(128)} %bitcast.place_ref.index_ref, s32[16]{0:T(128)S(1)} %copy-done.25, bf16[32,2048]{1,0:T(8,128)(2,1)S(1)} %copy-done.18, f32[1,2048]{1,0:T(1,128)S(1)} %bitcast.46, s32[1,32]{1,0:T(1,128)S(1)} %copy-done.24, ...), custom_call_target="tpu_custom_call" | custom-call | flops 144179200 | bytes 4505600 | tf_op jit(solution)/shard_map/prepare/pallas_call | solution.py:150
  11.9 5.1 %collective-permute-start.3 = (bf16[32,896]{1,0:T(8,128)(2,1)S(1)}, bf16[32,896]{1,0:T(8,128)(2,1)S(1)}, u32[]{:S(2)}, u32[]{:S(2)}) collective-permute-start(bf16[32,896]{1,0:T(8,128)(2,1)S(1)} %get-tuple-element.20.query_ref), channel_id=1, source_target_pairs={{0,12},{1,13},{2,14},{3,15},{4,8},{5,9},{6,10},{7,11},{8,4},{9,5},... | collective-permute-start | bytes 172040 | tf_op jit(solution)/shard_map/ppermute | solution.py:54
  19.7 2.3 %collective-permute-done.2 = bf16[32,896]{1,0:T(8,128)(2,1)S(1)} collective-permute-done((bf16[32,896]{1,0:T(8,128)(2,1)S(1)}, bf16[32,896]{1,0:T(8,128)(2,1)S(1)}, u32[]{:S(2)}, u32[]{:S(2)}) %collective-permute-start.2) | collective-permute-done | bytes 57376 | tf_op jit(solution)/shard_map/ppermute | solution.py:54
  24.5 4.3 %collective-permute-done.4.refs_1_.mix_low = bf16[4,32,896]{2,1,0:T(8,128)(2,1)S(1)} collective-permute-done((bf16[4,32,896]{2,1,0:T(8,128)(2,1)S(1)}, bf16[4,32,896]{2,1,0:T(8,128)(2,1)S(1)}, u32[]{:S(2)}, u32[]{:S(2)}) %collective-permute-start.4) | collective-permute-done | bytes 229408 | tf_op jit(solution)/shard_map/ppermute | solution.py:54
  35.1 4.2 %collective-permute-done.9 = bf16[4,144,128]{2,1,0:T(8,128)(2,1)S(1)} collective-permute-done((bf16[4,144,128]{2,1,0:T(8,128)(2,1)S(1)}, bf16[4,144,128]{2,1,0:T(8,128)(2,1)S(1)}, u32[]{:S(2)}, u32[]{:S(2)}) %collective-permute-start.9) | collective-permute-done | bytes 147488 | tf_op jit(solution)/shard_map/ppermute | solution.py:54
  39.4 2.2 %collective-permute-start.12 = (bf16[144,128]{1,0:T(8,128)(2,1)S(1)}, bf16[144,128]{1,0:T(8,128)(2,1)S(1)}, u32[]{:S(2)}, u32[]{:S(2)}) collective-permute-start(bf16[144,128]{1,0:T(8,128)(2,1)S(1)} %get-tuple-element.41), channel_id=1, source_target_pairs={{0,12},{1,13},{2,14},{3,15},{4,8},{5,9},{6,10},{7,11},{8,4},{9,5},... | collective-permute-start | bytes 110600 | tf_op jit(solution)/shard_map/ppermute | solution.py:54
  41.6 2.2 %collective-permute-start.10 = (bf16[144,128]{1,0:T(8,128)(2,1)S(1)}, bf16[144,128]{1,0:T(8,128)(2,1)S(1)}, u32[]{:S(2)}, u32[]{:S(2)}) collective-permute-start(bf16[144,128]{1,0:T(8,128)(2,1)S(1)} %get-tuple-element.43), channel_id=1, source_target_pairs={{0,4},{1,5},{2,6},{3,7},{4,0},{5,1},{6,2},{7,3},{8,12},{9,13},{10,... | collective-permute-start | bytes 110600 | tf_op jit(solution)/shard_map/ppermute | solution.py:54
  48.6 3.5 %collective-permute-done.13.other_ref = bf16[32,2048]{1,0:T(8,128)(2,1)S(1)} collective-permute-done((bf16[32,2048]{1,0:T(8,128)(2,1)S(1)}, bf16[32,2048]{1,0:T(8,128)(2,1)S(1)}, u32[]{:S(2)}, u32[]{:S(2)}) %collective-permute-start.13) | collective-permute-done | bytes 131104 | tf_op jit(solution)/shard_map/ppermute | solution.py:54
  52.9 2.1 %collective-permute-start.16 = (bf16[32,2048]{1,0:T(8,128)(2,1)S(1)}, bf16[32,2048]{1,0:T(8,128)(2,1)S(1)}, u32[]{:S(2)}, u32[]{:S(2)}) collective-permute-start(bf16[32,2048]{1,0:T(8,128)(2,1)S(1)} %get-tuple-element.29), channel_id=1, source_target_pairs={{0,12},{1,13},{2,14},{3,15},{4,8},{5,9},{6,10},{7,11},{8,4},{9,5},... | collective-permute-start | bytes 393224 | tf_op jit(solution)/shard_map/ppermute | solution.py:54
  57.3 2.7 %collective-permute-done.16 = bf16[32,2048]{1,0:T(8,128)(2,1)S(1)} collective-permute-done((bf16[32,2048]{1,0:T(8,128)(2,1)S(1)}, bf16[32,2048]{1,0:T(8,128)(2,1)S(1)}, u32[]{:S(2)}, u32[]{:S(2)}) %collective-permute-start.16) | collective-permute-done | bytes 131104 | tf_op jit(solution)/shard_map/ppermute | solution.py:54
  60.0 4.6 %collective-permute-done.15 = bf16[32,2048]{1,0:T(8,128)(2,1)S(1)} collective-permute-done((bf16[32,2048]{1,0:T(8,128)(2,1)S(1)}, bf16[32,2048]{1,0:T(8,128)(2,1)S(1)}, u32[]{:S(2)}, u32[]{:S(2)}) %collective-permute-start.15) | collective-permute-done | bytes 131104 | tf_op jit(solution)/shard_map/ppermute | solution.py:54
  66.8 11.0 %collective-permute-done.19.low_ref = bf16[4,32,2048]{2,1,0:T(8,128)(2,1)} collective-permute-done((bf16[4,32,2048]{2,1,0:T(8,128)(2,1)S(1)}, bf16[4,32,2048]{2,1,0:T(8,128)(2,1)}, u32[]{:S(2)}, u32[]{:S(2)}) %collective-permute-start.19) | collective-permute-done | bytes 524320 | tf_op jit(solution)/shard_map/ppermute | solution.py:54
  79.4 2.8 %collective-permute-start.27 = (bf16[8,640]{1,0:T(8,128)(2,1)S(1)}, bf16[8,640]{1,0:T(8,128)(2,1)S(1)}, u32[]{:S(2)}, u32[]{:S(2)}) collective-permute-start(bf16[8,640]{1,0:T(8,128)(2,1)S(1)} %get-tuple-element.35), channel_id=1, source_target_pairs={{0,4},{1,5},{2,6},{3,7},{4,0},{5,1},{6,2},{7,3},{8,12},{9,13},{10,... | collective-permute-start | bytes 30728 | tf_op jit(solution)/shard_map/ppermute | solution.py:54
  86.0 1.8 %copy-done.1 = bf16[1,704,2048]{2,1,0:T(8,128)(2,1)S(1)} copy-done((bf16[1,704,2048]{2,1,0:T(8,128)(2,1)S(1)}, bf16[1,704,2048]{2,1,0:T(8,128)(2,1)}, u32[]{:S(2)}) %copy-start.1) | copy-done | bytes 2883608
  87.8 1.8 %copy-done.2 = bf16[1,704,2048]{2,1,0:T(8,128)(2,1)S(1)} copy-done((bf16[1,704,2048]{2,1,0:T(8,128)(2,1)S(1)}, bf16[1,704,2048]{2,1,0:T(8,128)(2,1)}, u32[]{:S(2)}) %copy-start.2) | copy-done | bytes 2883608
  91.5 5.4 %expert.3 = (bf16[4,32,2048]{2,1,0:T(8,128)(2,1)S(1)}, bf16[4,32,2048]{2,1,0:T(8,128)(2,1)S(1)}) custom-call(s32[1]{0:T(128)} %bitcast.place_ref.index_ref, bf16[4,32,2048]{2,1,0:T(8,128)(2,1)} %collective-permute-done.19.low_ref, bf16[4,32,2048]{2,1,0:T(8,128)(2,1)S(1)} %collective-permute-done.20.high_ref, bf16[4,32,896]{2,1,0:T(8,128)(2,1)S(1)} %copy-done.14, ...), custom_call_target="tpu_custom_call" | custom-call | flops 2214592512 | bytes 8650752 | tf_op jit(solution)/shard_map/expert/pallas_call | solution.py:380
  97.5 5.1 %expert.2 = (bf16[4,32,2048]{2,1,0:T(8,128)(2,1)S(1)}, bf16[4,32,2048]{2,1,0:T(8,128)(2,1)}) custom-call(s32[1]{0:T(128)} %bitcast.place_ref.index_ref, bf16[4,32,2048]{2,1,0:T(8,128)(2,1)S(1)} %pad_maximum_fusion.low_ref, bf16[4,32,2048]{2,1,0:T(8,128)(2,1)S(1)} %collective-permute-done.17.high_ref, bf16[4,32,896]{2,1,0:T(8,128)(2,1)S(1)} %copy-done.9, ...), custom_call_target="tpu_custom_call" | custom-call | flops 2214592512 | bytes 8650752 | tf_op jit(solution)/shard_map/expert/pallas_call | solution.py:380
  104.9 12.8 %collective-permute-done.22 = bf16[4,32,2048]{2,1,0:T(8,128)(2,1)S(1)} collective-permute-done((bf16[4,32,2048]{2,1,0:T(8,128)(2,1)S(1)}, bf16[4,32,2048]{2,1,0:T(8,128)(2,1)S(1)}, u32[]{:S(2)}, u32[]{:S(2)}) %collective-permute-start.22) | collective-permute-done | bytes 524320 | tf_op jit(solution)/shard_map/ppermute | solution.py:54
  118.9 2.0 %collective-permute-start.23 = (bf16[32,2048]{1,0:T(8,128)(2,1)S(1)}, bf16[32,2048]{1,0:T(8,128)(2,1)S(1)}, u32[]{:S(2)}, u32[]{:S(2)}) collective-permute-start(bf16[32,2048]{1,0:T(8,128)(2,1)S(1)} %get-tuple-element.36), channel_id=1, source_target_pairs={{0,4},{1,5},{2,6},{3,7},{4,0},{5,1},{6,2},{7,3},{8,12},{9,13},{10,... | collective-permute-start | bytes 393224 | tf_op jit(solution)/shard_map/ppermute | solution.py:54
  122.5 2.4 %collective-permute-done.23 = bf16[32,2048]{1,0:T(8,128)(2,1)S(1)} collective-permute-done((bf16[32,2048]{1,0:T(8,128)(2,1)S(1)}, bf16[32,2048]{1,0:T(8,128)(2,1)S(1)}, u32[]{:S(2)}, u32[]{:S(2)}) %collective-permute-start.23) | collective-permute-done | bytes 131104 | tf_op jit(solution)/shard_map/ppermute | solution.py:54
  124.9 4.3 %collective-permute-done.25 = bf16[32,2048]{1,0:T(8,128)(2,1)S(1)} collective-permute-done((bf16[32,2048]{1,0:T(8,128)(2,1)S(1)}, bf16[32,2048]{1,0:T(8,128)(2,1)S(1)}, u32[]{:S(2)}, u32[]{:S(2)}) %collective-permute-start.25) | collective-permute-done | bytes 131104 | tf_op jit(solution)/shard_map/ppermute | solution.py:54
  129.2 4.7 %collective-permute-done.24 = bf16[32,2048]{1,0:T(8,128)(2,1)S(1)} collective-permute-done((bf16[32,2048]{1,0:T(8,128)(2,1)S(1)}, bf16[32,2048]{1,0:T(8,128)(2,1)S(1)}, u32[]{:S(2)}, u32[]{:S(2)}) %collective-permute-start.24) | collective-permute-done | bytes 131104 | tf_op jit(solution)/shard_map/ppermute | solution.py:54
  136.3 2.7 %collective-permute-done.26 = bf16[32,2048]{1,0:T(8,128)(2,1)S(1)} collective-permute-done((bf16[32,2048]{1,0:T(8,128)(2,1)S(1)}, bf16[32,2048]{1,0:T(8,128)(2,1)S(1)}, u32[]{:S(2)}, u32[]{:S(2)}) %collective-permute-start.26) | collective-permute-done | bytes 131104 | tf_op jit(solution)/shard_map/ppermute | solution.py:54
  (161 shorter events, 43.2 us)
Async XLA Ops:
  11.9 7.9 %collective-permute-start.3 = (bf16[32,896]{1,0:T(8,128)(2,1)S(1)}, bf16[32,896]{1,0:T(8,128)(2,1)S(1)}, u32[]{:S(2)}, u32[]{:S(2)}) collective-permute-start(bf16[32,896]{1,0:T(8,128)(2,1)S(1)} %get-tuple-element.20.query_ref), channel_id=1, source_target_pairs={{0,12},{1,13},{2,14},{3,15},{4,8},{5,9},{6,10},{7,11},{8,4},{9,5},... | collective-permute-start | bytes 172040 | tf_op jit(solution)/shard_map/ppermute | solution.py:54
  17.0 5.1 %collective-permute-start.2 = (bf16[32,896]{1,0:T(8,128)(2,1)S(1)}, bf16[32,896]{1,0:T(8,128)(2,1)S(1)}, u32[]{:S(2)}, u32[]{:S(2)}) collective-permute-start(bf16[32,896]{1,0:T(8,128)(2,1)S(1)} %get-tuple-element.20.query_ref), channel_id=1, source_target_pairs={{0,8},{1,9},{2,10},{3,11},{4,12},{5,13},{6,14},{7,15},{8,0},{9,1},... | collective-permute-start | bytes 172040 | tf_op jit(solution)/shard_map/ppermute | solution.py:54
  17.0 5.1 %collective-permute-start.1 = (bf16[32,896]{1,0:T(8,128)(2,1)S(1)}, bf16[32,896]{1,0:T(8,128)(2,1)S(1)}, u32[]{:S(2)}, u32[]{:S(2)}) collective-permute-start(bf16[32,896]{1,0:T(8,128)(2,1)S(1)} %get-tuple-element.20.query_ref), channel_id=1, source_target_pairs={{0,4},{1,5},{2,6},{3,7},{4,0},{5,1},{6,2},{7,3},{8,12},{9,13},{10,... | collective-permute-start | bytes 172040 | tf_op jit(solution)/shard_map/ppermute | solution.py:54
  17.6 11.2 %collective-permute-start = (f32[32,288]{1,0:T(8,128)S(1)}, f32[32,288]{1,0:T(8,128)S(1)}, u32[]{:S(2)}, u32[]{:S(2)}) collective-permute-start(f32[32,288]{1,0:T(8,128)S(1)} %get-tuple-element.18), channel_id=1, source_target_pairs={{0,16},{16,0},{1,17},{17,1},{2,18},{18,2},{3,19},{19,3},{4,20},{20... | collective-permute-start | bytes 110600 | tf_op jit(solution)/shard_map/ppermute | solution.py:54
  22.1 6.7 %collective-permute-start.4 = (bf16[4,32,896]{2,1,0:T(8,128)(2,1)S(1)}, bf16[4,32,896]{2,1,0:T(8,128)(2,1)S(1)}, u32[]{:S(2)}, u32[]{:S(2)}) collective-permute-start(bf16[4,32,896]{2,1,0:T(8,128)(2,1)S(1)} %pad_maximum_fusion.1.refs_0_.mix_low), channel_id=1, source_target_pairs={{0,2},{1,3},{2,0},{3,1},{4,6},{5,7},{6,4},{7,5},{8,10},{9,11},{10,... | collective-permute-start | bytes 688136 | tf_op jit(solution)/shard_map/ppermute | solution.py:54
  33.3 6.0 %collective-permute-start.9 = (bf16[4,144,128]{2,1,0:T(8,128)(2,1)S(1)}, bf16[4,144,128]{2,1,0:T(8,128)(2,1)S(1)}, u32[]{:S(2)}, u32[]{:S(2)}) collective-permute-start(bf16[4,144,128]{2,1,0:T(8,128)(2,1)S(1)} %add_convert_fusion.4), channel_id=1, source_target_pairs={{0,2},{1,3},{2,0},{3,1},{4,6},{5,7},{6,4},{7,5},{8,10},{9,11},{10,... | collective-permute-start | bytes 442376 | tf_op jit(solution)/shard_map/ppermute | solution.py:54
  39.4 5.8 %collective-permute-start.12 = (bf16[144,128]{1,0:T(8,128)(2,1)S(1)}, bf16[144,128]{1,0:T(8,128)(2,1)S(1)}, u32[]{:S(2)}, u32[]{:S(2)}) collective-permute-start(bf16[144,128]{1,0:T(8,128)(2,1)S(1)} %get-tuple-element.41), channel_id=1, source_target_pairs={{0,12},{1,13},{2,14},{3,15},{4,8},{5,9},{6,10},{7,11},{8,4},{9,5},... | collective-permute-start | bytes 110600 | tf_op jit(solution)/shard_map/ppermute | solution.py:54
  47.1 5.0 %collective-permute-start.13 = (bf16[32,2048]{1,0:T(8,128)(2,1)S(1)}, bf16[32,2048]{1,0:T(8,128)(2,1)S(1)}, u32[]{:S(2)}, u32[]{:S(2)}) collective-permute-start(bf16[32,2048]{1,0:T(8,128)(2,1)S(1)} %project_out.1.mine_ref), channel_id=1, source_target_pairs={{0,16},{16,0},{1,17},{17,1},{2,18},{18,2},{3,19},{19,3},{4,20},{20... | collective-permute-start | bytes 393224 | tf_op jit(solution)/shard_map/ppermute | solution.py:54
  52.9 7.1 %collective-permute-start.16 = (bf16[32,2048]{1,0:T(8,128)(2,1)S(1)}, bf16[32,2048]{1,0:T(8,128)(2,1)S(1)}, u32[]{:S(2)}, u32[]{:S(2)}) collective-permute-start(bf16[32,2048]{1,0:T(8,128)(2,1)S(1)} %get-tuple-element.29), channel_id=1, source_target_pairs={{0,12},{1,13},{2,14},{3,15},{4,8},{5,9},{6,10},{7,11},{8,4},{9,5},... | collective-permute-start | bytes 393224 | tf_op jit(solution)/shard_map/ppermute | solution.py:54
  55.0 9.7 %collective-permute-start.15 = (bf16[32,2048]{1,0:T(8,128)(2,1)S(1)}, bf16[32,2048]{1,0:T(8,128)(2,1)S(1)}, u32[]{:S(2)}, u32[]{:S(2)}) collective-permute-start(bf16[32,2048]{1,0:T(8,128)(2,1)S(1)} %get-tuple-element.29), channel_id=1, source_target_pairs={{0,8},{1,9},{2,10},{3,11},{4,12},{5,13},{6,14},{7,15},{8,0},{9,1},... | collective-permute-start | bytes 393224 | tf_op jit(solution)/shard_map/ppermute | solution.py:54
  55.7 8.9 %collective-permute-start.14 = (bf16[32,2048]{1,0:T(8,128)(2,1)S(1)}, bf16[32,2048]{1,0:T(8,128)(2,1)S(1)}, u32[]{:S(2)}, u32[]{:S(2)}) collective-permute-start(bf16[32,2048]{1,0:T(8,128)(2,1)S(1)} %get-tuple-element.29), channel_id=1, source_target_pairs={{0,4},{1,5},{2,6},{3,7},{4,0},{5,1},{6,2},{7,3},{8,12},{9,13},{10,... | collective-permute-start | bytes 393224 | tf_op jit(solution)/shard_map/ppermute | solution.py:54
  64.7 13.0 %collective-permute-start.19 = (bf16[4,32,2048]{2,1,0:T(8,128)(2,1)S(1)}, bf16[4,32,2048]{2,1,0:T(8,128)(2,1)}, u32[]{:S(2)}, u32[]{:S(2)}) collective-permute-start(bf16[4,32,2048]{2,1,0:T(8,128)(2,1)S(1)} %pad_maximum_fusion.low_ref), channel_id=1, source_target_pairs={{0,2},{1,3},{2,0},{3,1},{4,6},{5,7},{6,4},{7,5},{8,10},{9,11},{10,... | collective-permute-start | bytes 1572872 | tf_op jit(solution)/shard_map/ppermute | solution.py:54
  77.8 8.2 %collective-permute-start.20 = (bf16[4,32,2048]{2,1,0:T(8,128)(2,1)}, bf16[4,32,2048]{2,1,0:T(8,128)(2,1)S(1)}, u32[]{:S(2)}, u32[]{:S(2)}) collective-permute-start(bf16[4,32,2048]{2,1,0:T(8,128)(2,1)} %collective-permute-done.19.low_ref), channel_id=1, source_target_pairs={{0,1},{1,0},{2,3},{3,2},{4,5},{5,4},{6,7},{7,6},{8,9},{9,8},{10,11... | collective-permute-start | bytes 1572872 | tf_op jit(solution)/shard_map/ppermute | solution.py:54
  77.8 5.5 %collective-permute-start.29 = (bf16[8,640]{1,0:T(8,128)(2,1)S(1)}, bf16[8,640]{1,0:T(8,128)(2,1)S(1)}, u32[]{:S(2)}, u32[]{:S(2)}) collective-permute-start(bf16[8,640]{1,0:T(8,128)(2,1)S(1)} %get-tuple-element.35), channel_id=1, source_target_pairs={{0,12},{1,13},{2,14},{3,15},{4,8},{5,9},{6,10},{7,11},{8,4},{9,5},... | collective-permute-start | bytes 30728 | tf_op jit(solution)/shard_map/ppermute | solution.py:54
  84.0 19.9 %collective-permute-start.31 = (bf16[4,8,640]{2,1,0:T(8,128)(2,1)S(1)}, bf16[4,8,640]{2,1,0:T(8,128)(2,1)S(1)}, u32[]{:S(2)}, u32[]{:S(2)}) collective-permute-start(bf16[4,8,640]{2,1,0:T(8,128)(2,1)S(1)} %pad_maximum_fusion.4), channel_id=1, source_target_pairs={{0,1},{1,0},{2,3},{3,2},{4,5},{5,4},{6,7},{7,6},{8,9},{9,8},{10,11... | collective-permute-start | bytes 122888 | tf_op jit(solution)/shard_map/ppermute | solution.py:54
  84.1 13.2 %collective-permute-start.30 = (bf16[4,8,640]{2,1,0:T(8,128)(2,1)S(1)}, bf16[4,8,640]{2,1,0:T(8,128)(2,1)S(1)}, u32[]{:S(2)}, u32[]{:S(2)}) collective-permute-start(bf16[4,8,640]{2,1,0:T(8,128)(2,1)S(1)} %pad_maximum_fusion.4), channel_id=1, source_target_pairs={{0,2},{1,3},{2,0},{3,1},{4,6},{5,7},{6,4},{7,5},{8,10},{9,11},{10,... | collective-permute-start | bytes 122888 | tf_op jit(solution)/shard_map/ppermute | solution.py:54
  85.8 11.7 %collective-permute-start.17 = (bf16[4,32,2048]{2,1,0:T(8,128)(2,1)S(1)}, bf16[4,32,2048]{2,1,0:T(8,128)(2,1)S(1)}, u32[]{:S(2)}, u32[]{:S(2)}) collective-permute-start(bf16[4,32,2048]{2,1,0:T(8,128)(2,1)S(1)} %pad_maximum_fusion.low_ref), channel_id=1, source_target_pairs={{0,1},{1,0},{2,3},{3,2},{4,5},{5,4},{6,7},{7,6},{8,9},{9,8},{10,11... | collective-permute-start | bytes 1572872 | tf_op jit(solution)/shard_map/ppermute | solution.py:54
  96.9 6.2 %collective-permute-start.21 = (bf16[4,32,2048]{2,1,0:T(8,128)(2,1)S(1)}, bf16[4,32,2048]{2,1,0:T(8,128)(2,1)S(1)}, u32[]{:S(2)}, u32[]{:S(2)}) collective-permute-start(bf16[4,32,2048]{2,1,0:T(8,128)(2,1)S(1)} %get-tuple-element.33), channel_id=1, source_target_pairs={{0,1},{1,0},{2,3},{3,2},{4,5},{5,4},{6,7},{7,6},{8,9},{9,8},{10,11... | collective-permute-start | bytes 1572872 | tf_op jit(solution)/shard_map/ppermute | solution.py:54
  97.3 6.6 %collective-permute-start.32 = (bf16[4,8,640]{2,1,0:T(8,128)(2,1)S(1)}, bf16[4,8,640]{2,1,0:T(8,128)(2,1)S(1)}, u32[]{:S(2)}, u32[]{:S(2)}) collective-permute-start(bf16[4,8,640]{2,1,0:T(8,128)(2,1)S(1)} %collective-permute-done.30), channel_id=1, source_target_pairs={{0,1},{1,0},{2,3},{3,2},{4,5},{5,4},{6,7},{7,6},{8,9},{9,8},{10,11... | collective-permute-start | bytes 122888 | tf_op jit(solution)/shard_map/ppermute | solution.py:54
  103.5 14.2 %collective-permute-start.22 = (bf16[4,32,2048]{2,1,0:T(8,128)(2,1)S(1)}, bf16[4,32,2048]{2,1,0:T(8,128)(2,1)S(1)}, u32[]{:S(2)}, u32[]{:S(2)}) collective-permute-start(bf16[4,32,2048]{2,1,0:T(8,128)(2,1)S(1)} %add_convert_fusion.1), channel_id=1, source_target_pairs={{0,2},{1,3},{2,0},{3,1},{4,6},{5,7},{6,4},{7,5},{8,10},{9,11},{10,... | collective-permute-start | bytes 1572872 | tf_op jit(solution)/shard_map/ppermute | solution.py:54
  118.9 5.9 %collective-permute-start.23 = (bf16[32,2048]{1,0:T(8,128)(2,1)S(1)}, bf16[32,2048]{1,0:T(8,128)(2,1)S(1)}, u32[]{:S(2)}, u32[]{:S(2)}) collective-permute-start(bf16[32,2048]{1,0:T(8,128)(2,1)S(1)} %get-tuple-element.36), channel_id=1, source_target_pairs={{0,4},{1,5},{2,6},{3,7},{4,0},{5,1},{6,2},{7,3},{8,12},{9,13},{10,... | collective-permute-start | bytes 393224 | tf_op jit(solution)/shard_map/ppermute | solution.py:54
  120.9 8.2 %collective-permute-start.25 = (bf16[32,2048]{1,0:T(8,128)(2,1)S(1)}, bf16[32,2048]{1,0:T(8,128)(2,1)S(1)}, u32[]{:S(2)}, u32[]{:S(2)}) collective-permute-start(bf16[32,2048]{1,0:T(8,128)(2,1)S(1)} %get-tuple-element.37), channel_id=1, source_target_pairs={{0,12},{1,13},{2,14},{3,15},{4,8},{5,9},{6,10},{7,11},{8,4},{9,5},... | collective-permute-start | bytes 393224 | tf_op jit(solution)/shard_map/ppermute | solution.py:54
  122.4 11.5 %collective-permute-start.24 = (bf16[32,2048]{1,0:T(8,128)(2,1)S(1)}, bf16[32,2048]{1,0:T(8,128)(2,1)S(1)}, u32[]{:S(2)}, u32[]{:S(2)}) collective-permute-start(bf16[32,2048]{1,0:T(8,128)(2,1)S(1)} %get-tuple-element.38), channel_id=1, source_target_pairs={{0,8},{1,9},{2,10},{3,11},{4,12},{5,13},{6,14},{7,15},{8,0},{9,1},... | collective-permute-start | bytes 393224 | tf_op jit(solution)/shard_map/ppermute | solution.py:54
  133.9 5.0 %collective-permute-start.26 = (bf16[32,2048]{1,0:T(8,128)(2,1)S(1)}, bf16[32,2048]{1,0:T(8,128)(2,1)S(1)}, u32[]{:S(2)}, u32[]{:S(2)}) collective-permute-start(bf16[32,2048]{1,0:T(8,128)(2,1)S(1)} %fusion.2), channel_id=1, source_target_pairs={{0,16},{16,0},{1,17},{17,1},{2,18},{18,2},{3,19},{19,3},{4,20},{20... | collective-permute-start | bytes 393224 | tf_op jit(solution)/shard_map/ppermute | solution.py:54
  (44 other events, 498.3 us)

commit v2 on v1

--- a/solution.py
+++ b/solution.py
@@ -66,9 +66,11 @@
     return (left.astype(f32) + right.astype(f32)).astype(bf16)
 
 
-def scatter_blocks(pieces, count):
+def scatter_blocks(pieces, count, done=0):
     (radix, stride0), *rest = phases(count)
     for _, stride in reversed(rest):
+        if stride == done:
+            continue
         half = len(pieces) // 2
         got = [swap(p, "blk", stride) for p in pieces[half:]]
         pieces = [add16(p, g) for p, g in zip(pieces[:half], got)]
@@ -113,12 +115,14 @@
     trig_ref[:, :LANES] = cosine
     trig_ref[:, LANES:] = sine
     sigma = jax.nn.sigmoid(logits_ref[...])
-    weight = ROUTE_SCALE * sigma / jnp.sum(sigma, axis=-1, keepdims=True)
-    mix = jnp.zeros((tok, LANES), f32)
-    for k in range(weight.shape[1]):
-        mix = mix + jnp.where(lane % experts == routes_ref[:, k : k + 1], weight[:, k : k + 1], 0.0)
+    weight = ROUTE_SCALE * sigma / jnp.sum(sigma, axis=0, keepdims=True)
+    named = lax.broadcasted_iota(jnp.int32, (LANES, 1), 0)
+    mix = jnp.zeros((LANES, tok), f32)
+    for k in range(weight.shape[0]):
+        mix = mix + jnp.where(named % experts == routes_ref[k : k + 1], weight[k : k + 1], 0.0)
     high = mix.astype(bf16).astype(f32)
-    mix = jnp.where(lane < experts, high, jnp.where(lane < 2 * experts, mix - high, 0.0))
+    mix = jnp.where(named < experts, high, jnp.where(named < 2 * experts, mix - high, 0.0))
+    mix = nt(eye.astype(bf16), mix.astype(bf16))
     hidden = hidden_ref[...].astype(f32)
     mean_square = jnp.mean(hidden * hidden, axis=-1, keepdims=True)
     normed = (hidden * lax.rsqrt(mean_square + EPSILON) * gain_ref[...]).astype(bf16)
@@ -144,28 +148,33 @@
 def prepare(place, lengths, hidden, gain, parents, routes, logits, w_query, w_latent, heads, experts):
     tok, width = hidden.shape
     smem = pl.BlockSpec(memory_space=pltpu.SMEM)
-    vmem = pl.BlockSpec(memory_space=pltpu.VMEM)
-    anyw = pl.BlockSpec(memory_space=pl.ANY)
+    hbm = pl.BlockSpec(memory_space=pltpu.HBM)
     lanes = heads * NOPE + 3 * LANES
+    small = (hidden, gain[None], parents, routes.T, logits.T)
+    whole = lambda shape: pl.BlockSpec(shape, lambda i: (0,) * len(shape))
     return pl.pallas_call(
         functools.partial(pre_kernel, heads, experts),
+        grid=(1,),
         out_shape=(
             jax.ShapeDtypeStruct((tok, lanes), bf16),
             jax.ShapeDtypeStruct((tok, w_latent.shape[0]), f32),
             jax.ShapeDtypeStruct((tok, 2 * LANES), f32),
             jax.ShapeDtypeStruct((tok, tok), f32),
         ),
-        in_specs=[smem, smem, vmem, vmem, vmem, vmem, vmem, anyw, anyw],
-        out_specs=(vmem,) * 4,
+        in_specs=[smem, smem, *(whole(v.shape) for v in small), hbm, hbm],
+        out_specs=tuple(
+            whole(shape)
+            for shape in ((tok, lanes), (tok, w_latent.shape[0]), (tok, 2 * LANES), (tok, tok))
+        ),
         scratch_shapes=[
             pltpu.VMEM(w_query.shape, bf16),
             pltpu.VMEM(w_latent.shape, bf16),
             pltpu.SemaphoreType.DMA((2,)),
         ],
-        compiler_params=params(24),
+        compiler_params=params(56),
         cost_estimate=cost(2 * tok * width * 1100, 2 * width * 1100),
         name="prepare",
-    )(place, lengths, hidden, gain[None], parents, routes, logits, w_query, w_latent)
+    )(place, lengths, *small, w_query, w_latent)
 
 
 def spread(heads):
@@ -230,9 +239,16 @@
     return jnp.concatenate([numer, denom], axis=0)
 
 
-def slots_kernel(heads, slots, block, pieces, place_ref, live_ref, keys_ref, values_ref, *refs):
-    queries, outs = refs[:pieces], refs[pieces:]
-    each = queries[0].shape[0]
+def slots_kernel(
+    heads, slots, block, pieces, experts, place_ref, live_ref, index_ref, keys_ref, values_ref, *refs
+):
+    queries, outs, mixes = refs[:pieces], refs[pieces : 2 * pieces], refs[2 * pieces :]
+    each, tok, lanes = queries[0].shape
+    named = lax.broadcasted_iota(jnp.int32, (1, LANES), 1)
+    mine = (named == index_ref[0]) | (named == index_ref[0] + experts)
+    for query, mix in zip(queries, mixes):
+        shares = query[:, :, lanes - LANES :].reshape(each * tok, LANES).astype(f32)
+        mix[...] = jnp.sum(jnp.where(mine, shares, 0.0), axis=-1, keepdims=True)
     for out in outs:
         out[...] = jnp.zeros(out.shape, out.dtype)
     parts = []
@@ -256,20 +272,23 @@
                 out[place % each] = total.astype(bf16)
 
 
-def attend_slots(place, live, keys, values, queries, heads, block):
+def attend_slots(place, live, index, keys, values, queries, heads, block, experts):
     smem = pl.BlockSpec(memory_space=pltpu.SMEM)
     vmem = pl.BlockSpec(memory_space=pltpu.VMEM)
     slots, each, tok = place.shape[0], queries[0].shape[0], queries[0].shape[1]
+    pieces = len(queries)
     out = jax.ShapeDtypeStruct((each, heads * tok + 16, LANES), bf16)
-    return pl.pallas_call(
-        functools.partial(slots_kernel, heads, slots, block, len(queries)),
-        out_shape=(out,) * len(queries),
-        in_specs=[smem, smem, vmem, vmem] + [vmem] * len(queries),
-        out_specs=(vmem,) * len(queries),
+    mix = jax.ShapeDtypeStruct((each * tok, 1), f32)
+    results = pl.pallas_call(
+        functools.partial(slots_kernel, heads, slots, block, pieces, experts),
+        out_shape=(out,) * pieces + (mix,) * pieces,
+        in_specs=[smem, smem, smem, vmem, vmem] + [vmem] * pieces,
+        out_specs=(vmem,) * (2 * pieces),
         compiler_params=params(24),
         cost_estimate=cost(1 << 28, 2 << 20),
         name="attend_slots",
-    )(place, live, keys, values, *queries)
+    )(place, live, index, keys, values, *queries)
+    return list(results[:pieces]), results[pieces:]
 
 
 def own_kernel(heads, rows_ref, query_ref, reach_ref, key_ref, value_ref, out_ref):
@@ -337,8 +356,8 @@
 
 
 def expert_kernel(
-    experts, index_ref, low_ref, high_ref, mix_low, mix_high, gate_hbm, up_hbm, down_hbm,
-    out_low, out_high, gate, up, down, sems,
+    low_ref, high_ref, mix_low, mix_high, gate_hbm, up_hbm, down_hbm, out_low, out_high,
+    gate, up, down, sems,
 ):
     copies = [
         pltpu.make_async_copy(src.at[0], dst, sems.at[i])
@@ -350,13 +369,7 @@
     rows = jnp.concatenate(
         [r[...].reshape(each * tok, width) for r in (low_ref, high_ref)], axis=0
     )
-    mix = jnp.concatenate(
-        [r[...].reshape(each * tok, LANES) for r in (mix_low, mix_high)], axis=0
-    ).astype(f32)
-    lane = lax.broadcasted_iota(jnp.int32, (1, LANES), 1)
-    index = index_ref[0]
-    mine = (lane == index) | (lane == index + experts)
-    weight = jnp.sum(jnp.where(mine, mix, 0.0), axis=-1, keepdims=True)
+    weight = jnp.concatenate([mix_low[...], mix_high[...]], axis=0)
     copies[0].wait()
     gated = nt(rows, gate[...])
     gated = gated / (1.0 + jnp.exp(-gated))
@@ -368,27 +381,22 @@
     out_high[...] = out[each * tok :].reshape(each, tok, width)
 
 
-def expert(index, low, high, mix_low, mix_high, w_gate, w_up, w_down, experts):
-    smem = pl.BlockSpec(memory_space=pltpu.SMEM)
+def expert(low, high, mix_low, mix_high, w_gate, w_up, w_down):
     vmem = pl.BlockSpec(memory_space=pltpu.VMEM)
-    anyw = pl.BlockSpec(memory_space=pl.ANY)
+    hbm = pl.BlockSpec(memory_space=pltpu.HBM)
     each, tok, _ = low.shape
-    last = mix_low.shape[-1] // LANES - 1
-    mixed = pl.BlockSpec((each, tok, LANES), lambda i: (0, 0, last))
     out = jax.ShapeDtypeStruct(low.shape, bf16)
-    whole = pl.BlockSpec(low.shape, lambda i: (0, 0, 0))
     return pl.pallas_call(
-        functools.partial(expert_kernel, experts),
-        grid=(1,),
+        expert_kernel,
         out_shape=(out, out),
-        in_specs=[smem, whole, whole, mixed, mixed, anyw, anyw, anyw],
-        out_specs=(whole, whole),
+        in_specs=[vmem] * 4 + [hbm] * 3,
+        out_specs=(vmem, vmem),
         scratch_shapes=[pltpu.VMEM(w.shape[1:], bf16) for w in (w_gate, w_up, w_down)]
         + [pltpu.SemaphoreType.DMA((3,))],
-        compiler_params=params(40),
+        compiler_params=params(28),
         cost_estimate=cost(12 * each * tok * w_gate.size, 6 * w_gate.size),
         name="expert",
-    )(index, low, high, mix_low, mix_high, w_gate, w_up, w_down)
+    )(low, high, mix_low, mix_high, w_gate, w_up, w_down)
 
 
 def sum_heads(value):
@@ -445,8 +453,8 @@
     )
     live = jnp.where(slot_request >= 0, owner_length - slot_block * block, 0)
     place = place_of(owner ^ me, count)
-    partial = attend_slots(place, live, keys, values, queries, heads, block)
-    parts = scatter_blocks(list(partial), count)
+    partial, mixes = attend_slots(place, live, index, keys, values, queries, heads, block, experts)
+    parts = scatter_blocks(partial, count)
     own = attend_own(draft_rows, payload, reach, w_key_up, w_value_up, heads)
     mine, other = sum_heads(project_out(w_out, own, parts, heads, tok))
     resid, moe_in = norm(hidden_in, mine, other, moe_gain)
@@ -456,10 +464,37 @@
     chosen = jnp.dot(pick, draft_rows, preferred_element_type=f32).astype(bf16)
     target = new_slots.reshape(-1, 1)
     tail = jnp.concatenate([target // 256, target % 256], axis=1).astype(bf16)
-    sent = jnp.concatenate(
+    packed = jnp.concatenate(
         [chosen, tail, jnp.zeros((chosen.shape[0], LANES - ROPE - 2), bf16)], axis=1
     )
-    rows = jnp.concatenate(gather_blocks(sent, count)).reshape(-1, sent.shape[1])
+
+    (radix, stride), *rest = phases(count)
+    pieces = [moe_in] + [swap(moe_in, "blk", stride * j) for j in range(1, radix)]
+    packed, pieces[-1] = lax.optimization_barrier((packed, pieces[-1]))
+    tokens = [jnp.stack(pieces)]
+    rows = [jnp.stack([packed] + [swap(packed, "blk", stride * j) for j in range(1, radix)])]
+    for _, step in rest[:-1]:
+        tokens = tokens + [swap(t, "blk", step) for t in tokens]
+    half, near = len(tokens), rest[-1][1]
+    kept, got = [], []
+    for i in range(half):
+        if i:
+            tokens[i], kept[-1], sent, rows = lax.optimization_barrier(
+                (tokens[i], kept[-1], sent, rows)
+            )
+        far = swap(tokens[i], "blk", near)
+        keep, sent = expert(tokens[i], far, mixes[i], mixes[i + half], w_gate, w_up, w_down)
+        if not i:
+            rows[0], keep = lax.optimization_barrier((rows[0], keep))
+            for _, step in rest:
+                rows = rows + [swap(r, "blk", step) for r in rows]
+        kept.append(keep)
+        got.append(sent)
+    sums = [add16(k, swap(g, "blk", near)) for k, g in zip(kept, got)]
+    back = scatter_blocks(sums, count, near)
+
+    rows = jnp.concatenate(rows)
+    rows = rows.reshape(-1, packed.shape[1])
     at = RANK + ROPE
     slot = rows[:, at].astype(f32) * 256.0 + rows[:, at + 1].astype(f32)
     here = (me * NEW_DEV + jnp.arange(NEW_DEV, dtype=jnp.int32)).astype(f32)
@@ -467,14 +502,6 @@
         (here[:, None] == slot[None, :]).astype(bf16), rows[:, :at], preferred_element_type=f32
     ).astype(bf16)
 
-    tokens = gather_blocks(moe_in, count)
-    half = len(tokens) // 2
-    outs = [
-        expert(index, tokens[i], tokens[i + half], queries[i], queries[i + half],
-               w_gate, w_up, w_down, experts)
-        for i in range(half)
-    ]
-    back = scatter_blocks([o[0] for o in outs] + [o[1] for o in outs], count)
     total = back[0].astype(f32)
     for value in back[1:]:
         total = total + value.astype(f32)

time: 140 us -> 120 us (0.86)
  local copies, waits for them, and re-layouts: 15.5 us -> 0.8 us
  waiting for transfers between devices: 65.2 us -> 62.4 us
    unnamed x80 -> x41, local copies, waits for them, and re-layouts: 15.2 us -> 0.51 us
    ppermute x33, waiting for transfers between devices: 65.2 us -> 62.4 us  [swap(): return lax.ppermute(value, axis, [(i, i ^ bit) for i in range(count)])]
  transfers between devices with their start and end apart: 33 -> 33, of which waited for: 18 -> 21; matrix products, arithmetic and copies ran while one was open for 2% -> 3% of each run, Pallas kernels for 8% -> 5%
where the time goes in v2:
time: 120 us
  waiting for transfers between devices  62.4 us (52%)
  starting transfers between devices  34.9 us (29%)
  Pallas kernels  17.1 us (14%)
  other arithmetic  3 us (2%)
    ppermute x33, waiting for transfers between devices, swap(): return lax.ppermute(value, axis, [(i, i ^ bit) for i in range(count)])  62.4 us
    ppermute x33, starting transfers between devices, swap(): return lax.ppermute(value, axis, [(i, i ^ bit) for i in range(count)])  34.9 us
    pallas_call x2, Pallas kernels, expert(): pl.pallas_call(expert_kernel, out_shape=(out, out), in_specs=[vmem] * 4 +...  8.5 us
    pallas_call x1, Pallas kernels, prepare(): pl.pallas_call(functools.partial(pre_kernel, heads, experts), grid=(1,),...  5.24 us
  transfers between devices with their start and end apart: 33, of which 21 were waited for; matrix products, arithmetic and copies ran while one was open for 3% of the time, Pallas kernels for 5%

profile of v2, /device:TPU:0, one launch (start us, length us, event | category | flops | bytes accessed | tf_op | source)
XLA Modules:
  0.0 120.3 jit_solution(8207115044883349886)
XLA Ops:
  0.7 5.2 %prepare.1 = (bf16[32,896]{1,0:T(8,128)(2,1)}, f32[32,288]{1,0:T(8,128)}, f32[32,256]{1,0:T(8,128)}, f32[32,32]{1,0:T(8,128)}) custom-call(s32[1]{0:T(128)} %bitcast.place_ref.index_ref, s32[16]{0:T(128)} %len_ref.1, bf16[32,2048]{1,0:T(8,128)(2,1)} %hidden_ref.3, f32[1,2048]{1,0:T(1,128)} %bitcast.56, s32[1,32]{1,0:T(1,128)} %parents_ref.1, ...), custom_call_target="tpu_custom_call" | custom-call | flops 144179200 | bytes 4505600 | tf_op jit(solution)/shard_map/prepare/pallas_call | solution.py:155
  6.0 5.1 %collective-permute-start.3 = (bf16[32,896]{1,0:T(8,128)(2,1)}, bf16[32,896]{1,0:T(8,128)(2,1)S(1)}, u32[]{:S(2)}, u32[]{:S(2)}) collective-permute-start(bf16[32,896]{1,0:T(8,128)(2,1)} %get-tuple-element.34.query_ref), channel_id=1, source_target_pairs={{0,12},{1,13},{2,14},{3,15},{4,8},{5,9},{6,10},{7,11},{8,4},{9,5},... | collective-permute-start | bytes 172040 | tf_op jit(solution)/shard_map/ppermute | solution.py:54
  14.0 2.3 %collective-permute-done.2 = bf16[32,896]{1,0:T(8,128)(2,1)S(1)} collective-permute-done((bf16[32,896]{1,0:T(8,128)(2,1)}, bf16[32,896]{1,0:T(8,128)(2,1)S(1)}, u32[]{:S(2)}, u32[]{:S(2)}) %collective-permute-start.2) | collective-permute-done | bytes 57376 | tf_op jit(solution)/shard_map/ppermute | solution.py:54
  19.7 4.3 %collective-permute-done.4.refs_1_ = bf16[4,32,896]{2,1,0:T(8,128)(2,1)S(1)} collective-permute-done((bf16[4,32,896]{2,1,0:T(8,128)(2,1)S(1)}, bf16[4,32,896]{2,1,0:T(8,128)(2,1)S(1)}, u32[]{:S(2)}, u32[]{:S(2)}) %collective-permute-start.4) | collective-permute-done | bytes 229408 | tf_op jit(solution)/shard_map/ppermute | solution.py:54
  30.3 4.2 %collective-permute-done.9 = bf16[4,144,128]{2,1,0:T(8,128)(2,1)S(1)} collective-permute-done((bf16[4,144,128]{2,1,0:T(8,128)(2,1)S(1)}, bf16[4,144,128]{2,1,0:T(8,128)(2,1)S(1)}, u32[]{:S(2)}, u32[]{:S(2)}) %collective-permute-start.9) | collective-permute-done | bytes 147488 | tf_op jit(solution)/shard_map/ppermute | solution.py:54
  34.6 2.2 %collective-permute-start.12 = (bf16[144,128]{1,0:T(8,128)(2,1)S(1)}, bf16[144,128]{1,0:T(8,128)(2,1)S(1)}, u32[]{:S(2)}, u32[]{:S(2)}) collective-permute-start(bf16[144,128]{1,0:T(8,128)(2,1)S(1)} %get-tuple-element.67), channel_id=1, source_target_pairs={{0,12},{1,13},{2,14},{3,15},{4,8},{5,9},{6,10},{7,11},{8,4},{9,5},... | collective-permute-start | bytes 110600 | tf_op jit(solution)/shard_map/ppermute | solution.py:54
  36.8 2.2 %collective-permute-start.10 = (bf16[144,128]{1,0:T(8,128)(2,1)S(1)}, bf16[144,128]{1,0:T(8,128)(2,1)S(1)}, u32[]{:S(2)}, u32[]{:S(2)}) collective-permute-start(bf16[144,128]{1,0:T(8,128)(2,1)S(1)} %get-tuple-element.69), channel_id=1, source_target_pairs={{0,4},{1,5},{2,6},{3,7},{4,0},{5,1},{6,2},{7,3},{8,12},{9,13},{10,... | collective-permute-start | bytes 110600 | tf_op jit(solution)/shard_map/ppermute | solution.py:54
  43.9 3.3 %collective-permute-done.13.other_ref = bf16[32,2048]{1,0:T(8,128)(2,1)S(1)} collective-permute-done((bf16[32,2048]{1,0:T(8,128)(2,1)S(1)}, bf16[32,2048]{1,0:T(8,128)(2,1)S(1)}, u32[]{:S(2)}, u32[]{:S(2)}) %collective-permute-start.13) | collective-permute-done | bytes 131104 | tf_op jit(solution)/shard_map/ppermute | solution.py:54
  47.4 2.1 %collective-permute-start.16 = (bf16[32,2048]{1,0:T(8,128)(2,1)S(1)}, bf16[32,2048]{1,0:T(8,128)(2,1)S(1)}, u32[]{:S(2)}, u32[]{:S(2)}) collective-permute-start(bf16[32,2048]{1,0:T(8,128)(2,1)S(1)} %get-tuple-element.43), channel_id=1, source_target_pairs={{0,12},{1,13},{2,14},{3,15},{4,8},{5,9},{6,10},{7,11},{8,4},{9,5},... | collective-permute-start | bytes 393224 | tf_op jit(solution)/shard_map/ppermute | solution.py:54
  51.9 2.6 %collective-permute-done.16 = bf16[32,2048]{1,0:T(8,128)(2,1)S(1)} collective-permute-done((bf16[32,2048]{1,0:T(8,128)(2,1)S(1)}, bf16[32,2048]{1,0:T(8,128)(2,1)S(1)}, u32[]{:S(2)}, u32[]{:S(2)}) %collective-permute-start.16) | collective-permute-done | bytes 131104 | tf_op jit(solution)/shard_map/ppermute | solution.py:54
  54.6 4.6 %collective-permute-done.15 = bf16[32,2048]{1,0:T(8,128)(2,1)S(1)} collective-permute-done((bf16[32,2048]{1,0:T(8,128)(2,1)S(1)}, bf16[32,2048]{1,0:T(8,128)(2,1)S(1)}, u32[]{:S(2)}, u32[]{:S(2)}) %collective-permute-start.15) | collective-permute-done | bytes 131104 | tf_op jit(solution)/shard_map/ppermute | solution.py:54
  61.0 1.8 %collective-permute-start.20 = (bf16[8,640]{1,0:T(8,128)(2,1)S(1)}, bf16[8,640]{1,0:T(8,128)(2,1)S(1)}, u32[]{:S(2)}, u32[]{:S(2)}) collective-permute-start(bf16[8,640]{1,0:T(8,128)(2,1)S(1)} %maximum_maximum_fusion), channel_id=1, source_target_pairs={{0,12},{1,13},{2,14},{3,15},{4,8},{5,9},{6,10},{7,11},{8,4},{9,5},... | collective-permute-start | bytes 30728 | tf_op jit(solution)/shard_map/ppermute | solution.py:54
  62.8 2.6 %collective-permute-start.18 = (bf16[8,640]{1,0:T(8,128)(2,1)S(1)}, bf16[8,640]{1,0:T(8,128)(2,1)S(1)}, u32[]{:S(2)}, u32[]{:S(2)}) collective-permute-start(bf16[8,640]{1,0:T(8,128)(2,1)S(1)} %maximum_maximum_fusion), channel_id=1, source_target_pairs={{0,4},{1,5},{2,6},{3,7},{4,0},{5,1},{6,2},{7,3},{8,12},{9,13},{10,... | collective-permute-start | bytes 30728 | tf_op jit(solution)/shard_map/ppermute | solution.py:54
  67.4 4.3 %expert.2 = (bf16[4,32,2048]{2,1,0:T(8,128)(2,1)S(1)}, bf16[4,32,2048]{2,1,0:T(8,128)(2,1)S(1)}) custom-call(bf16[4,32,2048]{2,1,0:T(8,128)(2,1)S(1)} %pad_maximum_fusion.low_ref, bf16[4,32,2048]{2,1,0:T(8,128)(2,1)S(1)} %collective-permute-done.21.high_ref, f32[128,1]{1,0:T(8,128)S(1)} %get-tuple-element.46.mix_low, ...), custom_call_target="tpu_custom_call" | custom-call | flops 2214592512 | bytes 8650752 | tf_op jit(solution)/shard_map/expert/pallas_call | solution.py:389
  72.2 3.5 %collective-permute-done.22 = bf16[4,8,640]{2,1,0:T(8,128)(2,1)S(1)} collective-permute-done((bf16[4,8,640]{2,1,0:T(8,128)(2,1)S(1)}, bf16[4,8,640]{2,1,0:T(8,128)(2,1)S(1)}, u32[]{:S(2)}, u32[]{:S(2)}) %collective-permute-start.22) | collective-permute-done | bytes 40992 | tf_op jit(solution)/shard_map/ppermute | solution.py:54
  77.1 1.7 %collective-permute-done.26.high_ref = bf16[4,32,2048]{2,1,0:T(8,128)(2,1)S(1)} collective-permute-done((bf16[4,32,2048]{2,1,0:T(8,128)(2,1)S(1)}, bf16[4,32,2048]{2,1,0:T(8,128)(2,1)S(1)}, u32[]{:S(2)}, u32[]{:S(2)}) %collective-permute-start.26) | collective-permute-done | bytes 524320 | tf_op jit(solution)/shard_map/ppermute | solution.py:54
  78.9 4.2 %expert.3 = (bf16[4,32,2048]{2,1,0:T(8,128)(2,1)S(1)}, bf16[4,32,2048]{2,1,0:T(8,128)(2,1)S(1)}) custom-call(bf16[4,32,2048]{2,1,0:T(8,128)(2,1)S(1)} %collective-permute-done.17.low_ref, bf16[4,32,2048]{2,1,0:T(8,128)(2,1)S(1)} %collective-permute-done.26.high_ref, f32[128,1]{1,0:T(8,128)S(1)} %get-tuple-element.54.mix_low, ...), custom_call_target="tpu_custom_call" | custom-call | flops 2214592512 | bytes 8650752 | tf_op jit(solution)/shard_map/expert/pallas_call | solution.py:389
  86.1 13.2 %collective-permute-done.28 = bf16[4,32,2048]{2,1,0:T(8,128)(2,1)S(1)} collective-permute-done((bf16[4,32,2048]{2,1,0:T(8,128)(2,1)S(1)}, bf16[4,32,2048]{2,1,0:T(8,128)(2,1)S(1)}, u32[]{:S(2)}, u32[]{:S(2)}) %collective-permute-start.28) | collective-permute-done | bytes 524320 | tf_op jit(solution)/shard_map/ppermute | solution.py:54
  99.6 1.8 %collective-permute-start.29 = (bf16[32,2048]{1,0:T(8,128)(2,1)S(1)}, bf16[32,2048]{1,0:T(8,128)(2,1)S(1)}, u32[]{:S(2)}, u32[]{:S(2)}) collective-permute-start(bf16[32,2048]{1,0:T(8,128)(2,1)S(1)} %get-tuple-element.62), channel_id=1, source_target_pairs={{0,4},{1,5},{2,6},{3,7},{4,0},{5,1},{6,2},{7,3},{8,12},{9,13},{10,... | collective-permute-start | bytes 393224 | tf_op jit(solution)/shard_map/ppermute | solution.py:54
  101.4 1.8 %collective-permute-start.31 = (bf16[32,2048]{1,0:T(8,128)(2,1)S(1)}, bf16[32,2048]{1,0:T(8,128)(2,1)S(1)}, u32[]{:S(2)}, u32[]{:S(2)}) collective-permute-start(bf16[32,2048]{1,0:T(8,128)(2,1)S(1)} %get-tuple-element.63), channel_id=1, source_target_pairs={{0,12},{1,13},{2,14},{3,15},{4,8},{5,9},{6,10},{7,11},{8,4},{9,5},... | collective-permute-start | bytes 393224 | tf_op jit(solution)/shard_map/ppermute | solution.py:54
  103.1 2.1 %collective-permute-done.29 = bf16[32,2048]{1,0:T(8,128)(2,1)S(1)} collective-permute-done((bf16[32,2048]{1,0:T(8,128)(2,1)S(1)}, bf16[32,2048]{1,0:T(8,128)(2,1)S(1)}, u32[]{:S(2)}, u32[]{:S(2)}) %collective-permute-start.29) | collective-permute-done | bytes 131104 | tf_op jit(solution)/shard_map/ppermute | solution.py:54
  105.2 5.0 %collective-permute-done.31 = bf16[32,2048]{1,0:T(8,128)(2,1)S(1)} collective-permute-done((bf16[32,2048]{1,0:T(8,128)(2,1)S(1)}, bf16[32,2048]{1,0:T(8,128)(2,1)S(1)}, u32[]{:S(2)}, u32[]{:S(2)}) %collective-permute-start.31) | collective-permute-done | bytes 131104 | tf_op jit(solution)/shard_map/ppermute | solution.py:54
  110.2 4.3 %collective-permute-done.30 = bf16[32,2048]{1,0:T(8,128)(2,1)S(1)} collective-permute-done((bf16[32,2048]{1,0:T(8,128)(2,1)S(1)}, bf16[32,2048]{1,0:T(8,128)(2,1)S(1)}, u32[]{:S(2)}, u32[]{:S(2)}) %collective-permute-start.30) | collective-permute-done | bytes 131104 | tf_op jit(solution)/shard_map/ppermute | solution.py:54
  116.9 2.7 %collective-permute-done.32 = bf16[32,2048]{1,0:T(8,128)(2,1)S(1)} collective-permute-done((bf16[32,2048]{1,0:T(8,128)(2,1)S(1)}, bf16[32,2048]{1,0:T(8,128)(2,1)S(1)}, u32[]{:S(2)}, u32[]{:S(2)}) %collective-permute-start.32) | collective-permute-done | bytes 131104 | tf_op jit(solution)/shard_map/ppermute | solution.py:54
  (122 shorter events, 32.1 us)
Async XLA Ops:
  6.0 8.1 %collective-permute-start.3 = (bf16[32,896]{1,0:T(8,128)(2,1)}, bf16[32,896]{1,0:T(8,128)(2,1)S(1)}, u32[]{:S(2)}, u32[]{:S(2)}) collective-permute-start(bf16[32,896]{1,0:T(8,128)(2,1)} %get-tuple-element.34.query_ref), channel_id=1, source_target_pairs={{0,12},{1,13},{2,14},{3,15},{4,8},{5,9},{6,10},{7,11},{8,4},{9,5},... | collective-permute-start | bytes 172040 | tf_op jit(solution)/shard_map/ppermute | solution.py:54
  11.1 5.3 %collective-permute-start.2 = (bf16[32,896]{1,0:T(8,128)(2,1)}, bf16[32,896]{1,0:T(8,128)(2,1)S(1)}, u32[]{:S(2)}, u32[]{:S(2)}) collective-permute-start(bf16[32,896]{1,0:T(8,128)(2,1)} %get-tuple-element.34.query_ref), channel_id=1, source_target_pairs={{0,8},{1,9},{2,10},{3,11},{4,12},{5,13},{6,14},{7,15},{8,0},{9,1},... | collective-permute-start | bytes 172040 | tf_op jit(solution)/shard_map/ppermute | solution.py:54
  11.1 5.3 %collective-permute-start.1 = (bf16[32,896]{1,0:T(8,128)(2,1)}, bf16[32,896]{1,0:T(8,128)(2,1)S(1)}, u32[]{:S(2)}, u32[]{:S(2)}) collective-permute-start(bf16[32,896]{1,0:T(8,128)(2,1)} %get-tuple-element.34.query_ref), channel_id=1, source_target_pairs={{0,4},{1,5},{2,6},{3,7},{4,0},{5,1},{6,2},{7,3},{8,12},{9,13},{10,... | collective-permute-start | bytes 172040 | tf_op jit(solution)/shard_map/ppermute | solution.py:54
  11.7 12.3 %collective-permute-start = (f32[32,288]{1,0:T(8,128)}, f32[32,288]{1,0:T(8,128)S(1)}, u32[]{:S(2)}, u32[]{:S(2)}) collective-permute-start(f32[32,288]{1,0:T(8,128)} %get-tuple-element.32), channel_id=1, source_target_pairs={{0,16},{16,0},{1,17},{17,1},{2,18},{18,2},{3,19},{19,3},{4,20},{20... | collective-permute-start | bytes 110600 | tf_op jit(solution)/shard_map/ppermute | solution.py:54
  17.3 6.7 %collective-permute-start.4 = (bf16[4,32,896]{2,1,0:T(8,128)(2,1)S(1)}, bf16[4,32,896]{2,1,0:T(8,128)(2,1)S(1)}, u32[]{:S(2)}, u32[]{:S(2)}) collective-permute-start(bf16[4,32,896]{2,1,0:T(8,128)(2,1)S(1)} %pad_maximum_fusion.1.refs_0_), channel_id=1, source_target_pairs={{0,2},{1,3},{2,0},{3,1},{4,6},{5,7},{6,4},{7,5},{8,10},{9,11},{10,... | collective-permute-start | bytes 688136 | tf_op jit(solution)/shard_map/ppermute | solution.py:54
  19.6 4.7 %collective-permute-start.5 = (bf16[4,32,896]{2,1,0:T(8,128)(2,1)S(1)}, bf16[4,32,896]{2,1,0:T(8,128)(2,1)S(1)}, u32[]{:S(2)}, u32[]{:S(2)}) collective-permute-start(bf16[4,32,896]{2,1,0:T(8,128)(2,1)S(1)} %pad_maximum_fusion.1.refs_0_), channel_id=1, source_target_pairs={{0,1},{1,0},{2,3},{3,2},{4,5},{5,4},{6,7},{7,6},{8,9},{9,8},{10,11... | collective-permute-start | bytes 688136 | tf_op jit(solution)/shard_map/ppermute | solution.py:54
  28.5 6.0 %collective-permute-start.9 = (bf16[4,144,128]{2,1,0:T(8,128)(2,1)S(1)}, bf16[4,144,128]{2,1,0:T(8,128)(2,1)S(1)}, u32[]{:S(2)}, u32[]{:S(2)}) collective-permute-start(bf16[4,144,128]{2,1,0:T(8,128)(2,1)S(1)} %add_convert_fusion.4), channel_id=1, source_target_pairs={{0,2},{1,3},{2,0},{3,1},{4,6},{5,7},{6,4},{7,5},{8,10},{9,11},{10,... | collective-permute-start | bytes 442376 | tf_op jit(solution)/shard_map/ppermute | solution.py:54
  34.6 5.8 %collective-permute-start.12 = (bf16[144,128]{1,0:T(8,128)(2,1)S(1)}, bf16[144,128]{1,0:T(8,128)(2,1)S(1)}, u32[]{:S(2)}, u32[]{:S(2)}) collective-permute-start(bf16[144,128]{1,0:T(8,128)(2,1)S(1)} %get-tuple-element.67), channel_id=1, source_target_pairs={{0,12},{1,13},{2,14},{3,15},{4,8},{5,9},{6,10},{7,11},{8,4},{9,5},... | collective-permute-start | bytes 110600 | tf_op jit(solution)/shard_map/ppermute | solution.py:54
  36.8 4.9 %collective-permute-start.11 = (bf16[144,128]{1,0:T(8,128)(2,1)S(1)}, bf16[144,128]{1,0:T(8,128)(2,1)S(1)}, u32[]{:S(2)}, u32[]{:S(2)}) collective-permute-start(bf16[144,128]{1,0:T(8,128)(2,1)S(1)} %get-tuple-element.68), channel_id=1, source_target_pairs={{0,8},{1,9},{2,10},{3,11},{4,12},{5,13},{6,14},{7,15},{8,0},{9,1},... | collective-permute-start | bytes 110600 | tf_op jit(solution)/shard_map/ppermute | solution.py:54
  36.8 4.9 %collective-permute-start.10 = (bf16[144,128]{1,0:T(8,128)(2,1)S(1)}, bf16[144,128]{1,0:T(8,128)(2,1)S(1)}, u32[]{:S(2)}, u32[]{:S(2)}) collective-permute-start(bf16[144,128]{1,0:T(8,128)(2,1)S(1)} %get-tuple-element.69), channel_id=1, source_target_pairs={{0,4},{1,5},{2,6},{3,7},{4,0},{5,1},{6,2},{7,3},{8,12},{9,13},{10,... | collective-permute-start | bytes 110600 | tf_op jit(solution)/shard_map/ppermute | solution.py:54
  42.2 5.0 %collective-permute-start.13 = (bf16[32,2048]{1,0:T(8,128)(2,1)S(1)}, bf16[32,2048]{1,0:T(8,128)(2,1)S(1)}, u32[]{:S(2)}, u32[]{:S(2)}) collective-permute-start(bf16[32,2048]{1,0:T(8,128)(2,1)S(1)} %project_out.1.mine_ref), channel_id=1, source_target_pairs={{0,16},{16,0},{1,17},{17,1},{2,18},{18,2},{3,19},{19,3},{4,20},{20... | collective-permute-start | bytes 393224 | tf_op jit(solution)/shard_map/ppermute | solution.py:54
  47.4 7.2 %collective-permute-start.16 = (bf16[32,2048]{1,0:T(8,128)(2,1)S(1)}, bf16[32,2048]{1,0:T(8,128)(2,1)S(1)}, u32[]{:S(2)}, u32[]{:S(2)}) collective-permute-start(bf16[32,2048]{1,0:T(8,128)(2,1)S(1)} %get-tuple-element.43), channel_id=1, source_target_pairs={{0,12},{1,13},{2,14},{3,15},{4,8},{5,9},{6,10},{7,11},{8,4},{9,5},... | collective-permute-start | bytes 393224 | tf_op jit(solution)/shard_map/ppermute | solution.py:54
  49.5 9.7 %collective-permute-start.15 = (bf16[32,2048]{1,0:T(8,128)(2,1)S(1)}, bf16[32,2048]{1,0:T(8,128)(2,1)S(1)}, u32[]{:S(2)}, u32[]{:S(2)}) collective-permute-start(bf16[32,2048]{1,0:T(8,128)(2,1)S(1)} %get-tuple-element.43), channel_id=1, source_target_pairs={{0,8},{1,9},{2,10},{3,11},{4,12},{5,13},{6,14},{7,15},{8,0},{9,1},... | collective-permute-start | bytes 393224 | tf_op jit(solution)/shard_map/ppermute | solution.py:54
  50.2 8.9 %collective-permute-start.14 = (bf16[32,2048]{1,0:T(8,128)(2,1)S(1)}, bf16[32,2048]{1,0:T(8,128)(2,1)S(1)}, u32[]{:S(2)}, u32[]{:S(2)}) collective-permute-start(bf16[32,2048]{1,0:T(8,128)(2,1)S(1)} %get-tuple-element.43), channel_id=1, source_target_pairs={{0,4},{1,5},{2,6},{3,7},{4,0},{5,1},{6,2},{7,3},{8,12},{9,13},{10,... | collective-permute-start | bytes 393224 | tf_op jit(solution)/shard_map/ppermute | solution.py:54
  59.3 8.1 %collective-permute-start.21 = (bf16[4,32,2048]{2,1,0:T(8,128)(2,1)S(1)}, bf16[4,32,2048]{2,1,0:T(8,128)(2,1)S(1)}, u32[]{:S(2)}, u32[]{:S(2)}) collective-permute-start(bf16[4,32,2048]{2,1,0:T(8,128)(2,1)S(1)} %pad_maximum_fusion.low_ref), channel_id=1, source_target_pairs={{0,1},{1,0},{2,3},{3,2},{4,5},{5,4},{6,7},{7,6},{8,9},{9,8},{10,11... | collective-permute-start | bytes 1572872 | tf_op jit(solution)/shard_map/ppermute | solution.py:54
  59.3 16.4 %collective-permute-start.17 = (bf16[4,32,2048]{2,1,0:T(8,128)(2,1)S(1)}, bf16[4,32,2048]{2,1,0:T(8,128)(2,1)S(1)}, u32[]{:S(2)}, u32[]{:S(2)}) collective-permute-start(bf16[4,32,2048]{2,1,0:T(8,128)(2,1)S(1)} %pad_maximum_fusion.low_ref), channel_id=1, source_target_pairs={{0,2},{1,3},{2,0},{3,1},{4,6},{5,7},{6,4},{7,5},{8,10},{9,11},{10,... | collective-permute-start | bytes 1572872 | tf_op jit(solution)/shard_map/ppermute | solution.py:54
  61.0 5.5 %collective-permute-start.20 = (bf16[8,640]{1,0:T(8,128)(2,1)S(1)}, bf16[8,640]{1,0:T(8,128)(2,1)S(1)}, u32[]{:S(2)}, u32[]{:S(2)}) collective-permute-start(bf16[8,640]{1,0:T(8,128)(2,1)S(1)} %maximum_maximum_fusion), channel_id=1, source_target_pairs={{0,12},{1,13},{2,14},{3,15},{4,8},{5,9},{6,10},{7,11},{8,4},{9,5},... | collective-permute-start | bytes 30728 | tf_op jit(solution)/shard_map/ppermute | solution.py:54
  62.8 4.6 %collective-permute-start.19 = (bf16[8,640]{1,0:T(8,128)(2,1)S(1)}, bf16[8,640]{1,0:T(8,128)(2,1)S(1)}, u32[]{:S(2)}, u32[]{:S(2)}) collective-permute-start(bf16[8,640]{1,0:T(8,128)(2,1)S(1)} %maximum_maximum_fusion), channel_id=1, source_target_pairs={{0,8},{1,9},{2,10},{3,11},{4,12},{5,13},{6,14},{7,15},{8,0},{9,1},... | collective-permute-start | bytes 30728 | tf_op jit(solution)/shard_map/ppermute | solution.py:54
  62.8 4.6 %collective-permute-start.18 = (bf16[8,640]{1,0:T(8,128)(2,1)S(1)}, bf16[8,640]{1,0:T(8,128)(2,1)S(1)}, u32[]{:S(2)}, u32[]{:S(2)}) collective-permute-start(bf16[8,640]{1,0:T(8,128)(2,1)S(1)} %maximum_maximum_fusion), channel_id=1, source_target_pairs={{0,4},{1,5},{2,6},{3,7},{4,0},{5,1},{6,2},{7,3},{8,12},{9,13},{10,... | collective-permute-start | bytes 30728 | tf_op jit(solution)/shard_map/ppermute | solution.py:54
  85.2 14.1 %collective-permute-start.28 = (bf16[4,32,2048]{2,1,0:T(8,128)(2,1)S(1)}, bf16[4,32,2048]{2,1,0:T(8,128)(2,1)S(1)}, u32[]{:S(2)}, u32[]{:S(2)}) collective-permute-start(bf16[4,32,2048]{2,1,0:T(8,128)(2,1)S(1)} %add_convert_fusion.1), channel_id=1, source_target_pairs={{0,2},{1,3},{2,0},{3,1},{4,6},{5,7},{6,4},{7,5},{8,10},{9,11},{10,... | collective-permute-start | bytes 1572872 | tf_op jit(solution)/shard_map/ppermute | solution.py:54
  99.6 5.7 %collective-permute-start.29 = (bf16[32,2048]{1,0:T(8,128)(2,1)S(1)}, bf16[32,2048]{1,0:T(8,128)(2,1)S(1)}, u32[]{:S(2)}, u32[]{:S(2)}) collective-permute-start(bf16[32,2048]{1,0:T(8,128)(2,1)S(1)} %get-tuple-element.62), channel_id=1, source_target_pairs={{0,4},{1,5},{2,6},{3,7},{4,0},{5,1},{6,2},{7,3},{8,12},{9,13},{10,... | collective-permute-start | bytes 393224 | tf_op jit(solution)/shard_map/ppermute | solution.py:54
  101.4 8.9 %collective-permute-start.31 = (bf16[32,2048]{1,0:T(8,128)(2,1)S(1)}, bf16[32,2048]{1,0:T(8,128)(2,1)S(1)}, u32[]{:S(2)}, u32[]{:S(2)}) collective-permute-start(bf16[32,2048]{1,0:T(8,128)(2,1)S(1)} %get-tuple-element.63), channel_id=1, source_target_pairs={{0,12},{1,13},{2,14},{3,15},{4,8},{5,9},{6,10},{7,11},{8,4},{9,5},... | collective-permute-start | bytes 393224 | tf_op jit(solution)/shard_map/ppermute | solution.py:54
  103.1 11.4 %collective-permute-start.30 = (bf16[32,2048]{1,0:T(8,128)(2,1)S(1)}, bf16[32,2048]{1,0:T(8,128)(2,1)S(1)}, u32[]{:S(2)}, u32[]{:S(2)}) collective-permute-start(bf16[32,2048]{1,0:T(8,128)(2,1)S(1)} %get-tuple-element.64), channel_id=1, source_target_pairs={{0,8},{1,9},{2,10},{3,11},{4,12},{5,13},{6,14},{7,15},{8,0},{9,1},... | collective-permute-start | bytes 393224 | tf_op jit(solution)/shard_map/ppermute | solution.py:54
  114.6 5.0 %collective-permute-start.32 = (bf16[32,2048]{1,0:T(8,128)(2,1)S(1)}, bf16[32,2048]{1,0:T(8,128)(2,1)S(1)}, u32[]{:S(2)}, u32[]{:S(2)}) collective-permute-start(bf16[32,2048]{1,0:T(8,128)(2,1)S(1)} %fusion.2), channel_id=1, source_target_pairs={{0,16},{16,0},{1,17},{17,1},{2,18},{18,2},{3,19},{19,3},{4,20},{20... | collective-permute-start | bytes 393224 | tf_op jit(solution)/shard_map/ppermute | solution.py:54
  (28 other events, 442.5 us)

commit v3 on v2

--- a/solution.py
+++ b/solution.py
@@ -62,20 +62,25 @@
     return pieces
 
 
+def after(value, *others):
+    return lax.optimization_barrier((value, *others))[0]
+
+
 def add16(left, right):
     return (left.astype(f32) + right.astype(f32)).astype(bf16)
 
 
-def scatter_blocks(pieces, count, done=0):
-    (radix, stride0), *rest = phases(count)
-    for _, stride in reversed(rest):
-        if stride == done:
-            continue
+def fold_blocks(pieces, count):
+    for _, stride in reversed(phases(count)[1:]):
         half = len(pieces) // 2
         got = [swap(p, "blk", stride) for p in pieces[half:]]
         pieces = [add16(p, g) for p, g in zip(pieces[:half], got)]
-    (last,) = pieces
-    return [last[0]] + [swap(last[j], "blk", stride0 * j) for j in range(1, radix)]
+    return pieces[0]
+
+
+def trade_blocks(value, count):
+    radix, stride = phases(count)[0]
+    return [value[0]] + [swap(value[j], "blk", stride * j) for j in range(1, radix)]
 
 
 def place_of(relative, count):
@@ -242,13 +247,14 @@
 def slots_kernel(
     heads, slots, block, pieces, experts, place_ref, live_ref, index_ref, keys_ref, values_ref, *refs
 ):
-    queries, outs, mixes = refs[:pieces], refs[pieces : 2 * pieces], refs[2 * pieces :]
+    queries, outs, mix = refs[:pieces], refs[pieces : 2 * pieces], refs[2 * pieces]
     each, tok, lanes = queries[0].shape
     named = lax.broadcasted_iota(jnp.int32, (1, LANES), 1)
     mine = (named == index_ref[0]) | (named == index_ref[0] + experts)
-    for query, mix in zip(queries, mixes):
+    for i, query in enumerate(queries):
         shares = query[:, :, lanes - LANES :].reshape(each * tok, LANES).astype(f32)
-        mix[...] = jnp.sum(jnp.where(mine, shares, 0.0), axis=-1, keepdims=True)
+        share = jnp.sum(jnp.where(mine, shares, 0.0), axis=-1, keepdims=True)
+        mix[i * each : (i + 1) * each] = share.reshape(each, tok, 1)
     for out in outs:
         out[...] = jnp.zeros(out.shape, out.dtype)
     parts = []
@@ -278,17 +284,17 @@
     slots, each, tok = place.shape[0], queries[0].shape[0], queries[0].shape[1]
     pieces = len(queries)
     out = jax.ShapeDtypeStruct((each, heads * tok + 16, LANES), bf16)
-    mix = jax.ShapeDtypeStruct((each * tok, 1), f32)
+    mix = jax.ShapeDtypeStruct((pieces * each, tok, 1), f32)
     results = pl.pallas_call(
         functools.partial(slots_kernel, heads, slots, block, pieces, experts),
-        out_shape=(out,) * pieces + (mix,) * pieces,
+        out_shape=(out,) * pieces + (mix,),
         in_specs=[smem, smem, smem, vmem, vmem] + [vmem] * pieces,
-        out_specs=(vmem,) * (2 * pieces),
+        out_specs=(vmem,) * (pieces + 1),
         compiler_params=params(24),
         cost_estimate=cost(1 << 28, 2 << 20),
         name="attend_slots",
     )(place, live, index, keys, values, *queries)
-    return list(results[:pieces]), results[pieces:]
+    return list(results[:pieces]), results[pieces]
 
 
 def own_kernel(heads, rows_ref, query_ref, reach_ref, key_ref, value_ref, out_ref):
@@ -337,66 +343,105 @@
     )(w_out, own, *parts)
 
 
-def norm_kernel(hidden_ref, mine_ref, other_ref, gain_ref, resid_ref, out_ref):
+def norm_kernel(hidden_ref, mine_ref, other_ref, gain_ref, packed_ref, resid_ref, out_ref):
     added = mine_ref[...].astype(f32) + other_ref[...].astype(f32)
     resid = (hidden_ref[...].astype(f32) + added).astype(bf16)
     resid_ref[...] = resid
     value = resid.astype(f32)
     mean_square = jnp.mean(value * value, axis=-1, keepdims=True)
-    out_ref[...] = (value * lax.rsqrt(mean_square + EPSILON) * gain_ref[...]).astype(bf16)
-
-
-def norm(hidden, mine, other, gain):
-    out = jax.ShapeDtypeStruct(hidden.shape, bf16)
+    width = value.shape[1]
+    out_ref[:, :width] = (value * lax.rsqrt(mean_square + EPSILON) * gain_ref[...]).astype(bf16)
+    out_ref[:, width:] = packed_ref[...]
+
+
+def norm(hidden, mine, other, gain, packed):
+    tok, width = hidden.shape
     vmem = pl.BlockSpec(memory_space=pltpu.VMEM)
     return pl.pallas_call(
-        norm_kernel, out_shape=(out, out), in_specs=[vmem] * 4, out_specs=(vmem, vmem),
-        compiler_params=params(16), name="norm",
-    )(hidden, mine, other, gain[None])
-
-
-def expert_kernel(
-    low_ref, high_ref, mix_low, mix_high, gate_hbm, up_hbm, down_hbm, out_low, out_high,
-    gate, up, down, sems,
-):
-    copies = [
-        pltpu.make_async_copy(src.at[0], dst, sems.at[i])
-        for i, (src, dst) in enumerate(((gate_hbm, gate), (up_hbm, up), (down_hbm, down)))
-    ]
-    for copy in copies:
-        copy.start()
-    each, tok, width = low_ref.shape
-    rows = jnp.concatenate(
-        [r[...].reshape(each * tok, width) for r in (low_ref, high_ref)], axis=0
-    )
-    weight = jnp.concatenate([mix_low[...], mix_high[...]], axis=0)
-    copies[0].wait()
-    gated = nt(rows, gate[...])
+        norm_kernel,
+        out_shape=(
+            jax.ShapeDtypeStruct((tok, width), bf16),
+            jax.ShapeDtypeStruct((tok, width + packed.shape[1]), bf16),
+        ),
+        in_specs=[vmem] * 5,
+        out_specs=(vmem, vmem),
+        compiler_params=params(8),
+        name="norm",
+    )(hidden, mine, other, gain[None], packed)
+
+
+def expert_kernel(parts, cuts, *refs):
+    blocks = sum(cuts)
+    tokens, mixes, outs = refs[:parts], refs[parts : parts + blocks], refs[parts + blocks + 3 :]
+    gate, up, down = refs[parts + blocks : parts + blocks + 3]
+    tok, width = tokens[0].shape[1:]
+    rows = jnp.concatenate([r[i] for r in tokens for i in range(r.shape[0])], axis=0)
+    weight = jnp.concatenate([m[0] for m in mixes], axis=0)
+    gated = nt(rows, gate[0])
     gated = gated / (1.0 + jnp.exp(-gated))
-    copies[1].wait()
-    act = (gated * nt(rows, up[...])).astype(bf16)
-    copies[2].wait()
-    out = (nn(act, down[...]) * weight).astype(bf16)
-    out_low[...] = out[: each * tok].reshape(each, tok, width)
-    out_high[...] = out[each * tok :].reshape(each, tok, width)
-
-
-def expert(low, high, mix_low, mix_high, w_gate, w_up, w_down):
+    act = (gated * nt(rows, up[0])).astype(bf16)
+    out = (nn(act, down[0]) * weight).astype(bf16)
+    at = 0
+    for ref, size in zip(outs, cuts):
+        ref[...] = out[at * tok : (at + size) * tok].reshape(size, tok, width)
+        at += size
+
+
+def expert(tokens, places, mix, weights, cuts):
     vmem = pl.BlockSpec(memory_space=pltpu.VMEM)
-    hbm = pl.BlockSpec(memory_space=pltpu.HBM)
-    each, tok, _ = low.shape
-    out = jax.ShapeDtypeStruct(low.shape, bf16)
+    parts, size = len(tokens), weights[0].size
+    tok, width = tokens[0].shape[1], weights[0].shape[2]
+    blocks = [pl.BlockSpec((t.shape[0], tok, width), lambda i: (0, 0, 0)) for t in tokens]
+    shares = [pl.BlockSpec((1, tok, 1), lambda i, at=at: (at, 0, 0)) for at in places]
     return pl.pallas_call(
-        expert_kernel,
-        out_shape=(out, out),
-        in_specs=[vmem] * 4 + [hbm] * 3,
-        out_specs=(vmem, vmem),
-        scratch_shapes=[pltpu.VMEM(w.shape[1:], bf16) for w in (w_gate, w_up, w_down)]
-        + [pltpu.SemaphoreType.DMA((3,))],
-        compiler_params=params(28),
-        cost_estimate=cost(12 * each * tok * w_gate.size, 6 * w_gate.size),
+        functools.partial(expert_kernel, parts, cuts),
+        grid=(1,),
+        out_shape=tuple(jax.ShapeDtypeStruct((cut, tok, width), bf16) for cut in cuts),
+        in_specs=blocks + shares + [vmem] * len(weights),
+        out_specs=tuple(pl.BlockSpec((cut, tok, width), lambda i: (0, 0, 0)) for cut in cuts),
+        compiler_params=params(20),
+        cost_estimate=cost(6 * tok * len(places) * size, 6 * size),
         name="expert",
-    )(low, high, mix_low, mix_high, w_gate, w_up, w_down)
+    )(*tokens, *(mix for _ in places), *weights)
+
+
+def pack_rows(rows, tok):
+    count, width = rows.shape
+    lanes = -(-width // (tok // count * LANES)) * LANES
+    rows = jnp.pad(rows, ((0, 0), (0, tok // count * lanes - width)))
+    return jnp.concatenate([rows[:, at : at + lanes] for at in range(0, rows.shape[1], lanes)])
+
+
+def rows_kernel(count, index_ref, *refs):
+    out_ref = refs[-1]
+    target = index_ref[0] * NEW_DEV + lax.broadcasted_iota(jnp.int32, (1, NEW_DEV), 1)
+    width = out_ref.shape[1]
+    rows = []
+    for wide in [ref[i].astype(f32) for ref in refs[:-1] for i in range(ref.shape[0])]:
+        parts = [wide[at : at + count] for at in range(0, wide.shape[0], count)]
+        rows.append(jnp.concatenate(parts, axis=-1))
+    rows = jnp.concatenate(rows, axis=0)
+    slot = (rows[:, width : width + 1] * 256.0 + rows[:, width + 1 : width + 2]).astype(jnp.int32)
+    here = jnp.where(slot == target, 1.0, 0.0).astype(bf16)
+    out_ref[...] = lax.dot_general(
+        here, rows[:, :width].astype(bf16), (((0,), (0,)), ((), ())), preferred_element_type=f32
+    ).astype(bf16)
+
+
+def place_rows(index, pieces, count, width):
+    smem = pl.BlockSpec(memory_space=pltpu.SMEM)
+    out = (NEW_DEV, RANK + ROPE)
+    lanes = pieces[0].shape[2] - width
+    blocks = [pl.BlockSpec((*p.shape[:2], lanes), lambda i: (0, 0, width // lanes)) for p in pieces]
+    return pl.pallas_call(
+        functools.partial(rows_kernel, count),
+        grid=(1,),
+        out_shape=jax.ShapeDtypeStruct(out, bf16),
+        in_specs=[smem] + blocks,
+        out_specs=pl.BlockSpec(out, lambda i: (0, 0)),
+        compiler_params=params(8),
+        name="place_rows",
+    )(index, *pieces)
 
 
 def sum_heads(value):
@@ -453,61 +498,80 @@
     )
     live = jnp.where(slot_request >= 0, owner_length - slot_block * block, 0)
     place = place_of(owner ^ me, count)
-    partial, mixes = attend_slots(place, live, index, keys, values, queries, heads, block, experts)
-    parts = scatter_blocks(partial, count)
-    own = attend_own(draft_rows, payload, reach, w_key_up, w_value_up, heads)
-    mine, other = sum_heads(project_out(w_out, own, parts, heads, tok))
-    resid, moe_in = norm(hidden_in, mine, other, moe_gain)
-
+    partial, mix = attend_slots(place, live, index, keys, values, queries, heads, block, experts)
     node = jnp.arange(tok, dtype=jnp.int32)
     pick = (accepted.reshape(-1)[:, None] == node[None, :]).astype(bf16)
     chosen = jnp.dot(pick, draft_rows, preferred_element_type=f32).astype(bf16)
     target = new_slots.reshape(-1, 1)
     tail = jnp.concatenate([target // 256, target % 256], axis=1).astype(bf16)
-    packed = jnp.concatenate(
-        [chosen, tail, jnp.zeros((chosen.shape[0], LANES - ROPE - 2), bf16)], axis=1
-    )
+    packed = pack_rows(jnp.concatenate([chosen, tail], axis=1), tok)
+
+    own = attend_own(draft_rows, payload, reach, w_key_up, w_value_up, heads)
+    parts = trade_blocks(fold_blocks(partial, count), count)
+    mine, other = sum_heads(project_out(w_out, own, parts, heads, tok))
+    resid, moe_in = norm(hidden_in, mine, other, moe_gain, packed)
 
     (radix, stride), *rest = phases(count)
-    pieces = [moe_in] + [swap(moe_in, "blk", stride * j) for j in range(1, radix)]
-    packed, pieces[-1] = lax.optimization_barrier((packed, pieces[-1]))
-    tokens = [jnp.stack(pieces)]
-    rows = [jnp.stack([packed] + [swap(packed, "blk", stride * j) for j in range(1, radix)])]
+    near, half, mid = rest[-1][1], 1 << (len(rest) - 1), radix // 2
+    weights = (w_gate, w_up, w_down)
+    first = [swap(moe_in, "blk", stride * j) for j in range(1, radix)]
+    mine = [moe_in[None]]
     for _, step in rest[:-1]:
-        tokens = tokens + [swap(t, "blk", step) for t in tokens]
-    half, near = len(tokens), rest[-1][1]
-    kept, got = [], []
+        mine = mine + [swap(t, "blk", step) for t in mine]
+    first[-1] = after(first[-1], *mine[1:])
+    others = [jnp.stack(first)]
+    for _, step in rest[:-1]:
+        others = others + [swap(t, "blk", step) for t in others]
+    tokens = [list(pair) for pair in zip(mine, others)]
+    kept, sent = [], []
+    cuts = [mid] + [1] * (radix - mid)
     for i in range(half):
+        pair = tokens[i]
         if i:
-            tokens[i], kept[-1], sent, rows = lax.optimization_barrier(
-                (tokens[i], kept[-1], sent, rows)
-            )
-        far = swap(tokens[i], "blk", near)
-        keep, sent = expert(tokens[i], far, mixes[i], mixes[i + half], w_gate, w_up, w_down)
-        if not i:
-            rows[0], keep = lax.optimization_barrier((rows[0], keep))
-            for _, step in rest:
-                rows = rows + [swap(r, "blk", step) for r in rows]
-        kept.append(keep)
-        got.append(sent)
-    sums = [add16(k, swap(g, "blk", near)) for k, g in zip(kept, got)]
-    back = scatter_blocks(sums, count, near)
-
-    rows = jnp.concatenate(rows)
-    rows = rows.reshape(-1, packed.shape[1])
-    at = RANK + ROPE
-    slot = rows[:, at].astype(f32) * 256.0 + rows[:, at + 1].astype(f32)
-    here = (me * NEW_DEV + jnp.arange(NEW_DEV, dtype=jnp.int32)).astype(f32)
-    new_rows = jnp.dot(
-        (here[:, None] == slot[None, :]).astype(bf16), rows[:, :at], preferred_element_type=f32
-    ).astype(bf16)
-
-    total = back[0].astype(f32)
-    for value in back[1:]:
+            pair[1] = after(pair[1], kept[-1][0], sent[-1][0])
+        far = [swap(t, "blk", near) for t in pair]
+        tokens.append(far)
+        places = [at * radix + j for at in (i, i + half) for j in range(radix)]
+        inner = cuts if i + 1 == half else [radix]
+        done = list(expert(pair + far, places, mix, weights, cuts + inner))
+        kept.append(done[: len(cuts)])
+        sent.append(done[len(cuts) :])
+    order = [*range(1, len(cuts)), 0]
+    sums = []
+    for i in range(half):
+        if i + 1 == half:
+            got = [None] * len(cuts)
+            for at in order:
+                got[at] = swap(sent[i][at], "blk", near)
+        else:
+            got = swap(sent[i][0], "blk", near)
+            got = [got[:mid]] + [got[j : j + 1] for j in range(mid, radix)]
+        sums.append([add16(k, g) for k, g in zip(kept[i], got)])
+    for _, step in reversed(rest[:-1]):
+        part = len(sums) // 2
+        for i in range(part):
+            last = None
+            for at in order:
+                value = sums[part + i][at]
+                value = value if last is None else after(value, last)
+                last = sums[part + i][at] = value
+        got = [[swap(v, "blk", step) for v in values] for values in sums[part:]]
+        for i in range(part):
+            last = None
+            for at in order:
+                value = got[i][at] if last is None else after(got[i][at], last)
+                last = sums[i][at] = add16(sums[i][at], value)
+        sums = sums[:part]
+    (sums,) = sums
+    back = [swap(sums[at][0], "blk", stride * (mid + at - 1)) for at in order[:-1]]
+    back += [swap(sums[0][j], "blk", stride * j) for j in range(1, mid)]
+    total = sums[0][0].astype(f32)
+    for value in reversed(back):
         total = total + value.astype(f32)
     mine, other = sum_heads(total.astype(bf16))
-    routed = mine.astype(f32) + other.astype(f32)
-    layer_out = (resid.astype(f32) + routed).astype(bf16)
+    layer_out = (resid.astype(f32) + (mine.astype(f32) + other.astype(f32))).astype(bf16)
+    pieces = [piece for group in tokens for piece in group]
+    new_rows = place_rows(index, pieces, accepted.shape[1], hidden_in.shape[1])
     return (layer_out, new_rows)
 
 

time: 120 us -> 109 us (0.908)
  waiting for transfers between devices: 62.4 us -> 57.4 us
  starting transfers between devices: 34.9 us -> 31.7 us
  Pallas kernels: 17.1 us -> 14.7 us
    ppermute x33 -> x34, waiting for transfers between devices: 62.4 us -> 57.4 us  [swap(): return lax.ppermute(value, axis, [(i, i ^ bit) for i in range(count)])]
    ppermute x33 -> x34, starting transfers between devices: 34.9 us -> 31.7 us  [swap(): return lax.ppermute(value, axis, [(i, i ^ bit) for i in range(count)])]
    pallas_call x3 -> x4, Pallas kernels: 8.67 us -> 6.4 us  [the longest x2 5.29 us: expert(): pl.pallas_call(functools.partial(expert_kernel, parts, cuts), grid=(1,),...]
  transfers between devices with their start and end apart: 33 -> 34, of which waited for: 21 -> 22; matrix products, arithmetic and copies ran while one was open for 3% -> 2% of each run, Pallas kernels for 5% -> 4%
where the time goes in v3:
time: 109 us; the launch traced here: 108 us
  waiting for transfers between devices  57.4 us (53%)
  starting transfers between devices  31.7 us (29%)
  Pallas kernels  14.7 us (13%)
  other arithmetic  2.92 us (3%)
    ppermute x34, waiting for transfers between devices, swap(): return lax.ppermute(value, axis, [(i, i ^ bit) for i in range(count)])  57.4 us
    ppermute x34, starting transfers between devices, swap(): return lax.ppermute(value, axis, [(i, i ^ bit) for i in range(count)])  31.7 us
    pallas_call x2, Pallas kernels, expert(): pl.pallas_call(functools.partial(expert_kernel, parts, cuts), grid=(1,),...  5.29 us
    pallas_call x1, Pallas kernels, prepare(): pl.pallas_call(functools.partial(pre_kernel, heads, experts), grid=(1,),...  5.24 us
  transfers between devices with their start and end apart: 34, of which 22 were waited for; matrix products, arithmetic and copies ran while one was open for 2% of the time, Pallas kernels for 4%

profile of v3, /device:TPU:0, one launch (start us, length us, event | category | flops | bytes accessed | tf_op | source)
XLA Modules:
  0.0 108.5 jit_solution(5457333182620968924)
XLA Ops:
  0.7 5.2 %prepare.1 = (bf16[32,896]{1,0:T(8,128)(2,1)}, f32[32,288]{1,0:T(8,128)}, f32[32,256]{1,0:T(8,128)}, f32[32,32]{1,0:T(8,128)}) custom-call(s32[1]{0:T(128)} %bitcast.place_ref.index_ref, s32[16]{0:T(128)} %len_ref.1, bf16[32,2048]{1,0:T(8,128)(2,1)} %hidden_ref.3, f32[1,2048]{1,0:T(1,128)} %bitcast.47, s32[1,32]{1,0:T(1,128)} %parents_ref.1, ...), custom_call_target="tpu_custom_call" | custom-call | flops 144179200 | bytes 4505600 | tf_op jit(solution)/shard_map/prepare/pallas_call | solution.py:160
  6.0 5.1 %collective-permute-start.3 = (bf16[32,896]{1,0:T(8,128)(2,1)}, bf16[32,896]{1,0:T(8,128)(2,1)S(1)}, u32[]{:S(2)}, u32[]{:S(2)}) collective-permute-start(bf16[32,896]{1,0:T(8,128)(2,1)} %get-tuple-element.33.query_ref), channel_id=1, source_target_pairs={{0,12},{1,13},{2,14},{3,15},{4,8},{5,9},{6,10},{7,11},{8,4},{9,5},... | collective-permute-start | bytes 172040 | tf_op jit(solution)/shard_map/ppermute | solution.py:54
  11.7 1.6 %collective-permute-start = (f32[32,288]{1,0:T(8,128)}, f32[32,288]{1,0:T(8,128)S(1)}, u32[]{:S(2)}, u32[]{:S(2)}) collective-permute-start(f32[32,288]{1,0:T(8,128)} %get-tuple-element.31), channel_id=1, source_target_pairs={{0,16},{16,0},{1,17},{17,1},{2,18},{18,2},{3,19},{19,3},{4,20},{20... | collective-permute-start | bytes 110600 | tf_op jit(solution)/shard_map/ppermute | solution.py:54
  14.8 1.6 %collective-permute-done.2 = bf16[32,896]{1,0:T(8,128)(2,1)S(1)} collective-permute-done((bf16[32,896]{1,0:T(8,128)(2,1)}, bf16[32,896]{1,0:T(8,128)(2,1)S(1)}, u32[]{:S(2)}, u32[]{:S(2)}) %collective-permute-start.2) | collective-permute-done | bytes 57376 | tf_op jit(solution)/shard_map/ppermute | solution.py:54
  17.3 1.6 %collective-permute-start.4 = (bf16[4,32,896]{2,1,0:T(8,128)(2,1)S(1)}, bf16[4,32,896]{2,1,0:T(8,128)(2,1)S(1)}, u32[]{:S(2)}, u32[]{:S(2)}) collective-permute-start(bf16[4,32,896]{2,1,0:T(8,128)(2,1)S(1)} %pad_maximum_fusion.1.refs_0_), channel_id=1, source_target_pairs={{0,2},{1,3},{2,0},{3,1},{4,6},{5,7},{6,4},{7,5},{8,10},{9,11},{10,... | collective-permute-start | bytes 688136 | tf_op jit(solution)/shard_map/ppermute | solution.py:54
  19.2 4.8 %collective-permute-done.4.refs_1_ = bf16[4,32,896]{2,1,0:T(8,128)(2,1)S(1)} collective-permute-done((bf16[4,32,896]{2,1,0:T(8,128)(2,1)S(1)}, bf16[4,32,896]{2,1,0:T(8,128)(2,1)S(1)}, u32[]{:S(2)}, u32[]{:S(2)}) %collective-permute-start.4) | collective-permute-done | bytes 229408 | tf_op jit(solution)/shard_map/ppermute | solution.py:54
  28.2 1.7 %collective-permute-start.9 = (bf16[4,144,128]{2,1,0:T(8,128)(2,1)S(1)}, bf16[4,144,128]{2,1,0:T(8,128)(2,1)S(1)}, u32[]{:S(2)}, u32[]{:S(2)}) collective-permute-start(bf16[4,144,128]{2,1,0:T(8,128)(2,1)S(1)} %add_convert_fusion.4), channel_id=1, source_target_pairs={{0,2},{1,3},{2,0},{3,1},{4,6},{5,7},{6,4},{7,5},{8,10},{9,11},{10,... | collective-permute-start | bytes 442376 | tf_op jit(solution)/shard_map/ppermute | solution.py:54
  30.1 4.1 %collective-permute-done.9 = bf16[4,144,128]{2,1,0:T(8,128)(2,1)S(1)} collective-permute-done((bf16[4,144,128]{2,1,0:T(8,128)(2,1)S(1)}, bf16[4,144,128]{2,1,0:T(8,128)(2,1)S(1)}, u32[]{:S(2)}, u32[]{:S(2)}) %collective-permute-start.9) | collective-permute-done | bytes 147488 | tf_op jit(solution)/shard_map/ppermute | solution.py:54
  34.3 2.2 %collective-permute-start.12 = (bf16[144,128]{1,0:T(8,128)(2,1)S(1)}, bf16[144,128]{1,0:T(8,128)(2,1)S(1)}, u32[]{:S(2)}, u32[]{:S(2)}) collective-permute-start(bf16[144,128]{1,0:T(8,128)(2,1)S(1)} %get-tuple-element.60), channel_id=1, source_target_pairs={{0,12},{1,13},{2,14},{3,15},{4,8},{5,9},{6,10},{7,11},{8,4},{9,5},... | collective-permute-start | bytes 110600 | tf_op jit(solution)/shard_map/ppermute | solution.py:54
  36.5 2.2 %collective-permute-start.10 = (bf16[144,128]{1,0:T(8,128)(2,1)S(1)}, bf16[144,128]{1,0:T(8,128)(2,1)S(1)}, u32[]{:S(2)}, u32[]{:S(2)}) collective-permute-start(bf16[144,128]{1,0:T(8,128)(2,1)S(1)} %get-tuple-element.62), channel_id=1, source_target_pairs={{0,4},{1,5},{2,6},{3,7},{4,0},{5,1},{6,2},{7,3},{8,12},{9,13},{10,... | collective-permute-start | bytes 110600 | tf_op jit(solution)/shard_map/ppermute | solution.py:54
  43.5 3.4 %collective-permute-done.13.other_ref = bf16[32,2048]{1,0:T(8,128)(2,1)S(1)} collective-permute-done((bf16[32,2048]{1,0:T(8,128)(2,1)S(1)}, bf16[32,2048]{1,0:T(8,128)(2,1)S(1)}, u32[]{:S(2)}, u32[]{:S(2)}) %collective-permute-start.13) | collective-permute-done | bytes 131104 | tf_op jit(solution)/shard_map/ppermute | solution.py:54
  48.7 2.1 %collective-permute-start.16 = (bf16[32,2304]{1,0:T(8,128)(2,1)S(1)}, bf16[32,2304]{1,0:T(8,128)(2,1)S(1)}, u32[]{:S(2)}, u32[]{:S(2)}) collective-permute-start(bf16[32,2304]{1,0:T(8,128)(2,1)S(1)} %get-tuple-element.42), channel_id=1, source_target_pairs={{0,12},{1,13},{2,14},{3,15},{4,8},{5,9},{6,10},{7,11},{8,4},{9,5},... | collective-permute-start | bytes 442376 | tf_op jit(solution)/shard_map/ppermute | solution.py:54
  53.1 3.2 %collective-permute-done.16 = bf16[32,2304]{1,0:T(8,128)(2,1)S(1)} collective-permute-done((bf16[32,2304]{1,0:T(8,128)(2,1)S(1)}, bf16[32,2304]{1,0:T(8,128)(2,1)S(1)}, u32[]{:S(2)}, u32[]{:S(2)}) %collective-permute-start.16) | collective-permute-done | bytes 147488 | tf_op jit(solution)/shard_map/ppermute | solution.py:54
  56.3 5.4 %collective-permute-done.15 = bf16[32,2304]{1,0:T(8,128)(2,1)S(1)} collective-permute-done((bf16[32,2304]{1,0:T(8,128)(2,1)S(1)}, bf16[32,2304]{1,0:T(8,128)(2,1)S(1)}, u32[]{:S(2)}, u32[]{:S(2)}) %collective-permute-start.15) | collective-permute-done | bytes 147488 | tf_op jit(solution)/shard_map/ppermute | solution.py:54
  63.8 2.6 %expert.2 = (bf16[2,32,2048]{2,1,0:T(8,128)(2,1)S(1)}, bf16[1,32,2048]{2,1,0:T(8,128)(2,1)S(1)}, bf16[1,32,2048]{2,1,0:T(8,128)(2,1)S(1)}, bf16[4,32,2048]{2,1,0:T(8,128)(2,1)S(1)}) custom-call(bf16[1,32,2304]{2,1,0:T(8,128)(2,1)S(1)} %bitcast.35, bf16[3,32,2304]{2,1,0:T(8,128)(2,1)S(1)} %pad_maximum_fusion.refs_1_, ...), custom_call_target="tpu_custom_call" | custom-call | flops 2214592512 | bytes 8650752 | tf_op jit(solution)/shard_map/expert/pallas_call | solution.py:396
  66.4 7.9 %collective-permute-done.21.refs_1_.refs_3_ = bf16[3,32,2304]{2,1,0:T(8,128)(2,1)S(1)} collective-permute-done((bf16[3,32,2304]{2,1,0:T(8,128)(2,1)S(1)}, bf16[3,32,2304]{2,1,0:T(8,128)(2,1)S(1)}, u32[]{:S(2)}, u32[]{:S(2)}) %collective-permute-start.21) | collective-permute-done | bytes 442400 | tf_op jit(solution)/shard_map/ppermute | solution.py:54
  76.4 2.6 %expert.3 = (bf16[2,32,2048]{2,1,0:T(8,128)(2,1)S(1)}, bf16[1,32,2048]{2,1,0:T(8,128)(2,1)S(1)}, bf16[1,32,2048]{2,1,0:T(8,128)(2,1)S(1)}, bf16[2,32,2048]{2,1,0...) custom-call(bf16[1,32,2304]{2,1,0:T(8,128)(2,1)S(1)} %collective-permute-done.17.refs_0_.refs_2_, ...), custom_call_target="tpu_custom_call" | custom-call | flops 2214592512 | bytes 8650752 | tf_op jit(solution)/shard_map/expert/pallas_call | solution.py:396
  83.6 3.2 %collective-permute-done.29 = bf16[1,32,2048]{2,1,0:T(8,128)(2,1)S(1)} collective-permute-done((bf16[1,32,2048]{2,1,0:T(8,128)(2,1)S(1)}, bf16[1,32,2048]{2,1,0:T(8,128)(2,1)S(1)}, u32[]{:S(2)}, u32[]{:S(2)}) %collective-permute-start.29) | collective-permute-done | bytes 131104 | tf_op jit(solution)/shard_map/ppermute | solution.py:54
  86.9 2.8 %collective-permute-done.28 = bf16[1,32,2048]{2,1,0:T(8,128)(2,1)S(1)} collective-permute-done((bf16[1,32,2048]{2,1,0:T(8,128)(2,1)S(1)}, bf16[1,32,2048]{2,1,0:T(8,128)(2,1)S(1)}, u32[]{:S(2)}, u32[]{:S(2)}) %collective-permute-start.28) | collective-permute-done | bytes 131104 | tf_op jit(solution)/shard_map/ppermute | solution.py:54
  89.7 1.9 %collective-permute-start.31 = (bf16[32,2048]{1,0:T(8,128)(2,1)S(1)}, bf16[32,2048]{1,0:T(8,128)(2,1)S(1)}, u32[]{:S(2)}, u32[]{:S(2)}) collective-permute-start(bf16[32,2048]{1,0:T(8,128)(2,1)S(1)} %bitcast.43), channel_id=1, source_target_pairs={{0,12},{1,13},{2,14},{3,15},{4,8},{5,9},{6,10},{7,11},{8,4},{9,5},... | collective-permute-start | bytes 393224 | tf_op jit(solution)/shard_map/ppermute | solution.py:54
  91.6 2.9 %collective-permute-done.27 = bf16[2,32,2048]{2,1,0:T(8,128)(2,1)S(1)} collective-permute-done((bf16[2,32,2048]{2,1,0:T(8,128)(2,1)S(1)}, bf16[2,32,2048]{2,1,0:T(8,128)(2,1)S(1)}, u32[]{:S(2)}, u32[]{:S(2)}) %collective-permute-start.27) | collective-permute-done | bytes 262176 | tf_op jit(solution)/shard_map/ppermute | solution.py:54
  94.7 2.5 %collective-permute-done.31 = bf16[32,2048]{1,0:T(8,128)(2,1)S(1)} collective-permute-done((bf16[32,2048]{1,0:T(8,128)(2,1)S(1)}, bf16[32,2048]{1,0:T(8,128)(2,1)S(1)}, u32[]{:S(2)}, u32[]{:S(2)}) %collective-permute-start.31) | collective-permute-done | bytes 131104 | tf_op jit(solution)/shard_map/ppermute | solution.py:54
  97.2 4.5 %collective-permute-done.32 = bf16[32,2048]{1,0:T(8,128)(2,1)S(1)} collective-permute-done((bf16[32,2048]{1,0:T(8,128)(2,1)S(1)}, bf16[32,2048]{1,0:T(8,128)(2,1)S(1)}, u32[]{:S(2)}, u32[]{:S(2)}) %collective-permute-start.32) | collective-permute-done | bytes 131104 | tf_op jit(solution)/shard_map/ppermute | solution.py:54
  105.2 2.5 %collective-permute-done.33 = bf16[32,2048]{1,0:T(8,128)(2,1)S(1)} collective-permute-done((bf16[32,2048]{1,0:T(8,128)(2,1)S(1)}, bf16[32,2048]{1,0:T(8,128)(2,1)S(1)}, u32[]{:S(2)}, u32[]{:S(2)}) %collective-permute-start.33) | collective-permute-done | bytes 131104 | tf_op jit(solution)/shard_map/ppermute | solution.py:54
  (122 shorter events, 29.7 us)
Async XLA Ops:
  6.0 8.8 %collective-permute-start.3 = (bf16[32,896]{1,0:T(8,128)(2,1)}, bf16[32,896]{1,0:T(8,128)(2,1)S(1)}, u32[]{:S(2)}, u32[]{:S(2)}) collective-permute-start(bf16[32,896]{1,0:T(8,128)(2,1)} %get-tuple-element.33.query_ref), channel_id=1, source_target_pairs={{0,12},{1,13},{2,14},{3,15},{4,8},{5,9},{6,10},{7,11},{8,4},{9,5},... | collective-permute-start | bytes 172040 | tf_op jit(solution)/shard_map/ppermute | solution.py:54
  11.1 5.3 %collective-permute-start.2 = (bf16[32,896]{1,0:T(8,128)(2,1)}, bf16[32,896]{1,0:T(8,128)(2,1)S(1)}, u32[]{:S(2)}, u32[]{:S(2)}) collective-permute-start(bf16[32,896]{1,0:T(8,128)(2,1)} %get-tuple-element.33.query_ref), channel_id=1, source_target_pairs={{0,8},{1,9},{2,10},{3,11},{4,12},{5,13},{6,14},{7,15},{8,0},{9,1},... | collective-permute-start | bytes 172040 | tf_op jit(solution)/shard_map/ppermute | solution.py:54
  11.1 5.3 %collective-permute-start.1 = (bf16[32,896]{1,0:T(8,128)(2,1)}, bf16[32,896]{1,0:T(8,128)(2,1)S(1)}, u32[]{:S(2)}, u32[]{:S(2)}) collective-permute-start(bf16[32,896]{1,0:T(8,128)(2,1)} %get-tuple-element.33.query_ref), channel_id=1, source_target_pairs={{0,4},{1,5},{2,6},{3,7},{4,0},{5,1},{6,2},{7,3},{8,12},{9,13},{10,... | collective-permute-start | bytes 172040 | tf_op jit(solution)/shard_map/ppermute | solution.py:54
  11.7 7.1 %collective-permute-start = (f32[32,288]{1,0:T(8,128)}, f32[32,288]{1,0:T(8,128)S(1)}, u32[]{:S(2)}, u32[]{:S(2)}) collective-permute-start(f32[32,288]{1,0:T(8,128)} %get-tuple-element.31), channel_id=1, source_target_pairs={{0,16},{16,0},{1,17},{17,1},{2,18},{18,2},{3,19},{19,3},{4,20},{20... | collective-permute-start | bytes 110600 | tf_op jit(solution)/shard_map/ppermute | solution.py:54
  17.3 6.7 %collective-permute-start.4 = (bf16[4,32,896]{2,1,0:T(8,128)(2,1)S(1)}, bf16[4,32,896]{2,1,0:T(8,128)(2,1)S(1)}, u32[]{:S(2)}, u32[]{:S(2)}) collective-permute-start(bf16[4,32,896]{2,1,0:T(8,128)(2,1)S(1)} %pad_maximum_fusion.1.refs_0_), channel_id=1, source_target_pairs={{0,2},{1,3},{2,0},{3,1},{4,6},{5,7},{6,4},{7,5},{8,10},{9,11},{10,... | collective-permute-start | bytes 688136 | tf_op jit(solution)/shard_map/ppermute | solution.py:54
  19.1 5.0 %collective-permute-start.5 = (bf16[4,32,896]{2,1,0:T(8,128)(2,1)S(1)}, bf16[4,32,896]{2,1,0:T(8,128)(2,1)S(1)}, u32[]{:S(2)}, u32[]{:S(2)}) collective-permute-start(bf16[4,32,896]{2,1,0:T(8,128)(2,1)S(1)} %pad_maximum_fusion.1.refs_0_), channel_id=1, source_target_pairs={{0,1},{1,0},{2,3},{3,2},{4,5},{5,4},{6,7},{7,6},{8,9},{9,8},{10,11... | collective-permute-start | bytes 688136 | tf_op jit(solution)/shard_map/ppermute | solution.py:54
  28.2 6.0 %collective-permute-start.9 = (bf16[4,144,128]{2,1,0:T(8,128)(2,1)S(1)}, bf16[4,144,128]{2,1,0:T(8,128)(2,1)S(1)}, u32[]{:S(2)}, u32[]{:S(2)}) collective-permute-start(bf16[4,144,128]{2,1,0:T(8,128)(2,1)S(1)} %add_convert_fusion.4), channel_id=1, source_target_pairs={{0,2},{1,3},{2,0},{3,1},{4,6},{5,7},{6,4},{7,5},{8,10},{9,11},{10,... | collective-permute-start | bytes 442376 | tf_op jit(solution)/shard_map/ppermute | solution.py:54
  34.3 5.8 %collective-permute-start.12 = (bf16[144,128]{1,0:T(8,128)(2,1)S(1)}, bf16[144,128]{1,0:T(8,128)(2,1)S(1)}, u32[]{:S(2)}, u32[]{:S(2)}) collective-permute-start(bf16[144,128]{1,0:T(8,128)(2,1)S(1)} %get-tuple-element.60), channel_id=1, source_target_pairs={{0,12},{1,13},{2,14},{3,15},{4,8},{5,9},{6,10},{7,11},{8,4},{9,5},... | collective-permute-start | bytes 110600 | tf_op jit(solution)/shard_map/ppermute | solution.py:54
  36.5 4.9 %collective-permute-start.11 = (bf16[144,128]{1,0:T(8,128)(2,1)S(1)}, bf16[144,128]{1,0:T(8,128)(2,1)S(1)}, u32[]{:S(2)}, u32[]{:S(2)}) collective-permute-start(bf16[144,128]{1,0:T(8,128)(2,1)S(1)} %get-tuple-element.61), channel_id=1, source_target_pairs={{0,8},{1,9},{2,10},{3,11},{4,12},{5,13},{6,14},{7,15},{8,0},{9,1},... | collective-permute-start | bytes 110600 | tf_op jit(solution)/shard_map/ppermute | solution.py:54
  36.5 4.9 %collective-permute-start.10 = (bf16[144,128]{1,0:T(8,128)(2,1)S(1)}, bf16[144,128]{1,0:T(8,128)(2,1)S(1)}, u32[]{:S(2)}, u32[]{:S(2)}) collective-permute-start(bf16[144,128]{1,0:T(8,128)(2,1)S(1)} %get-tuple-element.62), channel_id=1, source_target_pairs={{0,4},{1,5},{2,6},{3,7},{4,0},{5,1},{6,2},{7,3},{8,12},{9,13},{10,... | collective-permute-start | bytes 110600 | tf_op jit(solution)/shard_map/ppermute | solution.py:54
  41.9 5.0 %collective-permute-start.13 = (bf16[32,2048]{1,0:T(8,128)(2,1)S(1)}, bf16[32,2048]{1,0:T(8,128)(2,1)S(1)}, u32[]{:S(2)}, u32[]{:S(2)}) collective-permute-start(bf16[32,2048]{1,0:T(8,128)(2,1)S(1)} %project_out.1.mine_ref), channel_id=1, source_target_pairs={{0,16},{16,0},{1,17},{17,1},{2,18},{18,2},{3,19},{19,3},{4,20},{20... | collective-permute-start | bytes 393224 | tf_op jit(solution)/shard_map/ppermute | solution.py:54
  47.1 6.0 %collective-permute-start.17 = (bf16[1,32,2304]{2,1,0:T(8,128)(2,1)S(1)}, bf16[1,32,2304]{2,1,0:T(8,128)(2,1)S(1)}, u32[]{:S(2)}, u32[]{:S(2)}) collective-permute-start(bf16[1,32,2304]{2,1,0:T(8,128)(2,1)S(1)} %bitcast.33), channel_id=1, source_target_pairs={{0,2},{1,3},{2,0},{3,1},{4,6},{5,7},{6,4},{7,5},{8,10},{9,11},{10,... | collective-permute-start | bytes 442376 | tf_op jit(solution)/shard_map/ppermute | solution.py:54
  48.7 7.6 %collective-permute-start.16 = (bf16[32,2304]{1,0:T(8,128)(2,1)S(1)}, bf16[32,2304]{1,0:T(8,128)(2,1)S(1)}, u32[]{:S(2)}, u32[]{:S(2)}) collective-permute-start(bf16[32,2304]{1,0:T(8,128)(2,1)S(1)} %get-tuple-element.42), channel_id=1, source_target_pairs={{0,12},{1,13},{2,14},{3,15},{4,8},{5,9},{6,10},{7,11},{8,4},{9,5},... | collective-permute-start | bytes 442376 | tf_op jit(solution)/shard_map/ppermute | solution.py:54
  50.8 10.9 %collective-permute-start.15 = (bf16[32,2304]{1,0:T(8,128)(2,1)S(1)}, bf16[32,2304]{1,0:T(8,128)(2,1)S(1)}, u32[]{:S(2)}, u32[]{:S(2)}) collective-permute-start(bf16[32,2304]{1,0:T(8,128)(2,1)S(1)} %get-tuple-element.42), channel_id=1, source_target_pairs={{0,8},{1,9},{2,10},{3,11},{4,12},{5,13},{6,14},{7,15},{8,0},{9,1},... | collective-permute-start | bytes 442376 | tf_op jit(solution)/shard_map/ppermute | solution.py:54
  51.6 10.1 %collective-permute-start.14 = (bf16[32,2304]{1,0:T(8,128)(2,1)S(1)}, bf16[32,2304]{1,0:T(8,128)(2,1)S(1)}, u32[]{:S(2)}, u32[]{:S(2)}) collective-permute-start(bf16[32,2304]{1,0:T(8,128)(2,1)S(1)} %get-tuple-element.42), channel_id=1, source_target_pairs={{0,4},{1,5},{2,6},{3,7},{4,0},{5,1},{6,2},{7,3},{8,12},{9,13},{10,... | collective-permute-start | bytes 442376 | tf_op jit(solution)/shard_map/ppermute | solution.py:54
  61.8 12.6 %collective-permute-start.21 = (bf16[3,32,2304]{2,1,0:T(8,128)(2,1)S(1)}, bf16[3,32,2304]{2,1,0:T(8,128)(2,1)S(1)}, u32[]{:S(2)}, u32[]{:S(2)}) collective-permute-start(bf16[3,32,2304]{2,1,0:T(8,128)(2,1)S(1)} %pad_maximum_fusion.refs_1_), channel_id=1, source_target_pairs={{0,2},{1,3},{2,0},{3,1},{4,6},{5,7},{6,4},{7,5},{8,10},{9,11},{10,... | collective-permute-start | bytes 1327112 | tf_op jit(solution)/shard_map/ppermute | solution.py:54
  79.2 4.4 %collective-permute-start.20 = (bf16[4,32,2048]{2,1,0:T(8,128)(2,1)S(1)}, bf16[4,32,2048]{2,1,0:T(8,128)(2,1)S(1)}, u32[]{:S(2)}, u32[]{:S(2)}) collective-permute-start(bf16[4,32,2048]{2,1,0:T(8,128)(2,1)S(1)} %get-tuple-element.46), channel_id=1, source_target_pairs={{0,1},{1,0},{2,3},{3,2},{4,5},{5,4},{6,7},{7,6},{8,9},{9,8},{10,11... | collective-permute-start | bytes 1572872 | tf_op jit(solution)/shard_map/ppermute | solution.py:54
  80.5 6.4 %collective-permute-start.29 = (bf16[1,32,2048]{2,1,0:T(8,128)(2,1)S(1)}, bf16[1,32,2048]{2,1,0:T(8,128)(2,1)S(1)}, u32[]{:S(2)}, u32[]{:S(2)}) collective-permute-start(bf16[1,32,2048]{2,1,0:T(8,128)(2,1)S(1)} %add_convert_fusion.11), channel_id=1, source_target_pairs={{0,2},{1,3},{2,0},{3,1},{4,6},{5,7},{6,4},{7,5},{8,10},{9,11},{10,... | collective-permute-start | bytes 393224 | tf_op jit(solution)/shard_map/ppermute | solution.py:54
  81.4 8.3 %collective-permute-start.28 = (bf16[1,32,2048]{2,1,0:T(8,128)(2,1)S(1)}, bf16[1,32,2048]{2,1,0:T(8,128)(2,1)S(1)}, u32[]{:S(2)}, u32[]{:S(2)}) collective-permute-start(bf16[1,32,2048]{2,1,0:T(8,128)(2,1)S(1)} %add_convert_fusion.12), channel_id=1, source_target_pairs={{0,2},{1,3},{2,0},{3,1},{4,6},{5,7},{6,4},{7,5},{8,10},{9,11},{10,... | collective-permute-start | bytes 393224 | tf_op jit(solution)/shard_map/ppermute | solution.py:54
  82.7 11.8 %collective-permute-start.27 = (bf16[2,32,2048]{2,1,0:T(8,128)(2,1)S(1)}, bf16[2,32,2048]{2,1,0:T(8,128)(2,1)S(1)}, u32[]{:S(2)}, u32[]{:S(2)}) collective-permute-start(bf16[2,32,2048]{2,1,0:T(8,128)(2,1)S(1)} %add_convert_fusion.1), channel_id=1, source_target_pairs={{0,2},{1,3},{2,0},{3,1},{4,6},{5,7},{6,4},{7,5},{8,10},{9,11},{10,... | collective-permute-start | bytes 786440 | tf_op jit(solution)/shard_map/ppermute | solution.py:54
  89.7 7.5 %collective-permute-start.31 = (bf16[32,2048]{1,0:T(8,128)(2,1)S(1)}, bf16[32,2048]{1,0:T(8,128)(2,1)S(1)}, u32[]{:S(2)}, u32[]{:S(2)}) collective-permute-start(bf16[32,2048]{1,0:T(8,128)(2,1)S(1)} %bitcast.43), channel_id=1, source_target_pairs={{0,12},{1,13},{2,14},{3,15},{4,8},{5,9},{6,10},{7,11},{8,4},{9,5},... | collective-permute-start | bytes 393224 | tf_op jit(solution)/shard_map/ppermute | solution.py:54
  91.6 10.1 %collective-permute-start.32 = (bf16[32,2048]{1,0:T(8,128)(2,1)S(1)}, bf16[32,2048]{1,0:T(8,128)(2,1)S(1)}, u32[]{:S(2)}, u32[]{:S(2)}) collective-permute-start(bf16[32,2048]{1,0:T(8,128)(2,1)S(1)} %bitcast.42), channel_id=1, source_target_pairs={{0,8},{1,9},{2,10},{3,11},{4,12},{5,13},{6,14},{7,15},{8,0},{9,1},... | collective-permute-start | bytes 393224 | tf_op jit(solution)/shard_map/ppermute | solution.py:54
  94.6 8.0 %collective-permute-start.30 = (bf16[32,2048]{1,0:T(8,128)(2,1)S(1)}, bf16[32,2048]{1,0:T(8,128)(2,1)S(1)}, u32[]{:S(2)}, u32[]{:S(2)}) collective-permute-start(bf16[32,2048]{1,0:T(8,128)(2,1)S(1)} %slice_bitcast_fusion), channel_id=1, source_target_pairs={{0,4},{1,5},{2,6},{3,7},{4,0},{5,1},{6,2},{7,3},{8,12},{9,13},{10,... | collective-permute-start | bytes 393224 | tf_op jit(solution)/shard_map/ppermute | solution.py:54
  102.7 5.0 %collective-permute-start.33 = (bf16[32,2048]{1,0:T(8,128)(2,1)S(1)}, bf16[32,2048]{1,0:T(8,128)(2,1)S(1)}, u32[]{:S(2)}, u32[]{:S(2)}) collective-permute-start(bf16[32,2048]{1,0:T(8,128)(2,1)S(1)} %fusion.2), channel_id=1, source_target_pairs={{0,16},{16,0},{1,17},{17,1},{2,18},{18,2},{3,19},{19,3},{4,20},{20... | collective-permute-start | bytes 393224 | tf_op jit(solution)/shard_map/ppermute | solution.py:54
  (29 other events, 402.9 us)

commit v4 on v3

--- a/solution.py
+++ b/solution.py
@@ -94,13 +94,22 @@
 
 
 def pre_kernel(
-    heads, experts, place_ref, len_ref, hidden_ref, gain_ref, parents_ref, routes_ref, logits_ref,
-    query_hbm, latent_hbm, out_ref, latent_ref, trig_ref, reach_ref, wq, wl, sems,
+    heads, experts, query_hbm, parents_hbm, lengths_hbm, routes_hbm, logits_hbm, hidden_hbm, gain_hbm,
+    latent_hbm, out_ref, latent_ref, trig_ref, reach_ref, wq, parents_ref, len_ref, routes_ref,
+    logits_ref, hidden_ref, gain_ref, wl, sems,
 ):
-    copy_q = pltpu.make_async_copy(query_hbm, wq, sems.at[0])
-    copy_l = pltpu.make_async_copy(latent_hbm, wl, sems.at[1])
-    copy_q.start()
-    copy_l.start()
+    copies = [
+        pltpu.make_async_copy(src, dst, sems.at[i])
+        for i, (src, dst) in enumerate((
+            (query_hbm, wq), (parents_hbm, parents_ref), (lengths_hbm, len_ref),
+            (routes_hbm, routes_ref), (logits_hbm, logits_ref), (hidden_hbm, hidden_ref),
+            (gain_hbm, gain_ref), (latent_hbm, wl),
+        ))
+    ]
+    for copy in copies[1:7] + copies[:1] + copies[7:]:
+        copy.start()
+    for copy in copies[1:7]:
+        copy.wait()
     tok = hidden_ref.shape[0]
     rows = lax.broadcasted_iota(jnp.int32, (tok, tok), 0)
     cols = lax.broadcasted_iota(jnp.int32, (tok, tok), 1)
@@ -112,7 +121,9 @@
     reach = nt(eye.astype(bf16), below.astype(bf16))
     reach_ref[...] = reach
     depth = jnp.sum(reach, axis=-1, keepdims=True) - 1.0
-    position = len_ref[place_ref[0]].astype(f32) + depth
+    at = lax.broadcasted_iota(jnp.int32, len_ref.shape, 1) == lax.axis_index("blk")
+    length = jnp.sum(jnp.where(at, len_ref[...].astype(f32), 0.0), axis=-1, keepdims=True)
+    position = length + depth
     lane = lax.broadcasted_iota(jnp.int32, (1, LANES), 1)
     freqs = ROPE_BASE ** (-2.0 * (lane % HALF).astype(f32) / ROPE)
     angles = position * freqs
@@ -131,7 +142,7 @@
     hidden = hidden_ref[...].astype(f32)
     mean_square = jnp.mean(hidden * hidden, axis=-1, keepdims=True)
     normed = (hidden * lax.rsqrt(mean_square + EPSILON) * gain_ref[...]).astype(bf16)
-    copy_q.wait()
+    copies[0].wait()
     size = NOPE + ROPE
     for h in range(heads):
         part = nt(normed, wq[h * size : h * size + NOPE])
@@ -146,40 +157,32 @@
     out_ref[:, base : base + LANES] = (first * cosine - second * sine).astype(bf16)
     out_ref[:, base + LANES : base + 2 * LANES] = (second * cosine + first * sine).astype(bf16)
     out_ref[:, base + 2 * LANES :] = mix.astype(bf16)
-    copy_l.wait()
+    copies[7].wait()
     latent_ref[...] = nt(normed, wl[...])
 
 
-def prepare(place, lengths, hidden, gain, parents, routes, logits, w_query, w_latent, heads, experts):
+def prepare(lengths, hidden, gain, parents, routes, logits, w_query, w_latent, heads, experts):
     tok, width = hidden.shape
-    smem = pl.BlockSpec(memory_space=pltpu.SMEM)
+    vmem = pl.BlockSpec(memory_space=pltpu.VMEM)
     hbm = pl.BlockSpec(memory_space=pltpu.HBM)
     lanes = heads * NOPE + 3 * LANES
-    small = (hidden, gain[None], parents, routes.T, logits.T)
-    whole = lambda shape: pl.BlockSpec(shape, lambda i: (0,) * len(shape))
+    args = (w_query, parents, lengths[None], routes.T, logits.T, hidden, gain[None], w_latent)
     return pl.pallas_call(
         functools.partial(pre_kernel, heads, experts),
-        grid=(1,),
         out_shape=(
             jax.ShapeDtypeStruct((tok, lanes), bf16),
             jax.ShapeDtypeStruct((tok, w_latent.shape[0]), f32),
             jax.ShapeDtypeStruct((tok, 2 * LANES), f32),
             jax.ShapeDtypeStruct((tok, tok), f32),
         ),
-        in_specs=[smem, smem, *(whole(v.shape) for v in small), hbm, hbm],
-        out_specs=tuple(
-            whole(shape)
-            for shape in ((tok, lanes), (tok, w_latent.shape[0]), (tok, 2 * LANES), (tok, tok))
-        ),
-        scratch_shapes=[
-            pltpu.VMEM(w_query.shape, bf16),
-            pltpu.VMEM(w_latent.shape, bf16),
-            pltpu.SemaphoreType.DMA((2,)),
-        ],
-        compiler_params=params(56),
+        in_specs=[hbm] * len(args),
+        out_specs=(vmem,) * 4,
+        scratch_shapes=[pltpu.VMEM(a.shape, a.dtype) for a in args]
+        + [pltpu.SemaphoreType.DMA((len(args),))],
+        compiler_params=params(58),
         cost_estimate=cost(2 * tok * width * 1100, 2 * width * 1100),
         name="prepare",
-    )(place, lengths, *small, w_query, w_latent)
+    )(*args)
 
 
 def spread(heads):
@@ -475,7 +478,7 @@
     experts = w_gate.shape[0] * count
     index = me[None]
     payload, latent, trig, reach = prepare(
-        index, lengths, hidden_in, attn_gain, parents, routes, route_logits, w_query, w_latent,
+        lengths, hidden_in, attn_gain, parents, routes, route_logits, w_query, w_latent,
         heads, experts,
     )
     queries = gather_blocks(payload, count)
@@ -550,12 +553,13 @@
     for _, step in reversed(rest[:-1]):
         part = len(sums) // 2
         for i in range(part):
-            last = None
-            for at in order:
-                value = sums[part + i][at]
-                value = value if last is None else after(value, last)
-                last = sums[part + i][at] = value
-        got = [[swap(v, "blk", step) for v in values] for values in sums[part:]]
+            lead = swap(sums[part + i][order[0]], "blk", step)
+            got = [None] * len(order)
+            got[order[0]] = lead
+            for at in order[1:]:
+                got[at] = swap(after(sums[part + i][at], lead), "blk", step)
+            sums[part + i] = got
+        got = sums[part:]
         for i in range(part):
             last = None
             for at in order:

time: 109 us -> 107 us (0.982)
  transfers between devices with their start and end apart: 34 -> 34, of which waited for: 22 -> 23; matrix products, arithmetic and copies ran while one was open for 2% -> 2% of each run, Pallas kernels for 4% -> 4%
where the time goes in v4:
time: 107 us
  waiting for transfers between devices  56.7 us (53%)
  starting transfers between devices  31.7 us (30%)
  Pallas kernels  13.9 us (13%)
  other arithmetic  2.92 us (3%)
    ppermute x34, waiting for transfers between devices, swap(): return lax.ppermute(value, axis, [(i, i ^ bit) for i in range(count)])  56.7 us
    ppermute x34, starting transfers between devices, swap(): return lax.ppermute(value, axis, [(i, i ^ bit) for i in range(count)])  31.7 us
    pallas_call x2, Pallas kernels, expert(): pl.pallas_call(functools.partial(expert_kernel, parts, cuts), grid=(1,),...  5.29 us
    pallas_call x1, Pallas kernels, prepare(): pl.pallas_call(functools.partial(pre_kernel, heads, experts), out_shape=(...  4.47 us
  transfers between devices with their start and end apart: 34, of which 23 were waited for; matrix products, arithmetic and copies ran while one was open for 2% of the time, Pallas kernels for 4%

profile of v4, /device:TPU:0, one launch (start us, length us, event | category | flops | bytes accessed | tf_op | source)
XLA Modules:
  0.0 106.9 jit_solution(6731754605703491909)
XLA Ops:
  0.7 4.5 %prepare.1 = (bf16[32,896]{1,0:T(8,128)(2,1)}, f32[32,288]{1,0:T(8,128)}, f32[32,256]{1,0:T(8,128)}, f32[32,32]{1,0:T(8,128)}) custom-call(bf16[768,2048]{1,0:T(8,128)(2,1)} %query_hbm.1, s32[1,32]{1,0:T(1,128)} %parents_hbm.1, s32[1,16]{1,0:T(1,128)} %bitcast.51, s32[6,32]{1,0:T(8,128)} %bitcast.49, f32[6,32]{1,0:T(8,128)} %bitcast.50, ...), custom_call_target="tpu_custom_call" | custom-call | flops 144179200 | bytes 4505600 | tf_op jit(solution)/shard_map/prepare/pallas_call | solution.py:170
  5.2 5.1 %collective-permute-start.3 = (bf16[32,896]{1,0:T(8,128)(2,1)}, bf16[32,896]{1,0:T(8,128)(2,1)S(1)}, u32[]{:S(2)}, u32[]{:S(2)}) collective-permute-start(bf16[32,896]{1,0:T(8,128)(2,1)} %get-tuple-element.33.query_ref), channel_id=1, source_target_pairs={{0,12},{1,13},{2,14},{3,15},{4,8},{5,9},{6,10},{7,11},{8,4},{9,5},... | collective-permute-start | bytes 172040 | tf_op jit(solution)/shard_map/ppermute | solution.py:54
  11.0 1.6 %collective-permute-start = (f32[32,288]{1,0:T(8,128)}, f32[32,288]{1,0:T(8,128)S(1)}, u32[]{:S(2)}, u32[]{:S(2)}) collective-permute-start(f32[32,288]{1,0:T(8,128)} %get-tuple-element.31), channel_id=1, source_target_pairs={{0,16},{16,0},{1,17},{17,1},{2,18},{18,2},{3,19},{19,3},{4,20},{20... | collective-permute-start | bytes 110600 | tf_op jit(solution)/shard_map/ppermute | solution.py:54
  14.0 1.6 %collective-permute-done.2 = bf16[32,896]{1,0:T(8,128)(2,1)S(1)} collective-permute-done((bf16[32,896]{1,0:T(8,128)(2,1)}, bf16[32,896]{1,0:T(8,128)(2,1)S(1)}, u32[]{:S(2)}, u32[]{:S(2)}) %collective-permute-start.2) | collective-permute-done | bytes 57376 | tf_op jit(solution)/shard_map/ppermute | solution.py:54
  16.5 1.6 %collective-permute-start.4 = (bf16[4,32,896]{2,1,0:T(8,128)(2,1)S(1)}, bf16[4,32,896]{2,1,0:T(8,128)(2,1)S(1)}, u32[]{:S(2)}, u32[]{:S(2)}) collective-permute-start(bf16[4,32,896]{2,1,0:T(8,128)(2,1)S(1)} %pad_maximum_fusion.1.refs_0_), channel_id=1, source_target_pairs={{0,2},{1,3},{2,0},{3,1},{4,6},{5,7},{6,4},{7,5},{8,10},{9,11},{10,... | collective-permute-start | bytes 688136 | tf_op jit(solution)/shard_map/ppermute | solution.py:54
  18.4 4.8 %collective-permute-done.4.refs_1_ = bf16[4,32,896]{2,1,0:T(8,128)(2,1)S(1)} collective-permute-done((bf16[4,32,896]{2,1,0:T(8,128)(2,1)S(1)}, bf16[4,32,896]{2,1,0:T(8,128)(2,1)S(1)}, u32[]{:S(2)}, u32[]{:S(2)}) %collective-permute-start.4) | collective-permute-done | bytes 229408 | tf_op jit(solution)/shard_map/ppermute | solution.py:54
  27.5 1.7 %collective-permute-start.9 = (bf16[4,144,128]{2,1,0:T(8,128)(2,1)S(1)}, bf16[4,144,128]{2,1,0:T(8,128)(2,1)S(1)}, u32[]{:S(2)}, u32[]{:S(2)}) collective-permute-start(bf16[4,144,128]{2,1,0:T(8,128)(2,1)S(1)} %add_convert_fusion.4), channel_id=1, source_target_pairs={{0,2},{1,3},{2,0},{3,1},{4,6},{5,7},{6,4},{7,5},{8,10},{9,11},{10,... | collective-permute-start | bytes 442376 | tf_op jit(solution)/shard_map/ppermute | solution.py:54
  29.4 4.1 %collective-permute-done.9 = bf16[4,144,128]{2,1,0:T(8,128)(2,1)S(1)} collective-permute-done((bf16[4,144,128]{2,1,0:T(8,128)(2,1)S(1)}, bf16[4,144,128]{2,1,0:T(8,128)(2,1)S(1)}, u32[]{:S(2)}, u32[]{:S(2)}) %collective-permute-start.9) | collective-permute-done | bytes 147488 | tf_op jit(solution)/shard_map/ppermute | solution.py:54
  33.5 2.2 %collective-permute-start.12 = (bf16[144,128]{1,0:T(8,128)(2,1)S(1)}, bf16[144,128]{1,0:T(8,128)(2,1)S(1)}, u32[]{:S(2)}, u32[]{:S(2)}) collective-permute-start(bf16[144,128]{1,0:T(8,128)(2,1)S(1)} %get-tuple-element.60), channel_id=1, source_target_pairs={{0,12},{1,13},{2,14},{3,15},{4,8},{5,9},{6,10},{7,11},{8,4},{9,5},... | collective-permute-start | bytes 110600 | tf_op jit(solution)/shard_map/ppermute | solution.py:54
  35.8 2.2 %collective-permute-start.10 = (bf16[144,128]{1,0:T(8,128)(2,1)S(1)}, bf16[144,128]{1,0:T(8,128)(2,1)S(1)}, u32[]{:S(2)}, u32[]{:S(2)}) collective-permute-start(bf16[144,128]{1,0:T(8,128)(2,1)S(1)} %get-tuple-element.62), channel_id=1, source_target_pairs={{0,4},{1,5},{2,6},{3,7},{4,0},{5,1},{6,2},{7,3},{8,12},{9,13},{10,... | collective-permute-start | bytes 110600 | tf_op jit(solution)/shard_map/ppermute | solution.py:54
  42.8 3.4 %collective-permute-done.13.other_ref = bf16[32,2048]{1,0:T(8,128)(2,1)S(1)} collective-permute-done((bf16[32,2048]{1,0:T(8,128)(2,1)S(1)}, bf16[32,2048]{1,0:T(8,128)(2,1)S(1)}, u32[]{:S(2)}, u32[]{:S(2)}) %collective-permute-start.13) | collective-permute-done | bytes 131104 | tf_op jit(solution)/shard_map/ppermute | solution.py:54
  47.9 2.0 %collective-permute-start.16 = (bf16[32,2304]{1,0:T(8,128)(2,1)S(1)}, bf16[32,2304]{1,0:T(8,128)(2,1)S(1)}, u32[]{:S(2)}, u32[]{:S(2)}) collective-permute-start(bf16[32,2304]{1,0:T(8,128)(2,1)S(1)} %get-tuple-element.42), channel_id=1, source_target_pairs={{0,12},{1,13},{2,14},{3,15},{4,8},{5,9},{6,10},{7,11},{8,4},{9,5},... | collective-permute-start | bytes 442376 | tf_op jit(solution)/shard_map/ppermute | solution.py:54
  52.3 3.2 %collective-permute-done.16 = bf16[32,2304]{1,0:T(8,128)(2,1)S(1)} collective-permute-done((bf16[32,2304]{1,0:T(8,128)(2,1)S(1)}, bf16[32,2304]{1,0:T(8,128)(2,1)S(1)}, u32[]{:S(2)}, u32[]{:S(2)}) %collective-permute-start.16) | collective-permute-done | bytes 147488 | tf_op jit(solution)/shard_map/ppermute | solution.py:54
  55.5 5.4 %collective-permute-done.15 = bf16[32,2304]{1,0:T(8,128)(2,1)S(1)} collective-permute-done((bf16[32,2304]{1,0:T(8,128)(2,1)S(1)}, bf16[32,2304]{1,0:T(8,128)(2,1)S(1)}, u32[]{:S(2)}, u32[]{:S(2)}) %collective-permute-start.15) | collective-permute-done | bytes 147488 | tf_op jit(solution)/shard_map/ppermute | solution.py:54
  63.0 2.6 %expert.2 = (bf16[2,32,2048]{2,1,0:T(8,128)(2,1)S(1)}, bf16[1,32,2048]{2,1,0:T(8,128)(2,1)S(1)}, bf16[1,32,2048]{2,1,0:T(8,128)(2,1)S(1)}, bf16[4,32,2048]{2,1,0:T(8,128)(2,1)S(1)}) custom-call(bf16[1,32,2304]{2,1,0:T(8,128)(2,1)S(1)} %bitcast.36, bf16[3,32,2304]{2,1,0:T(8,128)(2,1)S(1)} %pad_maximum_fusion.refs_1_, ...), custom_call_target="tpu_custom_call" | custom-call | flops 2214592512 | bytes 8650752 | tf_op jit(solution)/shard_map/expert/pallas_call | solution.py:399
  65.7 7.9 %collective-permute-done.21.refs_1_.refs_3_ = bf16[3,32,2304]{2,1,0:T(8,128)(2,1)S(1)} collective-permute-done((bf16[3,32,2304]{2,1,0:T(8,128)(2,1)S(1)}, bf16[3,32,2304]{2,1,0:T(8,128)(2,1)S(1)}, u32[]{:S(2)}, u32[]{:S(2)}) %collective-permute-start.21) | collective-permute-done | bytes 442400 | tf_op jit(solution)/shard_map/ppermute | solution.py:54
  75.6 2.6 %expert.3 = (bf16[2,32,2048]{2,1,0:T(8,128)(2,1)S(1)}, bf16[1,32,2048]{2,1,0:T(8,128)(2,1)S(1)}, bf16[1,32,2048]{2,1,0:T(8,128)(2,1)S(1)}, bf16[2,32,2048]{2,1,0...) custom-call(bf16[1,32,2304]{2,1,0:T(8,128)(2,1)S(1)} %collective-permute-done.17.refs_0_.refs_2_, ...), custom_call_target="tpu_custom_call" | custom-call | flops 2214592512 | bytes 8650752 | tf_op jit(solution)/shard_map/expert/pallas_call | solution.py:399
  81.0 4.3 %collective-permute-done.26 = bf16[1,32,2048]{2,1,0:T(8,128)(2,1)S(1)} collective-permute-done((bf16[1,32,2048]{2,1,0:T(8,128)(2,1)S(1)}, bf16[1,32,2048]{2,1,0:T(8,128)(2,1)S(1)}, u32[]{:S(2)}, u32[]{:S(2)}) %collective-permute-start.26) | collective-permute-done | bytes 131104 | tf_op jit(solution)/shard_map/ppermute | solution.py:54
  85.7 1.6 %collective-permute-start.27 = (bf16[2,32,2048]{2,1,0:T(8,128)(2,1)S(1)}, bf16[2,32,2048]{2,1,0:T(8,128)(2,1)S(1)}, u32[]{:S(2)}, u32[]{:S(2)}) collective-permute-start(bf16[2,32,2048]{2,1,0:T(8,128)(2,1)S(1)} %add_convert_fusion.1), channel_id=1, source_target_pairs={{0,2},{1,3},{2,0},{3,1},{4,6},{5,7},{6,4},{7,5},{8,10},{9,11},{10,... | collective-permute-start | bytes 786440 | tf_op jit(solution)/shard_map/ppermute | solution.py:54
  87.5 4.3 %collective-permute-done.29 = bf16[1,32,2048]{2,1,0:T(8,128)(2,1)S(1)} collective-permute-done((bf16[1,32,2048]{2,1,0:T(8,128)(2,1)S(1)}, bf16[1,32,2048]{2,1,0:T(8,128)(2,1)S(1)}, u32[]{:S(2)}, u32[]{:S(2)}) %collective-permute-start.29) | collective-permute-done | bytes 131104 | tf_op jit(solution)/shard_map/ppermute | solution.py:54
  91.8 1.9 %collective-permute-start.31 = (bf16[32,2048]{1,0:T(8,128)(2,1)S(1)}, bf16[32,2048]{1,0:T(8,128)(2,1)S(1)}, u32[]{:S(2)}, u32[]{:S(2)}) collective-permute-start(bf16[32,2048]{1,0:T(8,128)(2,1)S(1)} %bitcast.44), channel_id=1, source_target_pairs={{0,12},{1,13},{2,14},{3,15},{4,8},{5,9},{6,10},{7,11},{8,4},{9,5},... | collective-permute-start | bytes 393224 | tf_op jit(solution)/shard_map/ppermute | solution.py:54
  93.7 2.0 %collective-permute-done.27 = bf16[2,32,2048]{2,1,0:T(8,128)(2,1)S(1)} collective-permute-done((bf16[2,32,2048]{2,1,0:T(8,128)(2,1)S(1)}, bf16[2,32,2048]{2,1,0:T(8,128)(2,1)S(1)}, u32[]{:S(2)}, u32[]{:S(2)}) %collective-permute-start.27) | collective-permute-done | bytes 262176 | tf_op jit(solution)/shard_map/ppermute | solution.py:54
  96.6 3.3 %collective-permute-done.31 = bf16[32,2048]{1,0:T(8,128)(2,1)S(1)} collective-permute-done((bf16[32,2048]{1,0:T(8,128)(2,1)S(1)}, bf16[32,2048]{1,0:T(8,128)(2,1)S(1)}, u32[]{:S(2)}, u32[]{:S(2)}) %collective-permute-start.31) | collective-permute-done | bytes 131104 | tf_op jit(solution)/shard_map/ppermute | solution.py:54
  103.7 2.5 %collective-permute-done.33 = bf16[32,2048]{1,0:T(8,128)(2,1)S(1)} collective-permute-done((bf16[32,2048]{1,0:T(8,128)(2,1)S(1)}, bf16[32,2048]{1,0:T(8,128)(2,1)S(1)}, u32[]{:S(2)}, u32[]{:S(2)}) %collective-permute-start.33) | collective-permute-done | bytes 131104 | tf_op jit(solution)/shard_map/ppermute | solution.py:54
  (122 shorter events, 29.4 us)
Async XLA Ops:
  5.2 8.8 %collective-permute-start.3 = (bf16[32,896]{1,0:T(8,128)(2,1)}, bf16[32,896]{1,0:T(8,128)(2,1)S(1)}, u32[]{:S(2)}, u32[]{:S(2)}) collective-permute-start(bf16[32,896]{1,0:T(8,128)(2,1)} %get-tuple-element.33.query_ref), channel_id=1, source_target_pairs={{0,12},{1,13},{2,14},{3,15},{4,8},{5,9},{6,10},{7,11},{8,4},{9,5},... | collective-permute-start | bytes 172040 | tf_op jit(solution)/shard_map/ppermute | solution.py:54
  10.3 5.3 %collective-permute-start.2 = (bf16[32,896]{1,0:T(8,128)(2,1)}, bf16[32,896]{1,0:T(8,128)(2,1)S(1)}, u32[]{:S(2)}, u32[]{:S(2)}) collective-permute-start(bf16[32,896]{1,0:T(8,128)(2,1)} %get-tuple-element.33.query_ref), channel_id=1, source_target_pairs={{0,8},{1,9},{2,10},{3,11},{4,12},{5,13},{6,14},{7,15},{8,0},{9,1},... | collective-permute-start | bytes 172040 | tf_op jit(solution)/shard_map/ppermute | solution.py:54
  10.3 5.3 %collective-permute-start.1 = (bf16[32,896]{1,0:T(8,128)(2,1)}, bf16[32,896]{1,0:T(8,128)(2,1)S(1)}, u32[]{:S(2)}, u32[]{:S(2)}) collective-permute-start(bf16[32,896]{1,0:T(8,128)(2,1)} %get-tuple-element.33.query_ref), channel_id=1, source_target_pairs={{0,4},{1,5},{2,6},{3,7},{4,0},{5,1},{6,2},{7,3},{8,12},{9,13},{10,... | collective-permute-start | bytes 172040 | tf_op jit(solution)/shard_map/ppermute | solution.py:54
  11.0 7.1 %collective-permute-start = (f32[32,288]{1,0:T(8,128)}, f32[32,288]{1,0:T(8,128)S(1)}, u32[]{:S(2)}, u32[]{:S(2)}) collective-permute-start(f32[32,288]{1,0:T(8,128)} %get-tuple-element.31), channel_id=1, source_target_pairs={{0,16},{16,0},{1,17},{17,1},{2,18},{18,2},{3,19},{19,3},{4,20},{20... | collective-permute-start | bytes 110600 | tf_op jit(solution)/shard_map/ppermute | solution.py:54
  16.5 6.7 %collective-permute-start.4 = (bf16[4,32,896]{2,1,0:T(8,128)(2,1)S(1)}, bf16[4,32,896]{2,1,0:T(8,128)(2,1)S(1)}, u32[]{:S(2)}, u32[]{:S(2)}) collective-permute-start(bf16[4,32,896]{2,1,0:T(8,128)(2,1)S(1)} %pad_maximum_fusion.1.refs_0_), channel_id=1, source_target_pairs={{0,2},{1,3},{2,0},{3,1},{4,6},{5,7},{6,4},{7,5},{8,10},{9,11},{10,... | collective-permute-start | bytes 688136 | tf_op jit(solution)/shard_map/ppermute | solution.py:54
  18.3 5.0 %collective-permute-start.5 = (bf16[4,32,896]{2,1,0:T(8,128)(2,1)S(1)}, bf16[4,32,896]{2,1,0:T(8,128)(2,1)S(1)}, u32[]{:S(2)}, u32[]{:S(2)}) collective-permute-start(bf16[4,32,896]{2,1,0:T(8,128)(2,1)S(1)} %pad_maximum_fusion.1.refs_0_), channel_id=1, source_target_pairs={{0,1},{1,0},{2,3},{3,2},{4,5},{5,4},{6,7},{7,6},{8,9},{9,8},{10,11... | collective-permute-start | bytes 688136 | tf_op jit(solution)/shard_map/ppermute | solution.py:54
  27.5 6.0 %collective-permute-start.9 = (bf16[4,144,128]{2,1,0:T(8,128)(2,1)S(1)}, bf16[4,144,128]{2,1,0:T(8,128)(2,1)S(1)}, u32[]{:S(2)}, u32[]{:S(2)}) collective-permute-start(bf16[4,144,128]{2,1,0:T(8,128)(2,1)S(1)} %add_convert_fusion.4), channel_id=1, source_target_pairs={{0,2},{1,3},{2,0},{3,1},{4,6},{5,7},{6,4},{7,5},{8,10},{9,11},{10,... | collective-permute-start | bytes 442376 | tf_op jit(solution)/shard_map/ppermute | solution.py:54
  33.5 5.8 %collective-permute-start.12 = (bf16[144,128]{1,0:T(8,128)(2,1)S(1)}, bf16[144,128]{1,0:T(8,128)(2,1)S(1)}, u32[]{:S(2)}, u32[]{:S(2)}) collective-permute-start(bf16[144,128]{1,0:T(8,128)(2,1)S(1)} %get-tuple-element.60), channel_id=1, source_target_pairs={{0,12},{1,13},{2,14},{3,15},{4,8},{5,9},{6,10},{7,11},{8,4},{9,5},... | collective-permute-start | bytes 110600 | tf_op jit(solution)/shard_map/ppermute | solution.py:54
  35.8 4.9 %collective-permute-start.11 = (bf16[144,128]{1,0:T(8,128)(2,1)S(1)}, bf16[144,128]{1,0:T(8,128)(2,1)S(1)}, u32[]{:S(2)}, u32[]{:S(2)}) collective-permute-start(bf16[144,128]{1,0:T(8,128)(2,1)S(1)} %get-tuple-element.61), channel_id=1, source_target_pairs={{0,8},{1,9},{2,10},{3,11},{4,12},{5,13},{6,14},{7,15},{8,0},{9,1},... | collective-permute-start | bytes 110600 | tf_op jit(solution)/shard_map/ppermute | solution.py:54
  35.8 4.9 %collective-permute-start.10 = (bf16[144,128]{1,0:T(8,128)(2,1)S(1)}, bf16[144,128]{1,0:T(8,128)(2,1)S(1)}, u32[]{:S(2)}, u32[]{:S(2)}) collective-permute-start(bf16[144,128]{1,0:T(8,128)(2,1)S(1)} %get-tuple-element.62), channel_id=1, source_target_pairs={{0,4},{1,5},{2,6},{3,7},{4,0},{5,1},{6,2},{7,3},{8,12},{9,13},{10,... | collective-permute-start | bytes 110600 | tf_op jit(solution)/shard_map/ppermute | solution.py:54
  41.2 5.0 %collective-permute-start.13 = (bf16[32,2048]{1,0:T(8,128)(2,1)S(1)}, bf16[32,2048]{1,0:T(8,128)(2,1)S(1)}, u32[]{:S(2)}, u32[]{:S(2)}) collective-permute-start(bf16[32,2048]{1,0:T(8,128)(2,1)S(1)} %project_out.1.mine_ref), channel_id=1, source_target_pairs={{0,16},{16,0},{1,17},{17,1},{2,18},{18,2},{3,19},{19,3},{4,20},{20... | collective-permute-start | bytes 393224 | tf_op jit(solution)/shard_map/ppermute | solution.py:54
  46.4 6.0 %collective-permute-start.17 = (bf16[1,32,2304]{2,1,0:T(8,128)(2,1)S(1)}, bf16[1,32,2304]{2,1,0:T(8,128)(2,1)S(1)}, u32[]{:S(2)}, u32[]{:S(2)}) collective-permute-start(bf16[1,32,2304]{2,1,0:T(8,128)(2,1)S(1)} %bitcast.34), channel_id=1, source_target_pairs={{0,2},{1,3},{2,0},{3,1},{4,6},{5,7},{6,4},{7,5},{8,10},{9,11},{10,... | collective-permute-start | bytes 442376 | tf_op jit(solution)/shard_map/ppermute | solution.py:54
  47.9 7.6 %collective-permute-start.16 = (bf16[32,2304]{1,0:T(8,128)(2,1)S(1)}, bf16[32,2304]{1,0:T(8,128)(2,1)S(1)}, u32[]{:S(2)}, u32[]{:S(2)}) collective-permute-start(bf16[32,2304]{1,0:T(8,128)(2,1)S(1)} %get-tuple-element.42), channel_id=1, source_target_pairs={{0,12},{1,13},{2,14},{3,15},{4,8},{5,9},{6,10},{7,11},{8,4},{9,5},... | collective-permute-start | bytes 442376 | tf_op jit(solution)/shard_map/ppermute | solution.py:54
  50.0 10.9 %collective-permute-start.15 = (bf16[32,2304]{1,0:T(8,128)(2,1)S(1)}, bf16[32,2304]{1,0:T(8,128)(2,1)S(1)}, u32[]{:S(2)}, u32[]{:S(2)}) collective-permute-start(bf16[32,2304]{1,0:T(8,128)(2,1)S(1)} %get-tuple-element.42), channel_id=1, source_target_pairs={{0,8},{1,9},{2,10},{3,11},{4,12},{5,13},{6,14},{7,15},{8,0},{9,1},... | collective-permute-start | bytes 442376 | tf_op jit(solution)/shard_map/ppermute | solution.py:54
  50.8 10.1 %collective-permute-start.14 = (bf16[32,2304]{1,0:T(8,128)(2,1)S(1)}, bf16[32,2304]{1,0:T(8,128)(2,1)S(1)}, u32[]{:S(2)}, u32[]{:S(2)}) collective-permute-start(bf16[32,2304]{1,0:T(8,128)(2,1)S(1)} %get-tuple-element.42), channel_id=1, source_target_pairs={{0,4},{1,5},{2,6},{3,7},{4,0},{5,1},{6,2},{7,3},{8,12},{9,13},{10,... | collective-permute-start | bytes 442376 | tf_op jit(solution)/shard_map/ppermute | solution.py:54
  61.0 12.6 %collective-permute-start.21 = (bf16[3,32,2304]{2,1,0:T(8,128)(2,1)S(1)}, bf16[3,32,2304]{2,1,0:T(8,128)(2,1)S(1)}, u32[]{:S(2)}, u32[]{:S(2)}) collective-permute-start(bf16[3,32,2304]{2,1,0:T(8,128)(2,1)S(1)} %pad_maximum_fusion.refs_1_), channel_id=1, source_target_pairs={{0,2},{1,3},{2,0},{3,1},{4,6},{5,7},{6,4},{7,5},{8,10},{9,11},{10,... | collective-permute-start | bytes 1327112 | tf_op jit(solution)/shard_map/ppermute | solution.py:54
  78.5 8.9 %collective-permute-start.20 = (bf16[4,32,2048]{2,1,0:T(8,128)(2,1)S(1)}, bf16[4,32,2048]{2,1,0:T(8,128)(2,1)S(1)}, u32[]{:S(2)}, u32[]{:S(2)}) collective-permute-start(bf16[4,32,2048]{2,1,0:T(8,128)(2,1)S(1)} %get-tuple-element.46), channel_id=1, source_target_pairs={{0,1},{1,0},{2,3},{3,2},{4,5},{5,4},{6,7},{7,6},{8,9},{9,8},{10,11... | collective-permute-start | bytes 1572872 | tf_op jit(solution)/shard_map/ppermute | solution.py:54
  79.7 5.6 %collective-permute-start.26 = (bf16[1,32,2048]{2,1,0:T(8,128)(2,1)S(1)}, bf16[1,32,2048]{2,1,0:T(8,128)(2,1)S(1)}, u32[]{:S(2)}, u32[]{:S(2)}) collective-permute-start(bf16[1,32,2048]{2,1,0:T(8,128)(2,1)S(1)} %add_convert_fusion.12), channel_id=1, source_target_pairs={{0,2},{1,3},{2,0},{3,1},{4,6},{5,7},{6,4},{7,5},{8,10},{9,11},{10,... | collective-permute-start | bytes 393224 | tf_op jit(solution)/shard_map/ppermute | solution.py:54
  85.3 6.4 %collective-permute-start.29 = (bf16[1,32,2048]{2,1,0:T(8,128)(2,1)S(1)}, bf16[1,32,2048]{2,1,0:T(8,128)(2,1)S(1)}, u32[]{:S(2)}, u32[]{:S(2)}) collective-permute-start(bf16[1,32,2048]{2,1,0:T(8,128)(2,1)S(1)} %add_convert_fusion.10), channel_id=1, source_target_pairs={{0,2},{1,3},{2,0},{3,1},{4,6},{5,7},{6,4},{7,5},{8,10},{9,11},{10,... | collective-permute-start | bytes 393224 | tf_op jit(solution)/shard_map/ppermute | solution.py:54
  85.7 9.9 %collective-permute-start.27 = (bf16[2,32,2048]{2,1,0:T(8,128)(2,1)S(1)}, bf16[2,32,2048]{2,1,0:T(8,128)(2,1)S(1)}, u32[]{:S(2)}, u32[]{:S(2)}) collective-permute-start(bf16[2,32,2048]{2,1,0:T(8,128)(2,1)S(1)} %add_convert_fusion.1), channel_id=1, source_target_pairs={{0,2},{1,3},{2,0},{3,1},{4,6},{5,7},{6,4},{7,5},{8,10},{9,11},{10,... | collective-permute-start | bytes 786440 | tf_op jit(solution)/shard_map/ppermute | solution.py:54
  87.4 9.2 %collective-permute-start.32 = (bf16[32,2048]{1,0:T(8,128)(2,1)S(1)}, bf16[32,2048]{1,0:T(8,128)(2,1)S(1)}, u32[]{:S(2)}, u32[]{:S(2)}) collective-permute-start(bf16[32,2048]{1,0:T(8,128)(2,1)S(1)} %bitcast.43), channel_id=1, source_target_pairs={{0,8},{1,9},{2,10},{3,11},{4,12},{5,13},{6,14},{7,15},{8,0},{9,1},... | collective-permute-start | bytes 393224 | tf_op jit(solution)/shard_map/ppermute | solution.py:54
  91.8 8.1 %collective-permute-start.31 = (bf16[32,2048]{1,0:T(8,128)(2,1)S(1)}, bf16[32,2048]{1,0:T(8,128)(2,1)S(1)}, u32[]{:S(2)}, u32[]{:S(2)}) collective-permute-start(bf16[32,2048]{1,0:T(8,128)(2,1)S(1)} %bitcast.44), channel_id=1, source_target_pairs={{0,12},{1,13},{2,14},{3,15},{4,8},{5,9},{6,10},{7,11},{8,4},{9,5},... | collective-permute-start | bytes 393224 | tf_op jit(solution)/shard_map/ppermute | solution.py:54
  95.8 5.4 %collective-permute-start.30 = (bf16[32,2048]{1,0:T(8,128)(2,1)S(1)}, bf16[32,2048]{1,0:T(8,128)(2,1)S(1)}, u32[]{:S(2)}, u32[]{:S(2)}) collective-permute-start(bf16[32,2048]{1,0:T(8,128)(2,1)S(1)} %slice_bitcast_fusion), channel_id=1, source_target_pairs={{0,4},{1,5},{2,6},{3,7},{4,0},{5,1},{6,2},{7,3},{8,12},{9,13},{10,... | collective-permute-start | bytes 393224 | tf_op jit(solution)/shard_map/ppermute | solution.py:54
  101.2 5.0 %collective-permute-start.33 = (bf16[32,2048]{1,0:T(8,128)(2,1)S(1)}, bf16[32,2048]{1,0:T(8,128)(2,1)S(1)}, u32[]{:S(2)}, u32[]{:S(2)}) collective-permute-start(bf16[32,2048]{1,0:T(8,128)(2,1)S(1)} %fusion.2), channel_id=1, source_target_pairs={{0,16},{16,0},{1,17},{17,1},{2,18},{18,2},{3,19},{19,3},{4,20},{20... | collective-permute-start | bytes 393224 | tf_op jit(solution)/shard_map/ppermute | solution.py:54
  (29 other events, 393.9 us)

commit v5 on v4

--- a/solution.py
+++ b/solution.py
@@ -95,20 +95,20 @@
 
 def pre_kernel(
     heads, experts, query_hbm, parents_hbm, lengths_hbm, routes_hbm, logits_hbm, hidden_hbm, gain_hbm,
-    latent_hbm, out_ref, latent_ref, trig_ref, reach_ref, wq, parents_ref, len_ref, routes_ref,
-    logits_ref, hidden_ref, gain_ref, wl, sems,
+    out_ref, normed_ref, trig_ref, reach_ref, wq, parents_ref, len_ref, routes_ref,
+    logits_ref, hidden_ref, gain_ref, sems,
 ):
     copies = [
         pltpu.make_async_copy(src, dst, sems.at[i])
         for i, (src, dst) in enumerate((
             (query_hbm, wq), (parents_hbm, parents_ref), (lengths_hbm, len_ref),
             (routes_hbm, routes_ref), (logits_hbm, logits_ref), (hidden_hbm, hidden_ref),
-            (gain_hbm, gain_ref), (latent_hbm, wl),
+            (gain_hbm, gain_ref),
         ))
     ]
-    for copy in copies[1:7] + copies[:1] + copies[7:]:
+    for copy in copies[1:] + copies[:1]:
         copy.start()
-    for copy in copies[1:7]:
+    for copy in copies[1:]:
         copy.wait()
     tok = hidden_ref.shape[0]
     rows = lax.broadcasted_iota(jnp.int32, (tok, tok), 0)
@@ -157,21 +157,20 @@
     out_ref[:, base : base + LANES] = (first * cosine - second * sine).astype(bf16)
     out_ref[:, base + LANES : base + 2 * LANES] = (second * cosine + first * sine).astype(bf16)
     out_ref[:, base + 2 * LANES :] = mix.astype(bf16)
-    copies[7].wait()
-    latent_ref[...] = nt(normed, wl[...])
-
-
-def prepare(lengths, hidden, gain, parents, routes, logits, w_query, w_latent, heads, experts):
+    normed_ref[...] = normed
+
+
+def prepare(lengths, hidden, gain, parents, routes, logits, w_query, heads, experts):
     tok, width = hidden.shape
     vmem = pl.BlockSpec(memory_space=pltpu.VMEM)
     hbm = pl.BlockSpec(memory_space=pltpu.HBM)
     lanes = heads * NOPE + 3 * LANES
-    args = (w_query, parents, lengths[None], routes.T, logits.T, hidden, gain[None], w_latent)
+    args = (w_query, parents, lengths[None], routes.T, logits.T, hidden, gain[None])
     return pl.pallas_call(
         functools.partial(pre_kernel, heads, experts),
         out_shape=(
             jax.ShapeDtypeStruct((tok, lanes), bf16),
-            jax.ShapeDtypeStruct((tok, w_latent.shape[0]), f32),
+            jax.ShapeDtypeStruct((tok, width), bf16),
             jax.ShapeDtypeStruct((tok, 2 * LANES), f32),
             jax.ShapeDtypeStruct((tok, tok), f32),
         ),
@@ -403,7 +402,7 @@
         in_specs=blocks + shares + [vmem] * len(weights),
         out_specs=tuple(pl.BlockSpec((cut, tok, width), lambda i: (0, 0, 0)) for cut in cuts),
         compiler_params=params(20),
-        cost_estimate=cost(6 * tok * len(places) * size, 6 * size),
+        cost_estimate=cost(1, 1),
         name="expert",
     )(*tokens, *(mix for _ in places), *weights)
 
@@ -433,7 +432,7 @@
 
 def place_rows(index, pieces, count, width):
     smem = pl.BlockSpec(memory_space=pltpu.SMEM)
-    out = (NEW_DEV, RANK + ROPE)
+    out = (NEW_DEV, (RANK + ROPE) // 2)
     lanes = pieces[0].shape[2] - width
     blocks = [pl.BlockSpec((*p.shape[:2], lanes), lambda i: (0, 0, width // lanes)) for p in pieces]
     return pl.pallas_call(
@@ -477,13 +476,13 @@
     heads = w_key_up.shape[1] // NOPE
     experts = w_gate.shape[0] * count
     index = me[None]
-    payload, latent, trig, reach = prepare(
-        lengths, hidden_in, attn_gain, parents, routes, route_logits, w_query, w_latent,
+    payload, normed, trig, reach = prepare(
+        lengths, hidden_in, attn_gain, parents, routes, route_logits, w_query,
         heads, experts,
     )
     queries = gather_blocks(payload, count)
 
-    compressed = join_heads(latent)
+    compressed = join_heads(nt(normed, w_latent))
     low = compressed[:, :RANK]
     low = low * lax.rsqrt(jnp.mean(low * low, axis=-1, keepdims=True) + EPSILON) * kv_gain
     first, second = compressed[:, RANK : RANK + HALF], compressed[:, RANK + HALF :]
@@ -507,7 +506,10 @@
     chosen = jnp.dot(pick, draft_rows, preferred_element_type=f32).astype(bf16)
     target = new_slots.reshape(-1, 1)
     tail = jnp.concatenate([target // 256, target % 256], axis=1).astype(bf16)
-    packed = pack_rows(jnp.concatenate([chosen, tail], axis=1), tok)
+    span = (RANK + ROPE) // 2
+    odd = lax.axis_index("head") % 2 == 1
+    share = jnp.where(odd, chosen[:, span:], chosen[:, :span])
+    packed = pack_rows(jnp.concatenate([share, tail], axis=1), tok)
 
     own = attend_own(draft_rows, payload, reach, w_key_up, w_value_up, heads)
     parts = trade_blocks(fold_blocks(partial, count), count)
@@ -575,7 +577,9 @@
     mine, other = sum_heads(total.astype(bf16))
     layer_out = (resid.astype(f32) + (mine.astype(f32) + other.astype(f32))).astype(bf16)
     pieces = [piece for group in tokens for piece in group]
-    new_rows = place_rows(index, pieces, accepted.shape[1], hidden_in.shape[1])
+    share = place_rows(index, pieces, accepted.shape[1], hidden_in.shape[1])
+    other = swap(share, "head", 1)
+    new_rows = jnp.concatenate([jnp.where(odd, other, share), jnp.where(odd, share, other)], axis=1)
     return (layer_out, new_rows)
 
 

time: 107 us -> 106 us (level)
  waiting for transfers between devices: 56.7 us -> 52.6 us
  starting transfers between devices: 31.7 us -> 34 us
  matrix products: 0.19 us -> 1.58 us
  Pallas kernels: 13.9 us -> 12.8 us
    ppermute x34 -> x35, waiting for transfers between devices: 56.7 us -> 52.6 us  [swap(): return lax.ppermute(value, axis, [(i, i ^ bit) for i in range(count)])]
    ppermute x34 -> x35, starting transfers between devices: 31.7 us -> 34 us  [swap(): return lax.ppermute(value, axis, [(i, i ^ bit) for i in range(count)])]
    dot_general x0 -> x1, matrix products: none -> 1.39 us  [nt(): lax.dot_general(left, right, (((1,), (1,)), ((), ())), preferred_element_...]
  transfers between devices with their start and end apart: 34 -> 35, of which waited for: 23 -> 22; matrix products, arithmetic and copies ran while one was open for 2% -> 4% of each run, Pallas kernels for 4% -> 4%
where the time goes in v5:
time: 106 us; the launch traced here: 105 us
  waiting for transfers between devices  52.6 us (50%)
  starting transfers between devices  34 us (32%)
  Pallas kernels  12.8 us (12%)
  other arithmetic  2.89 us (3%)
  matrix products  1.58 us (1%)
    ppermute x35, waiting for transfers between devices, swap(): return lax.ppermute(value, axis, [(i, i ^ bit) for i in range(count)])  52.6 us
    ppermute x35, starting transfers between devices, swap(): return lax.ppermute(value, axis, [(i, i ^ bit) for i in range(count)])  34 us
    pallas_call x2, Pallas kernels, expert(): pl.pallas_call(functools.partial(expert_kernel, parts, cuts), grid=(1,),...  5.31 us
    pallas_call x1, Pallas kernels, prepare(): pl.pallas_call(functools.partial(pre_kernel, heads, experts), out_shape=(...  3.93 us
  transfers between devices with their start and end apart: 35, of which 22 were waited for; matrix products, arithmetic and copies ran while one was open for 4% of the time, Pallas kernels for 4%

profile of v5, /device:TPU:0, one launch (start us, length us, event | category | flops | bytes accessed | tf_op | source)
XLA Modules:
  0.0 105.5 jit_solution(520191440753914022)
XLA Ops:
  0.7 3.9 %prepare.1 = (bf16[32,896]{1,0:T(8,128)(2,1)}, bf16[32,2048]{1,0:T(8,128)(2,1)}, f32[32,256]{1,0:T(8,128)}, f32[32,32]{1,0:T(8,128)}) custom-call(bf16[768,2048]{1,0:T(8,128)(2,1)} %query_hbm.1, s32[1,32]{1,0:T(1,128)} %parents_hbm.1, s32[1,16]{1,0:T(1,128)} %bitcast.53, s32[6,32]{1,0:T(8,128)} %bitcast.51, f32[6,32]{1,0:T(8,128)} %bitcast.52, ...), custom_call_target="tpu_custom_call" | custom-call | flops 144179200 | bytes 4505600 | tf_op jit(solution)/shard_map/prepare/pallas_call | solution.py:169
  4.7 5.1 %collective-permute-start.3 = (bf16[32,896]{1,0:T(8,128)(2,1)}, bf16[32,896]{1,0:T(8,128)(2,1)S(1)}, u32[]{:S(2)}, u32[]{:S(2)}) collective-permute-start(bf16[32,896]{1,0:T(8,128)(2,1)} %get-tuple-element.33.query_ref), channel_id=1, source_target_pairs={{0,12},{1,13},{2,14},{3,15},{4,8},{5,9},{6,10},{7,11},{8,4},{9,5},... | collective-permute-start | bytes 172040 | tf_op jit(solution)/shard_map/ppermute | solution.py:54
  11.8 1.7 %collective-permute-start = (f32[32,288]{1,0:T(8,128)S(1)}, f32[32,288]{1,0:T(8,128)S(1)}, u32[]{:S(2)}, u32[]{:S(2)}) collective-permute-start(f32[32,288]{1,0:T(8,128)S(1)} %fusion.19), channel_id=1, source_target_pairs={{0,16},{16,0},{1,17},{17,1},{2,18},{18,2},{3,19},{19,3},{4,20},{20... | collective-permute-start | bytes 110600 | tf_op jit(solution)/shard_map/ppermute | solution.py:54
  16.3 1.7 %collective-permute-start.4 = (bf16[4,32,896]{2,1,0:T(8,128)(2,1)S(1)}, bf16[4,32,896]{2,1,0:T(8,128)(2,1)S(1)}, u32[]{:S(2)}, u32[]{:S(2)}) collective-permute-start(bf16[4,32,896]{2,1,0:T(8,128)(2,1)S(1)} %pad_maximum_fusion.1.refs_0_), channel_id=1, source_target_pairs={{0,2},{1,3},{2,0},{3,1},{4,6},{5,7},{6,4},{7,5},{8,10},{9,11},{10,... | collective-permute-start | bytes 688136 | tf_op jit(solution)/shard_map/ppermute | solution.py:54
  18.1 4.2 %collective-permute-done.4.refs_1_ = bf16[4,32,896]{2,1,0:T(8,128)(2,1)S(1)} collective-permute-done((bf16[4,32,896]{2,1,0:T(8,128)(2,1)S(1)}, bf16[4,32,896]{2,1,0:T(8,128)(2,1)S(1)}, u32[]{:S(2)}, u32[]{:S(2)}) %collective-permute-start.4) | collective-permute-done | bytes 229408 | tf_op jit(solution)/shard_map/ppermute | solution.py:54
  26.6 1.7 %collective-permute-start.9 = (bf16[4,144,128]{2,1,0:T(8,128)(2,1)S(1)}, bf16[4,144,128]{2,1,0:T(8,128)(2,1)S(1)}, u32[]{:S(2)}, u32[]{:S(2)}) collective-permute-start(bf16[4,144,128]{2,1,0:T(8,128)(2,1)S(1)} %add_convert_fusion.4), channel_id=1, source_target_pairs={{0,2},{1,3},{2,0},{3,1},{4,6},{5,7},{6,4},{7,5},{8,10},{9,11},{10,... | collective-permute-start | bytes 442376 | tf_op jit(solution)/shard_map/ppermute | solution.py:54
  28.4 4.2 %collective-permute-done.9 = bf16[4,144,128]{2,1,0:T(8,128)(2,1)S(1)} collective-permute-done((bf16[4,144,128]{2,1,0:T(8,128)(2,1)S(1)}, bf16[4,144,128]{2,1,0:T(8,128)(2,1)S(1)}, u32[]{:S(2)}, u32[]{:S(2)}) %collective-permute-start.9) | collective-permute-done | bytes 147488 | tf_op jit(solution)/shard_map/ppermute | solution.py:54
  32.7 3.8 %collective-permute-start.12 = (bf16[144,128]{1,0:T(8,128)(2,1)S(1)}, bf16[144,128]{1,0:T(8,128)(2,1)S(1)}, u32[]{:S(2)}, u32[]{:S(2)}) collective-permute-start(bf16[144,128]{1,0:T(8,128)(2,1)S(1)} %get-tuple-element.60), channel_id=1, source_target_pairs={{0,12},{1,13},{2,14},{3,15},{4,8},{5,9},{6,10},{7,11},{8,4},{9,5},... | collective-permute-start | bytes 110600 | tf_op jit(solution)/shard_map/ppermute | solution.py:54
  38.5 2.8 %collective-permute-done.11.refs_2_ = bf16[144,128]{1,0:T(8,128)(2,1)S(1)} collective-permute-done((bf16[144,128]{1,0:T(8,128)(2,1)S(1)}, bf16[144,128]{1,0:T(8,128)(2,1)S(1)}, u32[]{:S(2)}, u32[]{:S(2)}) %collective-permute-start.11) | collective-permute-done | bytes 36896 | tf_op jit(solution)/shard_map/ppermute | solution.py:54
  41.9 1.5 %collective-permute-start.13 = (bf16[32,2048]{1,0:T(8,128)(2,1)S(1)}, bf16[32,2048]{1,0:T(8,128)(2,1)S(1)}, u32[]{:S(2)}, u32[]{:S(2)}) collective-permute-start(bf16[32,2048]{1,0:T(8,128)(2,1)S(1)} %project_out.1.mine_ref), channel_id=1, source_target_pairs={{0,16},{16,0},{1,17},{17,1},{2,18},{18,2},{3,19},{19,3},{4,20},{20... | collective-permute-start | bytes 393224 | tf_op jit(solution)/shard_map/ppermute | solution.py:54
  43.5 3.4 %collective-permute-done.13.other_ref = bf16[32,2048]{1,0:T(8,128)(2,1)S(1)} collective-permute-done((bf16[32,2048]{1,0:T(8,128)(2,1)S(1)}, bf16[32,2048]{1,0:T(8,128)(2,1)S(1)}, u32[]{:S(2)}, u32[]{:S(2)}) %collective-permute-start.13) | collective-permute-done | bytes 131104 | tf_op jit(solution)/shard_map/ppermute | solution.py:54
  47.1 1.6 %collective-permute-start.17 = (bf16[1,32,2176]{2,1,0:T(8,128)(2,1)S(1)}, bf16[1,32,2176]{2,1,0:T(8,128)(2,1)S(1)}, u32[]{:S(2)}, u32[]{:S(2)}) collective-permute-start(bf16[1,32,2176]{2,1,0:T(8,128)(2,1)S(1)} %bitcast.36), channel_id=1, source_target_pairs={{0,2},{1,3},{2,0},{3,1},{4,6},{5,7},{6,4},{7,5},{8,10},{9,11},{10,... | collective-permute-start | bytes 417800 | tf_op jit(solution)/shard_map/ppermute | solution.py:54
  50.7 2.4 %collective-permute-start.14 = (bf16[32,2176]{1,0:T(8,128)(2,1)S(1)}, bf16[32,2176]{1,0:T(8,128)(2,1)S(1)}, u32[]{:S(2)}, u32[]{:S(2)}) collective-permute-start(bf16[32,2176]{1,0:T(8,128)(2,1)S(1)} %get-tuple-element.42), channel_id=1, source_target_pairs={{0,4},{1,5},{2,6},{3,7},{4,0},{5,1},{6,2},{7,3},{8,12},{9,13},{10,... | collective-permute-start | bytes 417800 | tf_op jit(solution)/shard_map/ppermute | solution.py:54
  53.0 2.7 %collective-permute-done.16 = bf16[32,2176]{1,0:T(8,128)(2,1)S(1)} collective-permute-done((bf16[32,2176]{1,0:T(8,128)(2,1)S(1)}, bf16[32,2176]{1,0:T(8,128)(2,1)S(1)}, u32[]{:S(2)}, u32[]{:S(2)}) %collective-permute-start.16) | collective-permute-done | bytes 139296 | tf_op jit(solution)/shard_map/ppermute | solution.py:54
  55.7 4.2 %collective-permute-done.15 = bf16[32,2176]{1,0:T(8,128)(2,1)S(1)} collective-permute-done((bf16[32,2176]{1,0:T(8,128)(2,1)S(1)}, bf16[32,2176]{1,0:T(8,128)(2,1)S(1)}, u32[]{:S(2)}, u32[]{:S(2)}) %collective-permute-start.15) | collective-permute-done | bytes 139296 | tf_op jit(solution)/shard_map/ppermute | solution.py:54
  62.0 2.7 %expert.2 = (bf16[2,32,2048]{2,1,0:T(8,128)(2,1)S(1)}, bf16[1,32,2048]{2,1,0:T(8,128)(2,1)S(1)}, bf16[1,32,2048]{2,1,0:T(8,128)(2,1)S(1)}, bf16[4,32,2048]{2,1,0:T(8,128)(2,1)S(1)}) custom-call(bf16[1,32,2176]{2,1,0:T(8,128)(2,1)S(1)} %bitcast.38, bf16[3,32,2176]{2,1,0:T(8,128)(2,1)S(1)} %pad_maximum_fusion.refs_1_, ...), custom_call_target="tpu_custom_call" | custom-call | flops 1 | bytes 1 | tf_op jit(solution)/shard_map/expert/pallas_call | solution.py:398
  64.7 7.4 %collective-permute-done.21.refs_1_.refs_3_ = bf16[3,32,2176]{2,1,0:T(8,128)(2,1)S(1)} collective-permute-done((bf16[3,32,2176]{2,1,0:T(8,128)(2,1)S(1)}, bf16[3,32,2176]{2,1,0:T(8,128)(2,1)S(1)}, u32[]{:S(2)}, u32[]{:S(2)}) %collective-permute-start.21) | collective-permute-done | bytes 417824 | tf_op jit(solution)/shard_map/ppermute | solution.py:54
  74.1 2.7 %expert.3 = (bf16[2,32,2048]{2,1,0:T(8,128)(2,1)S(1)}, bf16[1,32,2048]{2,1,0:T(8,128)(2,1)S(1)}, bf16[1,32,2048]{2,1,0:T(8,128)(2,1)S(1)}, bf16[2,32,2048]{2,1,0...) custom-call(bf16[1,32,2176]{2,1,0:T(8,128)(2,1)S(1)} %collective-permute-done.17.refs_0_.refs_2_, ...), custom_call_target="tpu_custom_call" | custom-call | flops 1 | bytes 1 | tf_op jit(solution)/shard_map/expert/pallas_call | solution.py:398
  79.5 4.3 %collective-permute-done.26 = bf16[1,32,2048]{2,1,0:T(8,128)(2,1)S(1)} collective-permute-done((bf16[1,32,2048]{2,1,0:T(8,128)(2,1)S(1)}, bf16[1,32,2048]{2,1,0:T(8,128)(2,1)S(1)}, u32[]{:S(2)}, u32[]{:S(2)}) %collective-permute-start.26) | collective-permute-done | bytes 131104 | tf_op jit(solution)/shard_map/ppermute | solution.py:54
  86.0 4.3 %collective-permute-done.29 = bf16[1,32,2048]{2,1,0:T(8,128)(2,1)S(1)} collective-permute-done((bf16[1,32,2048]{2,1,0:T(8,128)(2,1)S(1)}, bf16[1,32,2048]{2,1,0:T(8,128)(2,1)S(1)}, u32[]{:S(2)}, u32[]{:S(2)}) %collective-permute-start.29) | collective-permute-done | bytes 131104 | tf_op jit(solution)/shard_map/ppermute | solution.py:54
  90.3 2.4 %collective-permute-start.31 = (bf16[32,2048]{1,0:T(8,128)(2,1)S(1)}, bf16[32,2048]{1,0:T(8,128)(2,1)S(1)}, u32[]{:S(2)}, u32[]{:S(2)}) collective-permute-start(bf16[32,2048]{1,0:T(8,128)(2,1)S(1)} %bitcast.46), channel_id=1, source_target_pairs={{0,12},{1,13},{2,14},{3,15},{4,8},{5,9},{6,10},{7,11},{8,4},{9,5},... | collective-permute-start | bytes 393224 | tf_op jit(solution)/shard_map/ppermute | solution.py:54
  96.2 2.2 %collective-permute-done.31 = bf16[32,2048]{1,0:T(8,128)(2,1)S(1)} collective-permute-done((bf16[32,2048]{1,0:T(8,128)(2,1)S(1)}, bf16[32,2048]{1,0:T(8,128)(2,1)S(1)}, u32[]{:S(2)}, u32[]{:S(2)}) %collective-permute-start.31) | collective-permute-done | bytes 131104 | tf_op jit(solution)/shard_map/ppermute | solution.py:54
  99.7 1.6 %collective-permute-start.33 = (bf16[32,2048]{1,0:T(8,128)(2,1)S(1)}, bf16[32,2048]{1,0:T(8,128)(2,1)S(1)}, u32[]{:S(2)}, u32[]{:S(2)}) collective-permute-start(bf16[32,2048]{1,0:T(8,128)(2,1)S(1)} %fusion.2), channel_id=1, source_target_pairs={{0,16},{16,0},{1,17},{17,1},{2,18},{18,2},{3,19},{19,3},{4,20},{20... | collective-permute-start | bytes 393224 | tf_op jit(solution)/shard_map/ppermute | solution.py:54
  102.0 2.8 %collective-permute-done.33 = bf16[32,2048]{1,0:T(8,128)(2,1)S(1)} collective-permute-done((bf16[32,2048]{1,0:T(8,128)(2,1)S(1)}, bf16[32,2048]{1,0:T(8,128)(2,1)S(1)}, u32[]{:S(2)}, u32[]{:S(2)}) %collective-permute-start.33) | collective-permute-done | bytes 131104 | tf_op jit(solution)/shard_map/ppermute | solution.py:54
  (128 shorter events, 29.3 us)
Async XLA Ops:
  4.7 11.5 %collective-permute-start.3 = (bf16[32,896]{1,0:T(8,128)(2,1)}, bf16[32,896]{1,0:T(8,128)(2,1)S(1)}, u32[]{:S(2)}, u32[]{:S(2)}) collective-permute-start(bf16[32,896]{1,0:T(8,128)(2,1)} %get-tuple-element.33.query_ref), channel_id=1, source_target_pairs={{0,12},{1,13},{2,14},{3,15},{4,8},{5,9},{6,10},{7,11},{8,4},{9,5},... | collective-permute-start | bytes 172040 | tf_op jit(solution)/shard_map/ppermute | solution.py:54
  9.8 6.4 %collective-permute-start.2 = (bf16[32,896]{1,0:T(8,128)(2,1)}, bf16[32,896]{1,0:T(8,128)(2,1)S(1)}, u32[]{:S(2)}, u32[]{:S(2)}) collective-permute-start(bf16[32,896]{1,0:T(8,128)(2,1)} %get-tuple-element.33.query_ref), channel_id=1, source_target_pairs={{0,8},{1,9},{2,10},{3,11},{4,12},{5,13},{6,14},{7,15},{8,0},{9,1},... | collective-permute-start | bytes 172040 | tf_op jit(solution)/shard_map/ppermute | solution.py:54
  9.8 6.4 %collective-permute-start.1 = (bf16[32,896]{1,0:T(8,128)(2,1)}, bf16[32,896]{1,0:T(8,128)(2,1)S(1)}, u32[]{:S(2)}, u32[]{:S(2)}) collective-permute-start(bf16[32,896]{1,0:T(8,128)(2,1)} %get-tuple-element.33.query_ref), channel_id=1, source_target_pairs={{0,4},{1,5},{2,6},{3,7},{4,0},{5,1},{6,2},{7,3},{8,12},{9,13},{10,... | collective-permute-start | bytes 172040 | tf_op jit(solution)/shard_map/ppermute | solution.py:54
  16.3 6.1 %collective-permute-start.4 = (bf16[4,32,896]{2,1,0:T(8,128)(2,1)S(1)}, bf16[4,32,896]{2,1,0:T(8,128)(2,1)S(1)}, u32[]{:S(2)}, u32[]{:S(2)}) collective-permute-start(bf16[4,32,896]{2,1,0:T(8,128)(2,1)S(1)} %pad_maximum_fusion.1.refs_0_), channel_id=1, source_target_pairs={{0,2},{1,3},{2,0},{3,1},{4,6},{5,7},{6,4},{7,5},{8,10},{9,11},{10,... | collective-permute-start | bytes 688136 | tf_op jit(solution)/shard_map/ppermute | solution.py:54
  18.1 4.4 %collective-permute-start.5 = (bf16[4,32,896]{2,1,0:T(8,128)(2,1)S(1)}, bf16[4,32,896]{2,1,0:T(8,128)(2,1)S(1)}, u32[]{:S(2)}, u32[]{:S(2)}) collective-permute-start(bf16[4,32,896]{2,1,0:T(8,128)(2,1)S(1)} %pad_maximum_fusion.1.refs_0_), channel_id=1, source_target_pairs={{0,1},{1,0},{2,3},{3,2},{4,5},{5,4},{6,7},{7,6},{8,9},{9,8},{10,11... | collective-permute-start | bytes 688136 | tf_op jit(solution)/shard_map/ppermute | solution.py:54
  26.6 6.0 %collective-permute-start.9 = (bf16[4,144,128]{2,1,0:T(8,128)(2,1)S(1)}, bf16[4,144,128]{2,1,0:T(8,128)(2,1)S(1)}, u32[]{:S(2)}, u32[]{:S(2)}) collective-permute-start(bf16[4,144,128]{2,1,0:T(8,128)(2,1)S(1)} %add_convert_fusion.4), channel_id=1, source_target_pairs={{0,2},{1,3},{2,0},{3,1},{4,6},{5,7},{6,4},{7,5},{8,10},{9,11},{10,... | collective-permute-start | bytes 442376 | tf_op jit(solution)/shard_map/ppermute | solution.py:54
  32.7 5.9 %collective-permute-start.12 = (bf16[144,128]{1,0:T(8,128)(2,1)S(1)}, bf16[144,128]{1,0:T(8,128)(2,1)S(1)}, u32[]{:S(2)}, u32[]{:S(2)}) collective-permute-start(bf16[144,128]{1,0:T(8,128)(2,1)S(1)} %get-tuple-element.60), channel_id=1, source_target_pairs={{0,12},{1,13},{2,14},{3,15},{4,8},{5,9},{6,10},{7,11},{8,4},{9,5},... | collective-permute-start | bytes 110600 | tf_op jit(solution)/shard_map/ppermute | solution.py:54
  36.5 4.9 %collective-permute-start.11 = (bf16[144,128]{1,0:T(8,128)(2,1)S(1)}, bf16[144,128]{1,0:T(8,128)(2,1)S(1)}, u32[]{:S(2)}, u32[]{:S(2)}) collective-permute-start(bf16[144,128]{1,0:T(8,128)(2,1)S(1)} %get-tuple-element.61), channel_id=1, source_target_pairs={{0,8},{1,9},{2,10},{3,11},{4,12},{5,13},{6,14},{7,15},{8,0},{9,1},... | collective-permute-start | bytes 110600 | tf_op jit(solution)/shard_map/ppermute | solution.py:54
  36.5 4.9 %collective-permute-start.10 = (bf16[144,128]{1,0:T(8,128)(2,1)S(1)}, bf16[144,128]{1,0:T(8,128)(2,1)S(1)}, u32[]{:S(2)}, u32[]{:S(2)}) collective-permute-start(bf16[144,128]{1,0:T(8,128)(2,1)S(1)} %get-tuple-element.62), channel_id=1, source_target_pairs={{0,4},{1,5},{2,6},{3,7},{4,0},{5,1},{6,2},{7,3},{8,12},{9,13},{10,... | collective-permute-start | bytes 110600 | tf_op jit(solution)/shard_map/ppermute | solution.py:54
  41.9 5.0 %collective-permute-start.13 = (bf16[32,2048]{1,0:T(8,128)(2,1)S(1)}, bf16[32,2048]{1,0:T(8,128)(2,1)S(1)}, u32[]{:S(2)}, u32[]{:S(2)}) collective-permute-start(bf16[32,2048]{1,0:T(8,128)(2,1)S(1)} %project_out.1.mine_ref), channel_id=1, source_target_pairs={{0,16},{16,0},{1,17},{17,1},{2,18},{18,2},{3,19},{19,3},{4,20},{20... | collective-permute-start | bytes 393224 | tf_op jit(solution)/shard_map/ppermute | solution.py:54
  47.1 6.0 %collective-permute-start.17 = (bf16[1,32,2176]{2,1,0:T(8,128)(2,1)S(1)}, bf16[1,32,2176]{2,1,0:T(8,128)(2,1)S(1)}, u32[]{:S(2)}, u32[]{:S(2)}) collective-permute-start(bf16[1,32,2176]{2,1,0:T(8,128)(2,1)S(1)} %bitcast.36), channel_id=1, source_target_pairs={{0,2},{1,3},{2,0},{3,1},{4,6},{5,7},{6,4},{7,5},{8,10},{9,11},{10,... | collective-permute-start | bytes 417800 | tf_op jit(solution)/shard_map/ppermute | solution.py:54
  48.6 7.1 %collective-permute-start.16 = (bf16[32,2176]{1,0:T(8,128)(2,1)S(1)}, bf16[32,2176]{1,0:T(8,128)(2,1)S(1)}, u32[]{:S(2)}, u32[]{:S(2)}) collective-permute-start(bf16[32,2176]{1,0:T(8,128)(2,1)S(1)} %get-tuple-element.42), channel_id=1, source_target_pairs={{0,12},{1,13},{2,14},{3,15},{4,8},{5,9},{6,10},{7,11},{8,4},{9,5},... | collective-permute-start | bytes 417800 | tf_op jit(solution)/shard_map/ppermute | solution.py:54
  50.1 9.8 %collective-permute-start.15 = (bf16[32,2176]{1,0:T(8,128)(2,1)S(1)}, bf16[32,2176]{1,0:T(8,128)(2,1)S(1)}, u32[]{:S(2)}, u32[]{:S(2)}) collective-permute-start(bf16[32,2176]{1,0:T(8,128)(2,1)S(1)} %get-tuple-element.42), channel_id=1, source_target_pairs={{0,8},{1,9},{2,10},{3,11},{4,12},{5,13},{6,14},{7,15},{8,0},{9,1},... | collective-permute-start | bytes 417800 | tf_op jit(solution)/shard_map/ppermute | solution.py:54
  50.7 9.3 %collective-permute-start.14 = (bf16[32,2176]{1,0:T(8,128)(2,1)S(1)}, bf16[32,2176]{1,0:T(8,128)(2,1)S(1)}, u32[]{:S(2)}, u32[]{:S(2)}) collective-permute-start(bf16[32,2176]{1,0:T(8,128)(2,1)S(1)} %get-tuple-element.42), channel_id=1, source_target_pairs={{0,4},{1,5},{2,6},{3,7},{4,0},{5,1},{6,2},{7,3},{8,12},{9,13},{10,... | collective-permute-start | bytes 417800 | tf_op jit(solution)/shard_map/ppermute | solution.py:54
  60.1 12.1 %collective-permute-start.21 = (bf16[3,32,2176]{2,1,0:T(8,128)(2,1)S(1)}, bf16[3,32,2176]{2,1,0:T(8,128)(2,1)S(1)}, u32[]{:S(2)}, u32[]{:S(2)}) collective-permute-start(bf16[3,32,2176]{2,1,0:T(8,128)(2,1)S(1)} %pad_maximum_fusion.refs_1_), channel_id=1, source_target_pairs={{0,2},{1,3},{2,0},{3,1},{4,6},{5,7},{6,4},{7,5},{8,10},{9,11},{10,... | collective-permute-start | bytes 1253384 | tf_op jit(solution)/shard_map/ppermute | solution.py:54
  77.0 8.9 %collective-permute-start.20 = (bf16[4,32,2048]{2,1,0:T(8,128)(2,1)S(1)}, bf16[4,32,2048]{2,1,0:T(8,128)(2,1)S(1)}, u32[]{:S(2)}, u32[]{:S(2)}) collective-permute-start(bf16[4,32,2048]{2,1,0:T(8,128)(2,1)S(1)} %get-tuple-element.46), channel_id=1, source_target_pairs={{0,1},{1,0},{2,3},{3,2},{4,5},{5,4},{6,7},{7,6},{8,9},{9,8},{10,11... | collective-permute-start | bytes 1572872 | tf_op jit(solution)/shard_map/ppermute | solution.py:54
  78.2 5.6 %collective-permute-start.26 = (bf16[1,32,2048]{2,1,0:T(8,128)(2,1)S(1)}, bf16[1,32,2048]{2,1,0:T(8,128)(2,1)S(1)}, u32[]{:S(2)}, u32[]{:S(2)}) collective-permute-start(bf16[1,32,2048]{2,1,0:T(8,128)(2,1)S(1)} %add_convert_fusion.12), channel_id=1, source_target_pairs={{0,2},{1,3},{2,0},{3,1},{4,6},{5,7},{6,4},{7,5},{8,10},{9,11},{10,... | collective-permute-start | bytes 393224 | tf_op jit(solution)/shard_map/ppermute | solution.py:54
  83.8 6.4 %collective-permute-start.29 = (bf16[1,32,2048]{2,1,0:T(8,128)(2,1)S(1)}, bf16[1,32,2048]{2,1,0:T(8,128)(2,1)S(1)}, u32[]{:S(2)}, u32[]{:S(2)}) collective-permute-start(bf16[1,32,2048]{2,1,0:T(8,128)(2,1)S(1)} %add_convert_fusion.10), channel_id=1, source_target_pairs={{0,2},{1,3},{2,0},{3,1},{4,6},{5,7},{6,4},{7,5},{8,10},{9,11},{10,... | collective-permute-start | bytes 393224 | tf_op jit(solution)/shard_map/ppermute | solution.py:54
  84.3 9.8 %collective-permute-start.27 = (bf16[2,32,2048]{2,1,0:T(8,128)(2,1)S(1)}, bf16[2,32,2048]{2,1,0:T(8,128)(2,1)S(1)}, u32[]{:S(2)}, u32[]{:S(2)}) collective-permute-start(bf16[2,32,2048]{2,1,0:T(8,128)(2,1)S(1)} %add_convert_fusion.1), channel_id=1, source_target_pairs={{0,2},{1,3},{2,0},{3,1},{4,6},{5,7},{6,4},{7,5},{8,10},{9,11},{10,... | collective-permute-start | bytes 786440 | tf_op jit(solution)/shard_map/ppermute | solution.py:54
  85.9 10.3 %collective-permute-start.32 = (bf16[32,2048]{1,0:T(8,128)(2,1)S(1)}, bf16[32,2048]{1,0:T(8,128)(2,1)S(1)}, u32[]{:S(2)}, u32[]{:S(2)}) collective-permute-start(bf16[32,2048]{1,0:T(8,128)(2,1)S(1)} %bitcast.45), channel_id=1, source_target_pairs={{0,8},{1,9},{2,10},{3,11},{4,12},{5,13},{6,14},{7,15},{8,0},{9,1},... | collective-permute-start | bytes 393224 | tf_op jit(solution)/shard_map/ppermute | solution.py:54
  90.3 8.0 %collective-permute-start.31 = (bf16[32,2048]{1,0:T(8,128)(2,1)S(1)}, bf16[32,2048]{1,0:T(8,128)(2,1)S(1)}, u32[]{:S(2)}, u32[]{:S(2)}) collective-permute-start(bf16[32,2048]{1,0:T(8,128)(2,1)S(1)} %bitcast.46), channel_id=1, source_target_pairs={{0,12},{1,13},{2,14},{3,15},{4,8},{5,9},{6,10},{7,11},{8,4},{9,5},... | collective-permute-start | bytes 393224 | tf_op jit(solution)/shard_map/ppermute | solution.py:54
  94.3 5.4 %collective-permute-start.30 = (bf16[32,2048]{1,0:T(8,128)(2,1)S(1)}, bf16[32,2048]{1,0:T(8,128)(2,1)S(1)}, u32[]{:S(2)}, u32[]{:S(2)}) collective-permute-start(bf16[32,2048]{1,0:T(8,128)(2,1)S(1)} %slice_bitcast_fusion), channel_id=1, source_target_pairs={{0,4},{1,5},{2,6},{3,7},{4,0},{5,1},{6,2},{7,3},{8,12},{9,13},{10,... | collective-permute-start | bytes 393224 | tf_op jit(solution)/shard_map/ppermute | solution.py:54
  94.7 6.6 %collective-permute-start.34 = (bf16[16,288]{1,0:T(8,128)(2,1)S(1)}, bf16[16,288]{1,0:T(8,128)(2,1)S(1)}, u32[]{:S(2)}, u32[]{:S(2)}) collective-permute-start(bf16[16,288]{1,0:T(8,128)(2,1)S(1)} %place_rows.1), channel_id=1, source_target_pairs={{0,16},{16,0},{1,17},{17,1},{2,18},{18,2},{3,19},{19,3},{4,20},{20... | collective-permute-start | bytes 27656 | tf_op jit(solution)/shard_map/ppermute | solution.py:54
  99.7 5.0 %collective-permute-start.33 = (bf16[32,2048]{1,0:T(8,128)(2,1)S(1)}, bf16[32,2048]{1,0:T(8,128)(2,1)S(1)}, u32[]{:S(2)}, u32[]{:S(2)}) collective-permute-start(bf16[32,2048]{1,0:T(8,128)(2,1)S(1)} %fusion.2), channel_id=1, source_target_pairs={{0,16},{16,0},{1,17},{17,1},{2,18},{18,2},{3,19},{19,3},{4,20},{20... | collective-permute-start | bytes 393224 | tf_op jit(solution)/shard_map/ppermute | solution.py:54
  (30 other events, 347.4 us)

commit v6 on v5

--- a/solution.py
+++ b/solution.py
@@ -552,6 +552,9 @@
             got = swap(sent[i][0], "blk", near)
             got = [got[:mid]] + [got[j : j + 1] for j in range(mid, radix)]
         sums.append([add16(k, g) for k, g in zip(kept[i], got)])
+    pieces = [piece for group in tokens for piece in group]
+    share = place_rows(index, pieces, accepted.shape[1], hidden_in.shape[1])
+    other = swap(share, "head", 1)
     for _, step in reversed(rest[:-1]):
         part = len(sums) // 2
         for i in range(part):
@@ -574,12 +577,10 @@
     total = sums[0][0].astype(f32)
     for value in reversed(back):
         total = total + value.astype(f32)
+    total, other = lax.optimization_barrier((total, other))
+    new_rows = jnp.concatenate([jnp.where(odd, other, share), jnp.where(odd, share, other)], axis=1)
     mine, other = sum_heads(total.astype(bf16))
     layer_out = (resid.astype(f32) + (mine.astype(f32) + other.astype(f32))).astype(bf16)
-    pieces = [piece for group in tokens for piece in group]
-    share = place_rows(index, pieces, accepted.shape[1], hidden_in.shape[1])
-    other = swap(share, "head", 1)
-    new_rows = jnp.concatenate([jnp.where(odd, other, share), jnp.where(odd, share, other)], axis=1)
     return (layer_out, new_rows)
 
 

time: 106 us -> 106 us (level)
  no operation moved by 1% of the time
where the time goes in v6:
time: 106 us; the launch traced here: 105 us
  waiting for transfers between devices  52.6 us (50%)
  starting transfers between devices  34 us (32%)
  Pallas kernels  12.8 us (12%)
  other arithmetic  2.89 us (3%)
  matrix products  1.58 us (1%)
    ppermute x35, waiting for transfers between devices, swap(): return lax.ppermute(value, axis, [(i, i ^ bit) for i in range(count)])  52.6 us
    ppermute x35, starting transfers between devices, swap(): return lax.ppermute(value, axis, [(i, i ^ bit) for i in range(count)])  34 us
    pallas_call x2, Pallas kernels, expert(): pl.pallas_call(functools.partial(expert_kernel, parts, cuts), grid=(1,),...  5.31 us
    pallas_call x1, Pallas kernels, prepare(): pl.pallas_call(functools.partial(pre_kernel, heads, experts), out_shape=(...  3.93 us
  transfers between devices with their start and end apart: 35, of which 22 were waited for; matrix products, arithmetic and copies ran while one was open for 4% of the time, Pallas kernels for 4%

profile of v6, /device:TPU:0, one launch (start us, length us, event | category | flops | bytes accessed | tf_op | source)
XLA Modules:
  0.0 105.5 jit_solution(10302431806896021880)
XLA Ops:
  0.7 3.9 %prepare.1 = (bf16[32,896]{1,0:T(8,128)(2,1)}, bf16[32,2048]{1,0:T(8,128)(2,1)}, f32[32,256]{1,0:T(8,128)}, f32[32,32]{1,0:T(8,128)}) custom-call(bf16[768,2048]{1,0:T(8,128)(2,1)} %query_hbm.1, s32[1,32]{1,0:T(1,128)} %parents_hbm.1, s32[1,16]{1,0:T(1,128)} %bitcast.53, s32[6,32]{1,0:T(8,128)} %bitcast.51, f32[6,32]{1,0:T(8,128)} %bitcast.52, ...), custom_call_target="tpu_custom_call" | custom-call | flops 144179200 | bytes 4505600 | tf_op jit(solution)/shard_map/prepare/pallas_call | solution.py:169
  4.7 5.1 %collective-permute-start.3 = (bf16[32,896]{1,0:T(8,128)(2,1)}, bf16[32,896]{1,0:T(8,128)(2,1)S(1)}, u32[]{:S(2)}, u32[]{:S(2)}) collective-permute-start(bf16[32,896]{1,0:T(8,128)(2,1)} %get-tuple-element.35.query_ref), channel_id=1, source_target_pairs={{0,12},{1,13},{2,14},{3,15},{4,8},{5,9},{6,10},{7,11},{8,4},{9,5},... | collective-permute-start | bytes 172040 | tf_op jit(solution)/shard_map/ppermute | solution.py:54
  11.8 1.7 %collective-permute-start = (f32[32,288]{1,0:T(8,128)S(1)}, f32[32,288]{1,0:T(8,128)S(1)}, u32[]{:S(2)}, u32[]{:S(2)}) collective-permute-start(f32[32,288]{1,0:T(8,128)S(1)} %fusion.18), channel_id=1, source_target_pairs={{0,16},{16,0},{1,17},{17,1},{2,18},{18,2},{3,19},{19,3},{4,20},{20... | collective-permute-start | bytes 110600 | tf_op jit(solution)/shard_map/ppermute | solution.py:54
  16.3 1.7 %collective-permute-start.4 = (bf16[4,32,896]{2,1,0:T(8,128)(2,1)S(1)}, bf16[4,32,896]{2,1,0:T(8,128)(2,1)S(1)}, u32[]{:S(2)}, u32[]{:S(2)}) collective-permute-start(bf16[4,32,896]{2,1,0:T(8,128)(2,1)S(1)} %pad_maximum_fusion.1.refs_0_), channel_id=1, source_target_pairs={{0,2},{1,3},{2,0},{3,1},{4,6},{5,7},{6,4},{7,5},{8,10},{9,11},{10,... | collective-permute-start | bytes 688136 | tf_op jit(solution)/shard_map/ppermute | solution.py:54
  18.1 4.2 %collective-permute-done.4.refs_1_ = bf16[4,32,896]{2,1,0:T(8,128)(2,1)S(1)} collective-permute-done((bf16[4,32,896]{2,1,0:T(8,128)(2,1)S(1)}, bf16[4,32,896]{2,1,0:T(8,128)(2,1)S(1)}, u32[]{:S(2)}, u32[]{:S(2)}) %collective-permute-start.4) | collective-permute-done | bytes 229408 | tf_op jit(solution)/shard_map/ppermute | solution.py:54
  26.6 1.7 %collective-permute-start.9 = (bf16[4,144,128]{2,1,0:T(8,128)(2,1)S(1)}, bf16[4,144,128]{2,1,0:T(8,128)(2,1)S(1)}, u32[]{:S(2)}, u32[]{:S(2)}) collective-permute-start(bf16[4,144,128]{2,1,0:T(8,128)(2,1)S(1)} %add_convert_fusion.4), channel_id=1, source_target_pairs={{0,2},{1,3},{2,0},{3,1},{4,6},{5,7},{6,4},{7,5},{8,10},{9,11},{10,... | collective-permute-start | bytes 442376 | tf_op jit(solution)/shard_map/ppermute | solution.py:54
  28.4 4.2 %collective-permute-done.9 = bf16[4,144,128]{2,1,0:T(8,128)(2,1)S(1)} collective-permute-done((bf16[4,144,128]{2,1,0:T(8,128)(2,1)S(1)}, bf16[4,144,128]{2,1,0:T(8,128)(2,1)S(1)}, u32[]{:S(2)}, u32[]{:S(2)}) %collective-permute-start.9) | collective-permute-done | bytes 147488 | tf_op jit(solution)/shard_map/ppermute | solution.py:54
  32.7 3.8 %collective-permute-start.12 = (bf16[144,128]{1,0:T(8,128)(2,1)S(1)}, bf16[144,128]{1,0:T(8,128)(2,1)S(1)}, u32[]{:S(2)}, u32[]{:S(2)}) collective-permute-start(bf16[144,128]{1,0:T(8,128)(2,1)S(1)} %get-tuple-element.64), channel_id=1, source_target_pairs={{0,12},{1,13},{2,14},{3,15},{4,8},{5,9},{6,10},{7,11},{8,4},{9,5},... | collective-permute-start | bytes 110600 | tf_op jit(solution)/shard_map/ppermute | solution.py:54
  38.5 2.8 %collective-permute-done.11.refs_2_ = bf16[144,128]{1,0:T(8,128)(2,1)S(1)} collective-permute-done((bf16[144,128]{1,0:T(8,128)(2,1)S(1)}, bf16[144,128]{1,0:T(8,128)(2,1)S(1)}, u32[]{:S(2)}, u32[]{:S(2)}) %collective-permute-start.11) | collective-permute-done | bytes 36896 | tf_op jit(solution)/shard_map/ppermute | solution.py:54
  41.9 1.5 %collective-permute-start.13 = (bf16[32,2048]{1,0:T(8,128)(2,1)S(1)}, bf16[32,2048]{1,0:T(8,128)(2,1)S(1)}, u32[]{:S(2)}, u32[]{:S(2)}) collective-permute-start(bf16[32,2048]{1,0:T(8,128)(2,1)S(1)} %project_out.1.mine_ref), channel_id=1, source_target_pairs={{0,16},{16,0},{1,17},{17,1},{2,18},{18,2},{3,19},{19,3},{4,20},{20... | collective-permute-start | bytes 393224 | tf_op jit(solution)/shard_map/ppermute | solution.py:54
  43.5 3.4 %collective-permute-done.13.other_ref = bf16[32,2048]{1,0:T(8,128)(2,1)S(1)} collective-permute-done((bf16[32,2048]{1,0:T(8,128)(2,1)S(1)}, bf16[32,2048]{1,0:T(8,128)(2,1)S(1)}, u32[]{:S(2)}, u32[]{:S(2)}) %collective-permute-start.13) | collective-permute-done | bytes 131104 | tf_op jit(solution)/shard_map/ppermute | solution.py:54
  47.1 1.6 %collective-permute-start.17 = (bf16[1,32,2176]{2,1,0:T(8,128)(2,1)S(1)}, bf16[1,32,2176]{2,1,0:T(8,128)(2,1)S(1)}, u32[]{:S(2)}, u32[]{:S(2)}) collective-permute-start(bf16[1,32,2176]{2,1,0:T(8,128)(2,1)S(1)} %bitcast.36), channel_id=1, source_target_pairs={{0,2},{1,3},{2,0},{3,1},{4,6},{5,7},{6,4},{7,5},{8,10},{9,11},{10,... | collective-permute-start | bytes 417800 | tf_op jit(solution)/shard_map/ppermute | solution.py:54
  50.7 2.4 %collective-permute-start.14 = (bf16[32,2176]{1,0:T(8,128)(2,1)S(1)}, bf16[32,2176]{1,0:T(8,128)(2,1)S(1)}, u32[]{:S(2)}, u32[]{:S(2)}) collective-permute-start(bf16[32,2176]{1,0:T(8,128)(2,1)S(1)} %get-tuple-element.44), channel_id=1, source_target_pairs={{0,4},{1,5},{2,6},{3,7},{4,0},{5,1},{6,2},{7,3},{8,12},{9,13},{10,... | collective-permute-start | bytes 417800 | tf_op jit(solution)/shard_map/ppermute | solution.py:54
  53.0 2.7 %collective-permute-done.16 = bf16[32,2176]{1,0:T(8,128)(2,1)S(1)} collective-permute-done((bf16[32,2176]{1,0:T(8,128)(2,1)S(1)}, bf16[32,2176]{1,0:T(8,128)(2,1)S(1)}, u32[]{:S(2)}, u32[]{:S(2)}) %collective-permute-start.16) | collective-permute-done | bytes 139296 | tf_op jit(solution)/shard_map/ppermute | solution.py:54
  55.7 4.2 %collective-permute-done.15 = bf16[32,2176]{1,0:T(8,128)(2,1)S(1)} collective-permute-done((bf16[32,2176]{1,0:T(8,128)(2,1)S(1)}, bf16[32,2176]{1,0:T(8,128)(2,1)S(1)}, u32[]{:S(2)}, u32[]{:S(2)}) %collective-permute-start.15) | collective-permute-done | bytes 139296 | tf_op jit(solution)/shard_map/ppermute | solution.py:54
  62.0 2.7 %expert.2 = (bf16[2,32,2048]{2,1,0:T(8,128)(2,1)S(1)}, bf16[1,32,2048]{2,1,0:T(8,128)(2,1)S(1)}, bf16[1,32,2048]{2,1,0:T(8,128)(2,1)S(1)}, bf16[4,32,2048]{2,1,0:T(8,128)(2,1)S(1)}) custom-call(bf16[1,32,2176]{2,1,0:T(8,128)(2,1)S(1)} %bitcast.38, bf16[3,32,2176]{2,1,0:T(8,128)(2,1)S(1)} %pad_maximum_fusion.refs_1_, ...), custom_call_target="tpu_custom_call" | custom-call | flops 1 | bytes 1 | tf_op jit(solution)/shard_map/expert/pallas_call | solution.py:398
  64.7 7.4 %collective-permute-done.21.refs_1_.refs_3_ = bf16[3,32,2176]{2,1,0:T(8,128)(2,1)S(1)} collective-permute-done((bf16[3,32,2176]{2,1,0:T(8,128)(2,1)S(1)}, bf16[3,32,2176]{2,1,0:T(8,128)(2,1)S(1)}, u32[]{:S(2)}, u32[]{:S(2)}) %collective-permute-start.21) | collective-permute-done | bytes 417824 | tf_op jit(solution)/shard_map/ppermute | solution.py:54
  74.1 2.7 %expert.3 = (bf16[2,32,2048]{2,1,0:T(8,128)(2,1)S(1)}, bf16[1,32,2048]{2,1,0:T(8,128)(2,1)S(1)}, bf16[1,32,2048]{2,1,0:T(8,128)(2,1)S(1)}, bf16[2,32,2048]{2,1,0...) custom-call(bf16[1,32,2176]{2,1,0:T(8,128)(2,1)S(1)} %collective-permute-done.17.refs_0_.refs_2_, ...), custom_call_target="tpu_custom_call" | custom-call | flops 1 | bytes 1 | tf_op jit(solution)/shard_map/expert/pallas_call | solution.py:398
  79.6 4.3 %collective-permute-done.26 = bf16[1,32,2048]{2,1,0:T(8,128)(2,1)S(1)} collective-permute-done((bf16[1,32,2048]{2,1,0:T(8,128)(2,1)S(1)}, bf16[1,32,2048]{2,1,0:T(8,128)(2,1)S(1)}, u32[]{:S(2)}, u32[]{:S(2)}) %collective-permute-start.26) | collective-permute-done | bytes 131104 | tf_op jit(solution)/shard_map/ppermute | solution.py:54
  86.0 4.3 %collective-permute-done.29 = bf16[1,32,2048]{2,1,0:T(8,128)(2,1)S(1)} collective-permute-done((bf16[1,32,2048]{2,1,0:T(8,128)(2,1)S(1)}, bf16[1,32,2048]{2,1,0:T(8,128)(2,1)S(1)}, u32[]{:S(2)}, u32[]{:S(2)}) %collective-permute-start.29) | collective-permute-done | bytes 131104 | tf_op jit(solution)/shard_map/ppermute | solution.py:54
  90.3 2.4 %collective-permute-start.31 = (bf16[32,2048]{1,0:T(8,128)(2,1)S(1)}, bf16[32,2048]{1,0:T(8,128)(2,1)S(1)}, u32[]{:S(2)}, u32[]{:S(2)}) collective-permute-start(bf16[32,2048]{1,0:T(8,128)(2,1)S(1)} %bitcast.46), channel_id=1, source_target_pairs={{0,12},{1,13},{2,14},{3,15},{4,8},{5,9},{6,10},{7,11},{8,4},{9,5},... | collective-permute-start | bytes 393224 | tf_op jit(solution)/shard_map/ppermute | solution.py:54
  96.2 2.2 %collective-permute-done.31 = bf16[32,2048]{1,0:T(8,128)(2,1)S(1)} collective-permute-done((bf16[32,2048]{1,0:T(8,128)(2,1)S(1)}, bf16[32,2048]{1,0:T(8,128)(2,1)S(1)}, u32[]{:S(2)}, u32[]{:S(2)}) %collective-permute-start.31) | collective-permute-done | bytes 131104 | tf_op jit(solution)/shard_map/ppermute | solution.py:54
  99.7 1.6 %collective-permute-start.34 = (bf16[32,2048]{1,0:T(8,128)(2,1)S(1)}, bf16[32,2048]{1,0:T(8,128)(2,1)S(1)}, u32[]{:S(2)}, u32[]{:S(2)}) collective-permute-start(bf16[32,2048]{1,0:T(8,128)(2,1)S(1)} %fusion.1), channel_id=1, source_target_pairs={{0,16},{16,0},{1,17},{17,1},{2,18},{18,2},{3,19},{19,3},{4,20},{20... | collective-permute-start | bytes 393224 | tf_op jit(solution)/shard_map/ppermute | solution.py:54
  102.0 2.8 %collective-permute-done.34 = bf16[32,2048]{1,0:T(8,128)(2,1)S(1)} collective-permute-done((bf16[32,2048]{1,0:T(8,128)(2,1)S(1)}, bf16[32,2048]{1,0:T(8,128)(2,1)S(1)}, u32[]{:S(2)}, u32[]{:S(2)}) %collective-permute-start.34) | collective-permute-done | bytes 131104 | tf_op jit(solution)/shard_map/ppermute | solution.py:54
  (128 shorter events, 29.3 us)
Async XLA Ops:
  4.7 11.5 %collective-permute-start.3 = (bf16[32,896]{1,0:T(8,128)(2,1)}, bf16[32,896]{1,0:T(8,128)(2,1)S(1)}, u32[]{:S(2)}, u32[]{:S(2)}) collective-permute-start(bf16[32,896]{1,0:T(8,128)(2,1)} %get-tuple-element.35.query_ref), channel_id=1, source_target_pairs={{0,12},{1,13},{2,14},{3,15},{4,8},{5,9},{6,10},{7,11},{8,4},{9,5},... | collective-permute-start | bytes 172040 | tf_op jit(solution)/shard_map/ppermute | solution.py:54
  9.8 6.4 %collective-permute-start.2 = (bf16[32,896]{1,0:T(8,128)(2,1)}, bf16[32,896]{1,0:T(8,128)(2,1)S(1)}, u32[]{:S(2)}, u32[]{:S(2)}) collective-permute-start(bf16[32,896]{1,0:T(8,128)(2,1)} %get-tuple-element.35.query_ref), channel_id=1, source_target_pairs={{0,8},{1,9},{2,10},{3,11},{4,12},{5,13},{6,14},{7,15},{8,0},{9,1},... | collective-permute-start | bytes 172040 | tf_op jit(solution)/shard_map/ppermute | solution.py:54
  9.8 6.4 %collective-permute-start.1 = (bf16[32,896]{1,0:T(8,128)(2,1)}, bf16[32,896]{1,0:T(8,128)(2,1)S(1)}, u32[]{:S(2)}, u32[]{:S(2)}) collective-permute-start(bf16[32,896]{1,0:T(8,128)(2,1)} %get-tuple-element.35.query_ref), channel_id=1, source_target_pairs={{0,4},{1,5},{2,6},{3,7},{4,0},{5,1},{6,2},{7,3},{8,12},{9,13},{10,... | collective-permute-start | bytes 172040 | tf_op jit(solution)/shard_map/ppermute | solution.py:54
  16.3 6.1 %collective-permute-start.4 = (bf16[4,32,896]{2,1,0:T(8,128)(2,1)S(1)}, bf16[4,32,896]{2,1,0:T(8,128)(2,1)S(1)}, u32[]{:S(2)}, u32[]{:S(2)}) collective-permute-start(bf16[4,32,896]{2,1,0:T(8,128)(2,1)S(1)} %pad_maximum_fusion.1.refs_0_), channel_id=1, source_target_pairs={{0,2},{1,3},{2,0},{3,1},{4,6},{5,7},{6,4},{7,5},{8,10},{9,11},{10,... | collective-permute-start | bytes 688136 | tf_op jit(solution)/shard_map/ppermute | solution.py:54
  18.1 4.4 %collective-permute-start.5 = (bf16[4,32,896]{2,1,0:T(8,128)(2,1)S(1)}, bf16[4,32,896]{2,1,0:T(8,128)(2,1)S(1)}, u32[]{:S(2)}, u32[]{:S(2)}) collective-permute-start(bf16[4,32,896]{2,1,0:T(8,128)(2,1)S(1)} %pad_maximum_fusion.1.refs_0_), channel_id=1, source_target_pairs={{0,1},{1,0},{2,3},{3,2},{4,5},{5,4},{6,7},{7,6},{8,9},{9,8},{10,11... | collective-permute-start | bytes 688136 | tf_op jit(solution)/shard_map/ppermute | solution.py:54
  26.6 6.0 %collective-permute-start.9 = (bf16[4,144,128]{2,1,0:T(8,128)(2,1)S(1)}, bf16[4,144,128]{2,1,0:T(8,128)(2,1)S(1)}, u32[]{:S(2)}, u32[]{:S(2)}) collective-permute-start(bf16[4,144,128]{2,1,0:T(8,128)(2,1)S(1)} %add_convert_fusion.4), channel_id=1, source_target_pairs={{0,2},{1,3},{2,0},{3,1},{4,6},{5,7},{6,4},{7,5},{8,10},{9,11},{10,... | collective-permute-start | bytes 442376 | tf_op jit(solution)/shard_map/ppermute | solution.py:54
  32.7 5.9 %collective-permute-start.12 = (bf16[144,128]{1,0:T(8,128)(2,1)S(1)}, bf16[144,128]{1,0:T(8,128)(2,1)S(1)}, u32[]{:S(2)}, u32[]{:S(2)}) collective-permute-start(bf16[144,128]{1,0:T(8,128)(2,1)S(1)} %get-tuple-element.64), channel_id=1, source_target_pairs={{0,12},{1,13},{2,14},{3,15},{4,8},{5,9},{6,10},{7,11},{8,4},{9,5},... | collective-permute-start | bytes 110600 | tf_op jit(solution)/shard_map/ppermute | solution.py:54
  36.5 4.9 %collective-permute-start.11 = (bf16[144,128]{1,0:T(8,128)(2,1)S(1)}, bf16[144,128]{1,0:T(8,128)(2,1)S(1)}, u32[]{:S(2)}, u32[]{:S(2)}) collective-permute-start(bf16[144,128]{1,0:T(8,128)(2,1)S(1)} %get-tuple-element.65), channel_id=1, source_target_pairs={{0,8},{1,9},{2,10},{3,11},{4,12},{5,13},{6,14},{7,15},{8,0},{9,1},... | collective-permute-start | bytes 110600 | tf_op jit(solution)/shard_map/ppermute | solution.py:54
  36.5 4.9 %collective-permute-start.10 = (bf16[144,128]{1,0:T(8,128)(2,1)S(1)}, bf16[144,128]{1,0:T(8,128)(2,1)S(1)}, u32[]{:S(2)}, u32[]{:S(2)}) collective-permute-start(bf16[144,128]{1,0:T(8,128)(2,1)S(1)} %get-tuple-element.66), channel_id=1, source_target_pairs={{0,4},{1,5},{2,6},{3,7},{4,0},{5,1},{6,2},{7,3},{8,12},{9,13},{10,... | collective-permute-start | bytes 110600 | tf_op jit(solution)/shard_map/ppermute | solution.py:54
  41.9 5.0 %collective-permute-start.13 = (bf16[32,2048]{1,0:T(8,128)(2,1)S(1)}, bf16[32,2048]{1,0:T(8,128)(2,1)S(1)}, u32[]{:S(2)}, u32[]{:S(2)}) collective-permute-start(bf16[32,2048]{1,0:T(8,128)(2,1)S(1)} %project_out.1.mine_ref), channel_id=1, source_target_pairs={{0,16},{16,0},{1,17},{17,1},{2,18},{18,2},{3,19},{19,3},{4,20},{20... | collective-permute-start | bytes 393224 | tf_op jit(solution)/shard_map/ppermute | solution.py:54
  47.1 6.0 %collective-permute-start.17 = (bf16[1,32,2176]{2,1,0:T(8,128)(2,1)S(1)}, bf16[1,32,2176]{2,1,0:T(8,128)(2,1)S(1)}, u32[]{:S(2)}, u32[]{:S(2)}) collective-permute-start(bf16[1,32,2176]{2,1,0:T(8,128)(2,1)S(1)} %bitcast.36), channel_id=1, source_target_pairs={{0,2},{1,3},{2,0},{3,1},{4,6},{5,7},{6,4},{7,5},{8,10},{9,11},{10,... | collective-permute-start | bytes 417800 | tf_op jit(solution)/shard_map/ppermute | solution.py:54
  48.6 7.1 %collective-permute-start.16 = (bf16[32,2176]{1,0:T(8,128)(2,1)S(1)}, bf16[32,2176]{1,0:T(8,128)(2,1)S(1)}, u32[]{:S(2)}, u32[]{:S(2)}) collective-permute-start(bf16[32,2176]{1,0:T(8,128)(2,1)S(1)} %get-tuple-element.44), channel_id=1, source_target_pairs={{0,12},{1,13},{2,14},{3,15},{4,8},{5,9},{6,10},{7,11},{8,4},{9,5},... | collective-permute-start | bytes 417800 | tf_op jit(solution)/shard_map/ppermute | solution.py:54
  50.1 9.8 %collective-permute-start.15 = (bf16[32,2176]{1,0:T(8,128)(2,1)S(1)}, bf16[32,2176]{1,0:T(8,128)(2,1)S(1)}, u32[]{:S(2)}, u32[]{:S(2)}) collective-permute-start(bf16[32,2176]{1,0:T(8,128)(2,1)S(1)} %get-tuple-element.44), channel_id=1, source_target_pairs={{0,8},{1,9},{2,10},{3,11},{4,12},{5,13},{6,14},{7,15},{8,0},{9,1},... | collective-permute-start | bytes 417800 | tf_op jit(solution)/shard_map/ppermute | solution.py:54
  50.7 9.3 %collective-permute-start.14 = (bf16[32,2176]{1,0:T(8,128)(2,1)S(1)}, bf16[32,2176]{1,0:T(8,128)(2,1)S(1)}, u32[]{:S(2)}, u32[]{:S(2)}) collective-permute-start(bf16[32,2176]{1,0:T(8,128)(2,1)S(1)} %get-tuple-element.44), channel_id=1, source_target_pairs={{0,4},{1,5},{2,6},{3,7},{4,0},{5,1},{6,2},{7,3},{8,12},{9,13},{10,... | collective-permute-start | bytes 417800 | tf_op jit(solution)/shard_map/ppermute | solution.py:54
  60.1 12.1 %collective-permute-start.21 = (bf16[3,32,2176]{2,1,0:T(8,128)(2,1)S(1)}, bf16[3,32,2176]{2,1,0:T(8,128)(2,1)S(1)}, u32[]{:S(2)}, u32[]{:S(2)}) collective-permute-start(bf16[3,32,2176]{2,1,0:T(8,128)(2,1)S(1)} %pad_maximum_fusion.refs_1_), channel_id=1, source_target_pairs={{0,2},{1,3},{2,0},{3,1},{4,6},{5,7},{6,4},{7,5},{8,10},{9,11},{10,... | collective-permute-start | bytes 1253384 | tf_op jit(solution)/shard_map/ppermute | solution.py:54
  77.0 8.9 %collective-permute-start.20 = (bf16[4,32,2048]{2,1,0:T(8,128)(2,1)S(1)}, bf16[4,32,2048]{2,1,0:T(8,128)(2,1)S(1)}, u32[]{:S(2)}, u32[]{:S(2)}) collective-permute-start(bf16[4,32,2048]{2,1,0:T(8,128)(2,1)S(1)} %get-tuple-element.48), channel_id=1, source_target_pairs={{0,1},{1,0},{2,3},{3,2},{4,5},{5,4},{6,7},{7,6},{8,9},{9,8},{10,11... | collective-permute-start | bytes 1572872 | tf_op jit(solution)/shard_map/ppermute | solution.py:54
  78.2 5.6 %collective-permute-start.26 = (bf16[1,32,2048]{2,1,0:T(8,128)(2,1)S(1)}, bf16[1,32,2048]{2,1,0:T(8,128)(2,1)S(1)}, u32[]{:S(2)}, u32[]{:S(2)}) collective-permute-start(bf16[1,32,2048]{2,1,0:T(8,128)(2,1)S(1)} %add_convert_fusion.12), channel_id=1, source_target_pairs={{0,2},{1,3},{2,0},{3,1},{4,6},{5,7},{6,4},{7,5},{8,10},{9,11},{10,... | collective-permute-start | bytes 393224 | tf_op jit(solution)/shard_map/ppermute | solution.py:54
  83.8 6.4 %collective-permute-start.29 = (bf16[1,32,2048]{2,1,0:T(8,128)(2,1)S(1)}, bf16[1,32,2048]{2,1,0:T(8,128)(2,1)S(1)}, u32[]{:S(2)}, u32[]{:S(2)}) collective-permute-start(bf16[1,32,2048]{2,1,0:T(8,128)(2,1)S(1)} %add_convert_fusion.10), channel_id=1, source_target_pairs={{0,2},{1,3},{2,0},{3,1},{4,6},{5,7},{6,4},{7,5},{8,10},{9,11},{10,... | collective-permute-start | bytes 393224 | tf_op jit(solution)/shard_map/ppermute | solution.py:54
  84.3 9.8 %collective-permute-start.27 = (bf16[2,32,2048]{2,1,0:T(8,128)(2,1)S(1)}, bf16[2,32,2048]{2,1,0:T(8,128)(2,1)S(1)}, u32[]{:S(2)}, u32[]{:S(2)}) collective-permute-start(bf16[2,32,2048]{2,1,0:T(8,128)(2,1)S(1)} %add_convert_fusion.1), channel_id=1, source_target_pairs={{0,2},{1,3},{2,0},{3,1},{4,6},{5,7},{6,4},{7,5},{8,10},{9,11},{10,... | collective-permute-start | bytes 786440 | tf_op jit(solution)/shard_map/ppermute | solution.py:54
  85.9 10.3 %collective-permute-start.32 = (bf16[32,2048]{1,0:T(8,128)(2,1)S(1)}, bf16[32,2048]{1,0:T(8,128)(2,1)S(1)}, u32[]{:S(2)}, u32[]{:S(2)}) collective-permute-start(bf16[32,2048]{1,0:T(8,128)(2,1)S(1)} %bitcast.45), channel_id=1, source_target_pairs={{0,8},{1,9},{2,10},{3,11},{4,12},{5,13},{6,14},{7,15},{8,0},{9,1},... | collective-permute-start | bytes 393224 | tf_op jit(solution)/shard_map/ppermute | solution.py:54
  90.3 8.0 %collective-permute-start.31 = (bf16[32,2048]{1,0:T(8,128)(2,1)S(1)}, bf16[32,2048]{1,0:T(8,128)(2,1)S(1)}, u32[]{:S(2)}, u32[]{:S(2)}) collective-permute-start(bf16[32,2048]{1,0:T(8,128)(2,1)S(1)} %bitcast.46), channel_id=1, source_target_pairs={{0,12},{1,13},{2,14},{3,15},{4,8},{5,9},{6,10},{7,11},{8,4},{9,5},... | collective-permute-start | bytes 393224 | tf_op jit(solution)/shard_map/ppermute | solution.py:54
  94.3 5.4 %collective-permute-start.30 = (bf16[32,2048]{1,0:T(8,128)(2,1)S(1)}, bf16[32,2048]{1,0:T(8,128)(2,1)S(1)}, u32[]{:S(2)}, u32[]{:S(2)}) collective-permute-start(bf16[32,2048]{1,0:T(8,128)(2,1)S(1)} %slice_bitcast_fusion), channel_id=1, source_target_pairs={{0,4},{1,5},{2,6},{3,7},{4,0},{5,1},{6,2},{7,3},{8,12},{9,13},{10,... | collective-permute-start | bytes 393224 | tf_op jit(solution)/shard_map/ppermute | solution.py:54
  94.7 5.0 %collective-permute-start.33 = (bf16[16,288]{1,0:T(8,128)(2,1)S(1)}, bf16[16,288]{1,0:T(8,128)(2,1)S(1)}, u32[]{:S(2)}, u32[]{:S(2)}) collective-permute-start(bf16[16,288]{1,0:T(8,128)(2,1)S(1)} %place_rows.1), channel_id=1, source_target_pairs={{0,16},{16,0},{1,17},{17,1},{2,18},{18,2},{3,19},{19,3},{4,20},{20... | collective-permute-start | bytes 27656 | tf_op jit(solution)/shard_map/ppermute | solution.py:54
  99.7 5.0 %collective-permute-start.34 = (bf16[32,2048]{1,0:T(8,128)(2,1)S(1)}, bf16[32,2048]{1,0:T(8,128)(2,1)S(1)}, u32[]{:S(2)}, u32[]{:S(2)}) collective-permute-start(bf16[32,2048]{1,0:T(8,128)(2,1)S(1)} %fusion.1), channel_id=1, source_target_pairs={{0,16},{16,0},{1,17},{17,1},{2,18},{18,2},{3,19},{19,3},{4,20},{20... | collective-permute-start | bytes 393224 | tf_op jit(solution)/shard_map/ppermute | solution.py:54
  (30 other events, 347.4 us)
